TPU v7x, 256 devices: a whole 4x4x8 slice. The times are simulated.
256 devices in a mesh: dap: 128 (over x, z, y), dp: 2 (over core).
Axes of the slice: x: 4, y: 4, z: 8, core: 2. Of those that a mesh axis runs over, the one named last changes fastest.
Arguments:
- homolog_embedding_tensor: bfloat16 [64, 1024, 256], P('dp', 'dap'), parts along dimension 0, may hold values from -6 to 6
- standardizer_scale: float32 [256], replicated, may hold values from 0.1 to 1.9
- standardizer_shift: float32 [256], replicated, may hold values from -3 to 3
- first_operand_kernel: bfloat16 [256, 32], replicated, may hold values from -0.375 to 0.375
- left_projection_bias: float32 [32], replicated, may hold values from -3 to 3
- second_operand_kernel: bfloat16 [256, 32], replicated, may hold values from -0.375 to 0.375
- right_projection_bias: float32 [32], replicated, may hold values from -3 to 3
- output_weight_matrix: bfloat16 [1024, 128], replicated, may hold values from -0.75 to 0.75
- output_bias_vector: float32 [128], replicated, may hold values from -3 to 3
- pair_update_cotangent: bfloat16 [2048, 1024, 128], P(('dp', 'dap')), parts along dimension 0, may hold values from -24 to 24
Outputs:
- pair_representation_update: bfloat16 [2048, 1024, 128], P(('dp', 'dap')), parts along dimension 0
- alignment_gradient: float32 [64, 1024, 256], P('dp', 'dap'), parts along dimension 0
- norm_gain_gradient: float32 [512], P('dp'), parts along dimension 0
- norm_offset_gradient: float32 [512], P('dp'), parts along dimension 0
- left_weight_gradient: float32 [512, 32], P('dp'), parts along dimension 0
- left_bias_gradient: float32 [64], P('dp'), parts along dimension 0
- right_weight_gradient: float32 [512, 32], P('dp'), parts along dimension 0
- right_bias_gradient: float32 [64], P('dp'), parts along dimension 0
- output_weight_gradient: float32 [2048, 128], P('dp'), parts along dimension 0
- output_bias_gradient: float32 [256], P('dp'), parts along dimension 0
There are 2 independent parts, one for each index of `dp`. A program takes and returns all parts, laid end to end along the dimension named above; an argument that names none is the same for every part. Nothing has to cross between parts.
All inputs are finite; a program needn't handle non-finite values.
Results may differ from a plain program's by a relative error of at most 0.0056.
Values may be sent and summed in bfloat16 or wider, within the bound.
No kernel may reach another device: no remote copies, remote signals or barrier semaphores. Data moves between devices by JAX's collectives and lax.ppermute only.
A program may use at most 128 MiB of HBM per device.

v0:
```python
import math

import jax
import jax.numpy as jnp
from jax import lax
from jax.sharding import PartitionSpec as P

EPSILON = 1e-05


def normalize(features, standardizer_scale, standardizer_shift):
    average = jnp.mean(features, axis=-1, keepdims=True)
    centred = features - average
    spread = jnp.mean(centred * centred, axis=-1, keepdims=True)
    return centred * lax.rsqrt(spread + EPSILON) * standardizer_scale + standardizer_shift


def cotangent_outer(grad_flat, output_weight_matrix, scale_root):
    product = lax.dot_general(
        grad_flat,
        output_weight_matrix,
        (((1,), (1,)), ((), ())),
        preferred_element_type=jnp.float32,
    )
    return (product * scale_root).astype(jnp.bfloat16)


def per_device(
    homolog_embedding_tensor,
    standardizer_scale,
    standardizer_shift,
    first_operand_kernel,
    left_projection_bias,
    second_operand_kernel,
    right_projection_bias,
    output_weight_matrix,
    output_bias_vector,
    pair_update_cotangent,
):
    sequence_count = homolog_embedding_tensor.shape[0]
    local_residue_rows = homolog_embedding_tensor.shape[1]
    total_res = pair_update_cotangent.shape[1]
    chans = first_operand_kernel.shape[1]
    pair_ch = output_weight_matrix.shape[1]
    activations_fp32 = homolog_embedding_tensor.astype(jnp.float32)
    normed = normalize(activations_fp32, standardizer_scale, standardizer_shift).astype(
        jnp.bfloat16
    )
    left_proj = (
        jnp.einsum("sih,hc->sic", normed, first_operand_kernel, preferred_element_type=jnp.float32)
        + left_projection_bias
    ).astype(jnp.bfloat16)
    right_proj = (
        jnp.einsum("sih,hc->sic", normed, second_operand_kernel, preferred_element_type=jnp.float32)
        + right_projection_bias
    ).astype(jnp.bfloat16)
    right_flat = lax.all_gather(
        right_proj.reshape(sequence_count, local_residue_rows * chans), "dap", axis=1, tiled=True
    )
    right_all = right_flat.reshape(sequence_count, total_res, chans)
    scale_root = 1.0 / math.sqrt(total_res)
    width = min(total_res, 128)
    nblocks = total_res // width
    right_blocks = jnp.moveaxis(right_all.reshape(sequence_count, nblocks, width, chans), 1, 0)
    grad_blocks = jnp.moveaxis(
        pair_update_cotangent.reshape(local_residue_rows, nblocks, width, pair_ch), 1, 0
    )

    def advance(totals, pieces):
        w_total, b_total, a_total = totals
        right_piece, grad_piece = pieces
        outer = (
            jnp.einsum("sic,sjd->ijcd", left_proj, right_piece, preferred_element_type=jnp.float32)
            / sequence_count
        ).astype(jnp.bfloat16)
        outer_flat = outer.reshape(local_residue_rows * width, chans * chans)
        update = (
            jnp.dot(outer_flat, output_weight_matrix, preferred_element_type=jnp.float32)
            + output_bias_vector
        ).astype(jnp.bfloat16)
        grad_flat = grad_piece.reshape(local_residue_rows * width, pair_ch)
        outer_grad = cotangent_outer(grad_flat, output_weight_matrix, scale_root)
        w_total = w_total + lax.dot_general(
            outer_flat, grad_flat, (((0,), (0,)), ((), ())), preferred_element_type=jnp.float32
        )
        b_total = b_total + jnp.sum(grad_flat.astype(jnp.float32), axis=0)
        grad_four = outer_grad.reshape(local_residue_rows, width, chans, chans)
        a_total = (
            a_total
            + jnp.einsum(
                "ijcd,sjd->sic", grad_four, right_piece, preferred_element_type=jnp.float32
            )
            / sequence_count
        )
        right_part = (
            jnp.einsum("ijcd,sic->sjd", grad_four, left_proj, preferred_element_type=jnp.float32)
            / sequence_count
        )
        return (
            (w_total, b_total, a_total),
            (update.reshape(local_residue_rows, width, pair_ch), right_part),
        )

    start = (
        jnp.zeros((chans * chans, pair_ch), jnp.float32),
        jnp.zeros((pair_ch,), jnp.float32),
        jnp.zeros((sequence_count, local_residue_rows, chans), jnp.float32),
    )
    totals, outputs = lax.scan(advance, start, (right_blocks, grad_blocks))
    w_total, b_total, left_grad = totals
    pair_representation_update = jnp.moveaxis(outputs[0], 0, 1).reshape(
        local_residue_rows, total_res, pair_ch
    )
    partial_right = jnp.moveaxis(outputs[1], 0, 1).reshape(sequence_count, total_res * chans)
    right_grad = lax.psum_scatter(partial_right, "dap", scatter_dimension=1, tiled=True).reshape(
        sequence_count, local_residue_rows, chans
    )
    highest = lax.Precision.HIGHEST
    normed32 = normed.astype(jnp.float32)
    left_w_part = jnp.einsum("sih,sic->hc", normed32, left_grad, precision=highest)
    right_w_part = jnp.einsum("sih,sic->hc", normed32, right_grad, precision=highest)
    left_bias_part = jnp.sum(left_grad, axis=(0, 1))
    right_bias_part = jnp.sum(right_grad, axis=(0, 1))
    normalized_gradient = jnp.einsum(
        "sic,hc->sih", left_grad, first_operand_kernel.astype(jnp.float32), precision=highest
    )
    normalized_gradient = normalized_gradient + jnp.einsum(
        "sic,hc->sih", right_grad, second_operand_kernel.astype(jnp.float32), precision=highest
    )
    unused_out, backward_function = jax.vjp(
        normalize, activations_fp32, standardizer_scale, standardizer_shift
    )
    alignment_gradient, gain_gradient_share, offset_gradient_share = backward_function(
        normalized_gradient
    )
    summed = lax.psum(
        (
            gain_gradient_share,
            offset_gradient_share,
            left_w_part,
            left_bias_part,
            right_w_part,
            right_bias_part,
            w_total,
            b_total,
        ),
        "dap",
    )
    (
        norm_gain_gradient,
        norm_offset_gradient,
        left_weight_gradient,
        left_bias_gradient,
        right_weight_gradient,
        right_bias_gradient,
        w_sum,
        b_sum,
    ) = summed
    return (
        pair_representation_update,
        alignment_gradient,
        norm_gain_gradient,
        norm_offset_gradient,
        left_weight_gradient,
        left_bias_gradient,
        right_weight_gradient,
        right_bias_gradient,
        w_sum * scale_root,
        b_sum * scale_root,
    )


def solution(mesh):
    in_specs = (
        P("dp", "dap", None),
        P(),
        P(),
        P(),
        P(),
        P(),
        P(),
        P(),
        P(),
        P(("dp", "dap"), None, None),
    )
    out_specs = (
        P(("dp", "dap"), None, None),
        P("dp", "dap", None),
        P("dp"),
        P("dp"),
        P("dp", None),
        P("dp"),
        P("dp", None),
        P("dp"),
        P("dp", None),
        P("dp"),
    )
    return jax.shard_map(
        per_device, mesh=mesh, in_specs=in_specs, out_specs=out_specs, check_vma=False
    )
```

profile of v0, /device:TPU:8, one launch (start us, length us, event | category | flops | bytes accessed | tf_op | source)
XLA Modules:
  0.0 1407.2 jit_solution(14881228522786549975)
XLA Ops:
  9.4 1.2 fusion.40
  11.4 1.2 fusion.41
  12.7 109.2 %all-gather.2.cloned.1.call-done = bf16[32,32768]{1,0:T(8,128)(2,1)} async-done(((bf16[32,256]{1,0:T(8,128)(2,1)}), bf16[32,32768]{1,0:T(8,128)(2,1)}) %all-gather.2.cloned.1.call-update) | async-done | bytes 2097168 | tf_op jit(solution)/shard_map/all_gather | solution.py:57
  121.9 8.5 reshape_reshape.3
  130.4 8.6 copy.49
  139.0 123.9 %while.19 = (s32[]{:T(128)}, f32[1024,128]{1,0:T(8,128)S(1)}, f32[128]{0:T(128)S(1)}, f32[32,8,32]{2,0,1:T(8,128)S(1)}, bf16[8,8,128,128]{3,2,1,0:T(8,128)(2,1)}...) while((s32[]{:T(128)}, f32[1024,128]{1,0:T(8,128)S(1)}, ...), condition=%wide.region_4.5_spmd.clone, body=%wide.region_2.4_spmd.clone.sunk | while | flops 1011769472 | bytes 29725324 | solution.py:109
  139.0 1.1 convert_reduce_fusion.3
  140.8 2.6 copy.104
  143.4 2.2 copy.105
  145.6 2.7 fusion.107
  148.3 1.6 fusion.104
  151.6 1.3 fusion.109
  156.3 2.6 copy.104
  158.9 2.2 copy.105
  161.1 2.7 fusion.107
  163.8 1.6 fusion.104
  167.1 1.3 fusion.109
  169.9 1.1 convert_reduce_fusion.3
  171.8 2.6 copy.104
  174.3 2.2 copy.105
  176.6 2.7 fusion.107
  179.3 1.6 fusion.104
  182.6 1.3 fusion.109
  187.3 2.6 copy.104
  189.8 2.2 copy.105
  192.1 2.7 fusion.107
  194.8 1.6 fusion.104
  198.1 1.3 fusion.109
  200.9 1.1 convert_reduce_fusion.3
  202.8 2.6 copy.104
  205.3 2.2 copy.105
  207.6 2.7 fusion.107
  210.3 1.6 fusion.104
  213.6 1.3 fusion.109
  218.2 2.6 copy.104
  220.8 2.2 copy.105
  223.0 2.7 fusion.107
  225.8 1.6 fusion.104
  229.1 1.3 fusion.109
  233.7 2.6 copy.104
  236.3 2.2 copy.105
  238.5 2.7 fusion.107
  241.3 1.6 fusion.104
  244.6 1.3 fusion.109
  249.2 2.6 copy.104
  251.8 2.2 copy.105
  254.0 2.7 fusion.107
  256.7 1.6 fusion.104
  260.0 1.3 fusion.109
  263.9 10.6 copy.54
  274.6 11.6 reshape.86
  286.3 1.5 copy-done.3
  287.8 1.5 copy.52
  291.1 188.3 %all-reduce.4.cloned.1.call-done = f32[1024,128]{1,0:T(8,128)} async-done(((f32[1024,128]{1,0:T(8,128)}), f32[1024,128]{1,0:T(8,128)}) %all-reduce.4.cloned.1.call-update) | async-done | bytes 524304 | tf_op jit(solution)/shard_map/psum | solution.py:136
  479.4 1.9 broadcast_multiply_fusion
  481.3 693.6 %reduce-scatter.2.cloned.1.call-done = f32[32,256]{1,0:T(8,128)} async-done(((f32[32,32768]{1,0:T(8,128)}), f32[32,256]{1,0:T(8,128)}) %reduce-scatter.2.cloned.1.call-update) | async-done | bytes 32784 | tf_op jit(solution)/shard_map/reduce_scatter | solution.py:115
  1180.6 211.5 %all-reduce.6.cloned.1.call-done = (f32[256]{0:T(256)}, f32[256]{0:T(256)}, f32[256,32]{0,1:T(8,128)}, f32[32]{0:T(128)}, f32[256,32]{0,1:T(8,128)}, /*index=5*/f32[32]{0:T(128)}, f32[128]{0:T(128)}) async-done(((f32[256]{0:T(256)}, f32[256]{0:T(256)}, f32[256,32]{0,1:T(8,128)}, f32[32]{0:T(128)}, f32[256,32]{0,1:T(8,128)}, /*index=5*/f32[32]{0:T(128)}, f32[128]{0:T(128)}), (f32[256]{0:T(256)}, ...) | async-done | bytes 68368 | tf_op jit(solution)/shard_map/psum | solution.py:136
  1392.1 1.1 broadcast_multiply_fusion.2
  1393.2 1.2 copy.134
  1394.4 1.2 copy.135
  1395.6 1.4 copy.136
  1397.0 1.1 copy.137
  1398.1 1.4 copy.138
  1399.5 1.2 copy.139
  (104 shorter events, 48.1 us)
Async XLA Ops:
  7.2 2.2 copy-start
  7.2 114.7 %all-gather.2.cloned.1.call-start = ((), (), s32[]{:S(2)}) async-start(), calls=%async_computation.1 | async-start | bytes 2113536 | tf_op jit(solution)/shard_map/all_gather | solution.py:57
  11.3 468.1 %all-reduce.4.cloned.1.call-start = ((), (), s32[]{:S(2)}) async-start(), calls=%async_computation.3 | async-start | bytes 1048576 | tf_op jit(solution)/shard_map/psum | solution.py:136
  130.4 8.6 copy-start.1
  130.4 8.6 copy-start.9
  262.9 0.8 copy-start.4
  262.9 11.7 copy-start.5
  263.7 911.2 %reduce-scatter.2.cloned.1.call-start = ((), (), s32[]{:S(2)}) async-start(), calls=%async_computation.2 | async-start | bytes 4227072 | tf_op jit(solution)/shard_map/reduce_scatter | solution.py:115
  286.2 1.6 copy-start.3
  286.2 1105.9 %all-reduce.6.cloned.1.call-start = ((), (), s32[]{:S(2)}) async-start(), calls=%async_computation.4 | async-start | bytes 138240 | tf_op jit(solution)/shard_map/psum | solution.py:136
  287.8 2.0 copy-start.2
  287.8 2.0 copy-start.7
  287.8 2.0 copy-start.8
  287.8 3.0 copy-start.6
Sparse Core Ops, SparseCore 0:
  12.0 109.8 all-gather.1
  263.8 215.5 all-reduce.3
  482.1 692.7 reduce-scatter.1
  1182.3 209.7 all-reduce.5
where the time goes:
time: 1410 us
  waiting for transfers between devices  1200 us (85%)
  local copies, waits for them, and re-layouts  103 us (7%)
  matrix products  69.4 us (5%)
  other arithmetic  17.5 us (1%)
    reduce_scatter x1, waiting for transfers between devices, per_device(): lax.psum_scatter(partial_right, 'dap', scatter_dimension=1, tiled=True)  694 us
    psum x2, waiting for transfers between devices, per_device(): lax.psum((gain_gradient_share, offset_gradient_share, left_w_part, left_b...  400 us
    all_gather x1, waiting for transfers between devices, per_device(): lax.all_gather(right_proj.reshape(sequence_count, local_residue_rows * ch...  109 us
  transfers between devices with their start and end apart: 4, of which 4 were waited for; matrix products, arithmetic and copies ran while one was open for 2% of the time, Pallas kernels for 0%

commit v1 on v0

v1 whole, which is shorter than its diff:
```python
import math

import jax
import jax.numpy as jnp
from jax import lax
from jax.experimental import pallas as pl
from jax.experimental.pallas import tpu as pltpu
from jax.sharding import Mesh, PartitionSpec as P

EPSILON = 1e-05
F32 = jnp.float32
BF16 = jnp.bfloat16
S = 32
I = 8
C = 32
H = 256
Z = 128
J = 1024
NX, NZ, NY = 4, 8, 4
ND = NX * NZ * NY
Q = J // NX
SCALE = 1.0 / (math.sqrt(J) * S)
ROOT = 1.0 / math.sqrt(J)
NT = (((1,), (1,)), ((), ()))
TN = (((0,), (0,)), ((), ()))
PARAMS = pltpu.CompilerParams(vmem_limit_bytes=52 * 1024 * 1024)


def dot(a, b, dims=(((1,), (0,)), ((), ()))):
    return lax.dot_general(a, b, dims, preferred_element_type=F32)


def iota(shape, dim):
    return lax.broadcasted_iota(jnp.int32, shape, dim)


def one_hot(condition):
    return jnp.where(condition, 1.0, 0.0).astype(BF16)


def to_residue_major():
    row, col = iota((I * S, I * S), 0), iota((I * S, I * S), 1)
    return one_hot((row // S == col % I) & (row % S == col // I))


def split(value):
    high = value.astype(BF16)
    return high, (value - high.astype(F32)).astype(BF16)


def layer_norm_parts(x_ref):
    features = x_ref[...].astype(F32).reshape(S * I, H)
    average = jnp.mean(features, axis=-1, keepdims=True)
    centred = features - average
    spread = jnp.mean(centred * centred, axis=-1, keepdims=True)
    inverse = lax.rsqrt(spread + EPSILON)
    return centred, inverse


def rows_of(g_ref, quarter):
    start = pl.multiple_of(quarter * Q, Q)
    return jnp.concatenate([g_ref[i, pl.ds(start, Q), :] for i in range(I)], axis=1)


def first_kernel(
    x_ref, gain_ref, shift_ref, k1_ref, b1_ref, k2_ref, b2_ref, w_ref, g_ref,
    left_ref, right_ref, wd_ref, t_ref, p0_ref, p1_ref, p2_ref, p3_ref,
    w_scratch,
):
    plane = lax.axis_index("x")
    centred, inverse = layer_norm_parts(x_ref)
    normed = (centred * inverse * gain_ref[...] + shift_ref[...]).astype(BF16)
    left = (dot(normed, k1_ref[...]) + b1_ref[...]).astype(BF16)
    right = (dot(normed, k2_ref[...]) + b2_ref[...]).astype(BF16)
    left = dot(to_residue_major(), left).astype(BF16)
    left_ref[...] = left
    spread = dot(right, one_hot(iota((C, C * S), 0) == iota((C, C * S), 1) // S))
    keep = iota((S * I, C * S), 0) // I == iota((S * I, C * S), 1) % S
    kept = jnp.where(keep, spread, 0.0).astype(BF16)
    gather = one_hot(iota((I, S * I), 0) == iota((I, S * I), 1) % I)
    right_ref[...] = dot(gather, kept).astype(BF16)
    w_scratch[...] = w_ref[...].astype(F32)
    for d in range(C):
        wd_ref[:, d * Z : (d + 1) * Z] = w_scratch[pl.ds(d, C, stride=C), :].astype(BF16)
    for d in range(0, C, 2):
        block = dot(left, wd_ref[:, d * Z : (d + 2) * Z]).astype(BF16)
        for e in range(2):
            for i in range(I):
                t_ref[(d + e) * S : (d + e + 1) * S, i * Z : (i + 1) * Z] = block[
                    i * S : (i + 1) * S, e * Z : (e + 1) * Z
                ]
    for k, out in enumerate((p0_ref, p1_ref, p2_ref, p3_ref)):
        rows = rows_of(g_ref, (plane + k) % NX)
        out[...] = (dot(rows, t_ref[...], NT) * SCALE).astype(BF16)


def second_kernel(
    r0_ref, r1_ref, r2_ref, r3_ref, g_ref, left_ref, wd_ref, t_ref, bias_ref,
    x_ref, gain_ref, shift_ref, k1_ref, k2_ref, pieces_ref,
    update_ref, align_ref, pack_ref,
    rt_scratch, m_scratch, w_scratch,
):
    plane = lax.axis_index("x")
    bias = jnp.concatenate([bias_ref[...]] * I, axis=1)
    rights = (r0_ref, r1_ref, r2_ref, r3_ref)
    quarters = [(plane + NX - k) % NX for k in range(NX)]
    for k in range(NX):
        rt_scratch[:, k * Q : (k + 1) * Q] = rights[k][...].T
    for k in range(NX):
        block = (dot(rights[k][...], t_ref[...]) * (1.0 / S) + bias).astype(BF16)
        start = pl.multiple_of(quarters[k] * Q, Q)
        for i in range(I):
            update_ref[i, pl.ds(start, Q), :] = block[:, i * Z : (i + 1) * Z]
    bias_grad = jnp.zeros((1, Z), F32)
    for i in range(0, I, 2):
        pair = []
        for n in (i, i + 1):
            parts = [g_ref[n, pl.ds(pl.multiple_of(q * Q, Q), Q), :] for q in quarters]
            pair.append(jnp.concatenate(parts, axis=0))
            bias_grad = bias_grad + jnp.sum(pair[-1].astype(F32), axis=0, keepdims=True)
        u = dot(rt_scratch[...], jnp.concatenate(pair, axis=1)).astype(BF16)
        for e in range(2):
            for d in range(C):
                m_scratch[(i + e) * S : (i + e + 1) * S, d * Z : (d + 1) * Z] = u[
                    d * S : (d + 1) * S, e * Z : (e + 1) * Z
                ]
    left_grad = dot(m_scratch[...], wd_ref[...], NT) * SCALE
    w_part = dot(left_ref[...], m_scratch[...], TN) * SCALE
    for d in range(C):
        w_scratch[d * C : (d + 1) * C, :] = w_part[:, d * Z : (d + 1) * Z]
    total = jnp.sum(pieces_ref[...].astype(F32).reshape(NZ * NY, I, C * S), axis=0)
    high, low = split(total)
    scatter = one_hot(iota((S * I, I), 0) % I == iota((S * I, I), 1))
    keep = iota((S * I, C * S), 0) // I == iota((S * I, C * S), 1) % S
    fold = one_hot(iota((C * S, C), 0) // S == iota((C * S, C), 1))
    rg_high, rg_low = [
        dot(jnp.where(keep, dot(scatter, part), 0.0).astype(BF16), fold) for part in (high, low)
    ]
    right_grad = rg_high + rg_low
    high, low = split(left_grad)
    order = to_residue_major()
    left_grad = dot(order, high, TN) + dot(order, low, TN)
    lg_high, lg_low = split(left_grad)
    rg_high, rg_low = rg_high.astype(BF16), rg_low.astype(BF16)
    normed_grad = (
        dot(lg_high, k1_ref[...], NT)
        + dot(lg_low, k1_ref[...], NT)
        + dot(rg_high, k2_ref[...], NT)
        + dot(rg_low, k2_ref[...], NT)
    )
    centred, inverse = layer_norm_parts(x_ref)
    unit = centred * inverse
    normed = (unit * gain_ref[...] + shift_ref[...]).astype(BF16)
    unit_grad = normed_grad * gain_ref[...]
    mean_one = jnp.mean(unit_grad, axis=-1, keepdims=True)
    mean_two = jnp.mean(unit_grad * unit, axis=-1, keepdims=True)
    align_ref[...] = (inverse * (unit_grad - mean_one - unit * mean_two)).reshape(S, I, H)
    gain_grad = jnp.sum(normed_grad * unit, axis=0, keepdims=True)
    offset_grad = jnp.sum(normed_grad, axis=0, keepdims=True)
    both = jnp.concatenate([lg_high, rg_high, lg_low, rg_low], axis=1)
    weights = dot(both, normed, TN)
    weights = weights[: 2 * C] + weights[2 * C :]
    weights = jnp.concatenate([weights[:, :Z], weights[:, Z:]], axis=0)
    biases = jnp.sum(jnp.concatenate([left_grad, right_grad], axis=1), axis=0, keepdims=True)
    biases = jnp.concatenate([biases, jnp.zeros((1, Z - 2 * C), F32)], axis=1)
    row = iota((ND, Z), 0)
    others = jnp.zeros((ND, Z), F32)
    for n, value in enumerate(
        (gain_grad[:, :Z], gain_grad[:, Z:], offset_grad[:, :Z], offset_grad[:, Z:], biases, bias_grad)
    ):
        others = jnp.where(row == n, value, others)
    pack_ref[...] = packed(w_scratch[...].reshape(ND, 8, Z), weights, others)


def packed(w_rows, weights, others):
    where = iota((w_rows.shape[0], 8, Z), 1)
    block = jnp.zeros(where.shape, F32)
    n = 0
    for table in (weights, others):
        for half in split(table):
            block = jnp.where(where == n, half.astype(F32)[:, None, :], block)
            n += 1
    return jnp.concatenate([w_rows, block], axis=1).astype(BF16)


def sum_kernel(in_ref, out_ref):
    total = jnp.sum(in_ref[...].astype(F32), axis=0)
    block = packed(total[None, :8], total[8:9] + total[9:10], total[10:11] + total[11:12])
    out_ref[...] = jnp.broadcast_to(block, (ND, 16, Z))


def last_kernel(
    in_ref, gain_ref, offset_ref, lw_ref, lb_ref, rw_ref, rb_ref, w_ref, wb_ref, scratch, w_scratch
):
    blocks = in_ref[...].astype(F32)
    scratch[...] = blocks[:, 8:].reshape(ND * 8, Z)
    w_scratch[...] = blocks[:, :8].reshape(ND * 8, Z)
    for c in range(C):
        w_ref[c * C : (c + 1) * C, :] = w_scratch[pl.ds(c, C, stride=C), :]
    weights, others = [
        scratch[pl.ds(n, ND, stride=8), :] + scratch[pl.ds(n + 1, ND, stride=8), :] for n in (0, 2)
    ]
    flipped = weights.T
    lw_ref[:Z, :] = flipped[:, :C]
    lw_ref[Z:, :] = flipped[:, 2 * C : 3 * C]
    rw_ref[:Z, :] = flipped[:, C : 2 * C]
    rw_ref[Z:, :] = flipped[:, 3 * C :]
    gain_ref[:, :Z] = others[0:1]
    gain_ref[:, Z:] = others[1:2]
    offset_ref[:, :Z] = others[2:3]
    offset_ref[:, Z:] = others[3:4]
    lb_ref[...] = others[4:5, :C]
    rb_ref[...] = others[4:5, C : 2 * C]
    wb_ref[...] = others[5:6] * ROOT


def shape(dims, dtype):
    return jax.ShapeDtypeStruct(dims, dtype)


def shifted(array, step):
    return lax.ppermute(array, "x", [(n, (n + step) % NX) for n in range(NX)])


def per_device(x, gain, shift, k1, b1, k2, b2, w, bias, g):
    gain, shift, b1, b2, bias = [v.reshape(1, -1) for v in (gain, shift, b1, b2, bias)]
    left, right, wd, t, p0, p1, p2, p3 = pl.pallas_call(
        first_kernel,
        out_shape=(
            shape((I * S, C), BF16),
            shape((I, C * S), BF16),
            shape((C, C * Z), BF16),
            shape((C * S, I * Z), BF16),
        )
        + (shape((Q, C * S), BF16),) * NX,
        scratch_shapes=[pltpu.VMEM((C * C, Z), F32)],
        compiler_params=PARAMS,
        name="first",
    )(x, gain, shift, k1, b1, k2, b2, w, g)
    arrived = [shifted(p, k) for k, p in ((1, p1), (3, p3), (2, p2))]
    copies = jnp.broadcast_to(right[None], (NZ * NY, I, C * S)).reshape(Q, C * S)
    r0 = lax.all_to_all(copies, ("z", "y"), 0, 0, tiled=True)
    r1, r3, r2 = [shifted(r0, k) for k in (1, 3, 2)]
    own = p0.astype(F32)
    for p in arrived:
        own = own + p.astype(F32)
    pieces = lax.all_to_all(own.astype(BF16), ("z", "y"), 0, 0, tiled=True)
    update, align, pack = pl.pallas_call(
        second_kernel,
        out_shape=(
            shape((I, J, Z), BF16),
            shape((S, I, H), F32),
            shape((ND, 16, Z), BF16),
        ),
        scratch_shapes=[
            pltpu.VMEM((C * S, J), BF16),
            pltpu.VMEM((I * S, C * Z), BF16),
            pltpu.VMEM((C * C, Z), F32),
        ],
        compiler_params=PARAMS,
        name="second",
    )(r0, r1, r2, r3, g, left, wd, t, bias, x, gain, shift, k1, k2, pieces)
    parts = lax.all_to_all(pack, ("x", "z", "y"), 0, 0, tiled=True)
    block = pl.pallas_call(
        sum_kernel, out_shape=shape((ND, 16, Z), BF16), compiler_params=PARAMS, name="sum"
    )(parts)
    sums = lax.all_to_all(block, ("x", "z", "y"), 0, 0, tiled=True)
    gain_g, offset_g, lw, lb, rw, rb, w_g, wb = pl.pallas_call(
        last_kernel,
        out_shape=(
            shape((1, H), F32),
            shape((1, H), F32),
            shape((H, C), F32),
            shape((1, C), F32),
            shape((H, C), F32),
            shape((1, C), F32),
            shape((C * C, Z), F32),
            shape((1, Z), F32),
        ),
        scratch_shapes=[pltpu.VMEM((ND * 8, Z), F32), pltpu.VMEM((C * C, Z), F32)],
        compiler_params=PARAMS,
        name="last",
    )(sums)
    return (
        update,
        align,
        gain_g.reshape(H),
        offset_g.reshape(H),
        lw,
        lb.reshape(C),
        rw,
        rb.reshape(C),
        w_g,
        wb.reshape(Z),
    )


def solution(mesh):
    grid = Mesh(mesh.devices.reshape(NX, NZ, NY, 2), ("x", "z", "y", "dp"))
    dap = ("x", "z", "y")
    in_specs = (P("dp", dap, None),) + (P(),) * 8 + (P(("dp",) + dap, None, None),)
    out_specs = (
        P(("dp",) + dap, None, None),
        P("dp", dap, None),
        P("dp"),
        P("dp"),
        P("dp", None),
        P("dp"),
        P("dp", None),
        P("dp"),
        P("dp", None),
        P("dp"),
    )
    return jax.shard_map(
        per_device, mesh=grid, in_specs=in_specs, out_specs=out_specs, check_vma=False
    )
```

time: 1410 us -> 160 us (0.11)
  waiting for transfers between devices: 1200 us -> 43.8 us
  local copies, waits for them, and re-layouts: 103 us -> 9.42 us
  matrix products: 69.4 us -> 0 us
  blocking collectives: 0 us -> 55.7 us
  starting transfers between devices: 0.34 us -> 30.1 us
  Pallas kernels: 0 us -> 18.3 us
  other arithmetic: 17.5 us -> 1.15 us
    reduce_scatter x1 -> x0, waiting for transfers between devices: 694 us -> none  [per_device(): lax.psum_scatter(partial_right, 'dap', scatter_dimension=1, tiled=True)]
    psum x2 -> x0, waiting for transfers between devices: 400 us -> none  [per_device(): lax.psum((gain_gradient_share, offset_gradient_share, left_w_part, left_b...]
    all_gather x1 -> x0, waiting for transfers between devices: 109 us -> none  [per_device(): lax.all_gather(right_proj.reshape(sequence_count, local_residue_rows * ch...]
    dot_general x54 -> x0, matrix products: 69.4 us -> none  [the longest x8 21.9 us: advance(): jnp.einsum('ijcd,sjd->sic', grad_four, right_piece, preferred_element_typ...]
    all_to_all x0 -> x2, blocking collectives: none -> 55.7 us  [the longest x1 30.6 us: per_device(): parts = lax.all_to_all(pack, ('x', 'z', 'y'), 0, 0, tiled=True)]
    ppermute x0 -> x6, waiting for transfers between devices: none -> 43.8 us  [shifted(): return lax.ppermute(array, 'x', [(n, (n + step) % NX) for n in range(NX)])]
    convert_element_type x16 -> x0, local copies, waits for them, and re-layouts: 27.1 us -> none  [the longest x8 20.6 us: cotangent_outer(): return (product * scale_root).astype(jnp.bfloat16)]
    all_to_all x0 -> x2, starting transfers between devices: none -> 21.5 us  [the longest x1 11.7 us: per_device(): r0 = lax.all_to_all(copies, ('z', 'y'), 0, 0, tiled=True)]
  transfers between devices with their start and end apart: 4 -> 8, of which waited for: 4 -> 6; matrix products, arithmetic and copies ran while one was open for 2% -> 1% of each run, Pallas kernels for 0% -> 0%
where the time goes in v1:
time: 160 us; the launch traced here: 159 us
  blocking collectives  55.7 us (35%)
  waiting for transfers between devices  43.8 us (27%)
  starting transfers between devices  30.1 us (19%)
  Pallas kernels  18.3 us (11%)
  local copies, waits for them, and re-layouts  9.42 us (6%)
    ppermute x6, waiting for transfers between devices, shifted(): return lax.ppermute(array, 'x', [(n, (n + step) % NX) for n in range(NX)])  43.8 us
    all_to_all x1, blocking collectives, per_device(): parts = lax.all_to_all(pack, ('x', 'z', 'y'), 0, 0, tiled=True)  30.6 us
    all_to_all x1, blocking collectives, per_device(): sums = lax.all_to_all(block, ('x', 'z', 'y'), 0, 0, tiled=True)  25.1 us
    all_to_all x1, starting transfers between devices, per_device(): r0 = lax.all_to_all(copies, ('z', 'y'), 0, 0, tiled=True)  11.7 us
    pallas_call x1, Pallas kernels, per_device(): pl.pallas_call(second_kernel, out_shape=(shape((I, J, Z), BF16), shape((S...  10.8 us
    all_to_all x1, starting transfers between devices, per_device(): pieces = lax.all_to_all(own.astype(BF16), ('z', 'y'), 0, 0, tiled=True)  9.78 us
    ppermute x6, starting transfers between devices, shifted(): return lax.ppermute(array, 'x', [(n, (n + step) % NX) for n in range(NX)])  8.62 us
    unnamed x32, local copies, waits for them, and re-layouts  8.55 us
  transfers between devices with their start and end apart: 8, of which 6 were waited for; matrix products, arithmetic and copies ran while one was open for 1% of the time, Pallas kernels for 0%

profile of v1, /device:TPU:8, one launch (start us, length us, event | category | flops | bytes accessed | tf_op | source)
XLA Modules:
  0.0 159.2 jit_solution(14760610152299502112)
XLA Ops:
  0.6 0.8 copy.20.k1_ref
  1.5 0.8 copy.21.k2_ref
  2.3 0.0 copy-start
  2.3 0.9 copy-done
  3.2 0.0 copy-start.2
  3.2 0.9 copy-done.2
  4.2 0.0 copy-start.3
  4.2 0.7 copy-done.3
  4.9 0.0 copy-start.5
  4.9 0.7 copy-done.5
  5.5 0.0 copy-start.8
  5.5 0.7 copy-done.8
  6.2 0.0 copy-start.9
  6.2 0.7 copy-done.9
  6.8 6.1 %first.1 = (bf16[256,32]{1,0:T(8,128)(2,1)S(1)}, bf16[8,1024]{1,0:T(8,128)(2,1)S(1)}, bf16[32,4096]{1,0:T(8,128)(2,1)S(1)}, bf16[1024,1024]{1,0:T(8,128)(2,1)}, ...) custom-call(bf16[32,8,256]{2,1,0:T(8,128)(2,1)S(1)} %copy-done, ...), custom_call_target="tpu_custom_call" | custom-call | tf_op jit(solution)/shard_map/first/pallas_call | solution.py:227
  12.9 0.9 broadcast_in_dim.2
  13.8 11.7 %all-to-all-start = ((bf16[32,8,1024]{2,1,0:T(8,128)(2,1)}), bf16[32,8,1024]{2,1,0:T(8,128)(2,1)S(1)}, u32[]{:S(2)}, u32[]{:S(2)}) async-start(bf16[32,8,1024]{2,1,0:T(8,128)(2,1)} %broadcast_in_dim.2), calls=%async_computation | async-start | bytes 1048576 | tf_op jit(solution)/shard_map/all_to_all | solution.py:242
  25.5 0.0 copy-start.1
  25.5 0.0 copy-start.4
  25.5 0.0 copy-start.6
  25.5 0.0 copy-start.7
  25.5 1.6 collective-permute-start.3
  27.1 1.8 %collective-permute-start.4 = (bf16[256,1024]{1,0:T(8,128)(2,1)}, bf16[256,1024]{1,0:T(8,128)(2,1)S(1)}, u32[]{:S(2)}, u32[]{:S(2)}) collective-permute-start(bf16[256,1024]{1,0:T(8,128)(2,1)} %get-tuple-element.35), channel_id=1, source_target_pairs={{0,192},{64,0},{128,64},{192,128},{1,193},{65,1},{129,65},{193,129... | collective-permute-start | bytes 1572872 | tf_op jit(solution)/shard_map/ppermute | solution.py:222
  28.8 1.8 %collective-permute-start.5 = (bf16[256,1024]{1,0:T(8,128)(2,1)}, bf16[256,1024]{1,0:T(8,128)(2,1)S(1)}, u32[]{:S(2)}, u32[]{:S(2)}) collective-permute-start(bf16[256,1024]{1,0:T(8,128)(2,1)} %get-tuple-element.36), channel_id=1, source_target_pairs={{0,128},{64,192},{128,0},{192,64},{1,129},{65,193},{129,1},{193,65... | collective-permute-start | bytes 1572872 | tf_op jit(solution)/shard_map/ppermute | solution.py:222
  30.7 10.0 %collective-permute-done.3 = bf16[256,1024]{1,0:T(8,128)(2,1)S(1)} collective-permute-done((bf16[256,1024]{1,0:T(8,128)(2,1)S(1)}, bf16[256,1024]{1,0:T(8,128)(2,1)S(1)}, u32[]{:S(2)}, u32[]{:S(2)}) %collective-permute-start.3) | collective-permute-done | bytes 524320 | tf_op jit(solution)/shard_map/ppermute | solution.py:222
  40.7 10.1 %collective-permute-done.4 = bf16[256,1024]{1,0:T(8,128)(2,1)S(1)} collective-permute-done((bf16[256,1024]{1,0:T(8,128)(2,1)}, bf16[256,1024]{1,0:T(8,128)(2,1)S(1)}, u32[]{:S(2)}, u32[]{:S(2)}) %collective-permute-start.4) | collective-permute-done | bytes 524320 | tf_op jit(solution)/shard_map/ppermute | solution.py:222
  50.8 1.4 collective-permute-done.5
  52.1 1.1 fusion
  53.3 0.0 all-to-all-done
  53.3 9.8 %all-to-all-start.1 = ((bf16[32,8,1024]{2,1,0:T(8,128)(2,1)}), bf16[32,8,1024]{2,1,0:T(8,128)(2,1)S(1)}, u32[]{:S(2)}, u32[]{:S(2)}) async-start(bf16[32,8,1024]{2,1,0:T(8,128)(2,1)} %fusion), calls=%async_computation.1 | async-start | bytes 1048576 | tf_op jit(solution)/shard_map/all_to_all | solution.py:247
  63.1 2.3 %collective-permute-start.2 = (bf16[256,1024]{1,0:T(8,128)(2,1)S(1)}, bf16[256,1024]{1,0:T(8,128)(2,1)S(1)}, u32[]{:S(2)}, u32[]{:S(2)}) collective-permute-start(bf16[256,1024]{1,0:T(8,128)(2,1)S(1)} %bitcast.14), channel_id=1, source_target_pairs={{0,192},{64,0},{128,64},{192,128},{1,193},{65,1},{129,65},{193,129... | collective-permute-start | bytes 1572872 | tf_op jit(solution)/shard_map/ppermute | solution.py:222
  65.3 1.2 collective-permute-start.1
  66.6 0.0 collective-permute-start
  66.6 11.4 %collective-permute-done.2.r3_ref = bf16[256,1024]{1,0:T(8,128)(2,1)S(1)} collective-permute-done((bf16[256,1024]{1,0:T(8,128)(2,1)S(1)}, bf16[256,1024]{1,0:T(8,128)(2,1)S(1)}, u32[]{:S(2)}, u32[]{:S(2)}) %collective-permute-start.2) | collective-permute-done | bytes 524320 | tf_op jit(solution)/shard_map/ppermute | solution.py:222
  78.0 0.0 copy-start.11
  78.0 3.7 %collective-permute-done.1.r2_ref = bf16[256,1024]{1,0:T(8,128)(2,1)S(1)} collective-permute-done((bf16[256,1024]{1,0:T(8,128)(2,1)S(1)}, bf16[256,1024]{1,0:T(8,128)(2,1)S(1)}, u32[]{:S(2)}, u32[]{:S(2)}) %collective-permute-start.1) | collective-permute-done | bytes 524320 | tf_op jit(solution)/shard_map/ppermute | solution.py:222
  81.7 0.0 copy-start.12
  81.7 7.2 %collective-permute-done.r1_ref = bf16[256,1024]{1,0:T(8,128)(2,1)S(1)} collective-permute-done((bf16[256,1024]{1,0:T(8,128)(2,1)S(1)}, bf16[256,1024]{1,0:T(8,128)(2,1)S(1)}, u32[]{:S(2)}, u32[]{:S(2)}) %collective-permute-start) | collective-permute-done | bytes 524320 | tf_op jit(solution)/shard_map/ppermute | solution.py:222
  88.9 0.0 copy-start.13
  88.9 0.0 all-to-all-done.1
  88.9 0.0 copy-start.10
  88.9 0.0 copy-done.11
  88.9 0.0 copy-done.12
  88.9 0.8 copy-done.13
  89.7 0.2 copy-done.10
  89.9 0.0 copy-done.1
  89.9 0.0 copy-done.4
  89.9 0.0 copy-done.6
  89.9 0.0 copy-done.7
  89.9 10.8 %second.1 = (bf16[8,1024,128]{2,1,0:T(8,128)(2,1)}, f32[32,8,256]{2,1,0:T(8,128)}, bf16[128,16,128]{2,1,0:T(8,128)(2,1)S(1)}) custom-call(bf16[256,1024]{1,0:T(8,128)(2,1)S(1)} %bitcast.17, bf16[256,1024]{1,0:T(8,128)(2,1)} %copy-done.13, bf16[256,1024]{1,0:T(8,128)(2,1)} %copy-done.12, bf16[256,1024]{1,0:T(8,128)(2,1)} %copy-done.11, ...), custom_call_target="tpu_custom_call" | custom-call | tf_op jit(solution)/shard_map/second/pallas_call | solution.py:248
  100.7 30.6 %all_to_all.29.in_ref = bf16[128,16,128]{2,1,0:T(8,128)(2,1)S(1)} all-to-all(bf16[128,16,128]{2,1,0:T(8,128)(2,1)S(1)} %get-tuple-element.39), channel_id=1, replica_groups=mesh['x'=4,'z'=8,'y'=4,'dp'=2] {'x','z','y'}, dimensions={0} | all-to-all | bytes 1048576 | tf_op jit(solution)/shard_map/all_to_all | solution.py:263
  131.3 0.2 sum.1
  131.5 25.1 %all_to_all.30.in_ref = bf16[128,16,128]{2,1,0:T(8,128)(2,1)S(1)} all-to-all(bf16[128,16,128]{2,1,0:T(8,128)(2,1)S(1)} %sum.1), channel_id=1, replica_groups=mesh['x'=4,'z'=8,'y'=4,'dp'=2] {'x','z','y'}, dimensions={0} | all-to-all | bytes 1048576 | tf_op jit(solution)/shard_map/all_to_all | solution.py:267
  156.6 1.3 last.1
  157.8 0.7 copy.24
  158.5 0.7 copy.25
Async XLA Ops:
  2.3 0.9 copy-start
  3.2 0.9 copy-start.2
  4.2 0.7 copy-start.3
  4.9 0.7 copy-start.5
  5.5 0.7 copy-start.8
  6.2 0.7 copy-start.9
  13.8 39.5 %all-to-all-start = ((bf16[32,8,1024]{2,1,0:T(8,128)(2,1)}), bf16[32,8,1024]{2,1,0:T(8,128)(2,1)S(1)}, u32[]{:S(2)}, u32[]{:S(2)}) async-start(bf16[32,8,1024]{2,1,0:T(8,128)(2,1)} %broadcast_in_dim.2), calls=%async_computation | async-start | bytes 1048576 | tf_op jit(solution)/shard_map/all_to_all | solution.py:242
  25.5 64.4 %copy-start.1 = (bf16[32,8,256]{2,1,0:T(8,128)(2,1)S(1)}, bf16[32,8,256]{2,1,0:T(8,128)(2,1)}, u32[]{:S(2)}) copy-start(bf16[32,8,256]{2,1,0:T(8,128)(2,1)} %x_ref.3) | copy-start | bytes 393220
  25.5 64.4 %copy-start.4 = (f32[256]{0:T(256)S(1)}, f32[256]{0:T(256)}, u32[]{:S(2)}) copy-start(f32[256]{0:T(256)} %param.11) | copy-start | bytes 3076
  25.5 64.4 %copy-start.6 = (f32[256]{0:T(256)S(1)}, f32[256]{0:T(256)}, u32[]{:S(2)}) copy-start(f32[256]{0:T(256)} %param.12) | copy-start | bytes 3076
  25.5 64.4 %copy-start.7 = (f32[128]{0:T(128)S(1)}, f32[128]{0:T(128)}, u32[]{:S(2)}) copy-start(f32[128]{0:T(128)} %param.18) | copy-start | bytes 1540
  25.5 15.2 %collective-permute-start.3 = (bf16[256,1024]{1,0:T(8,128)(2,1)S(1)}, bf16[256,1024]{1,0:T(8,128)(2,1)S(1)}, u32[]{:S(2)}, u32[]{:S(2)}) collective-permute-start(bf16[256,1024]{1,0:T(8,128)(2,1)S(1)} %get-tuple-element.34), channel_id=1, source_target_pairs={{0,64},{64,128},{128,192},{192,0},{1,65},{65,129},{129,193},{193,1... | collective-permute-start | bytes 1572872 | tf_op jit(solution)/shard_map/ppermute | solution.py:222
  27.1 23.7 %collective-permute-start.4 = (bf16[256,1024]{1,0:T(8,128)(2,1)}, bf16[256,1024]{1,0:T(8,128)(2,1)S(1)}, u32[]{:S(2)}, u32[]{:S(2)}) collective-permute-start(bf16[256,1024]{1,0:T(8,128)(2,1)} %get-tuple-element.35), channel_id=1, source_target_pairs={{0,192},{64,0},{128,64},{192,128},{1,193},{65,1},{129,65},{193,129... | collective-permute-start | bytes 1572872 | tf_op jit(solution)/shard_map/ppermute | solution.py:222
  28.8 23.3 %collective-permute-start.5 = (bf16[256,1024]{1,0:T(8,128)(2,1)}, bf16[256,1024]{1,0:T(8,128)(2,1)S(1)}, u32[]{:S(2)}, u32[]{:S(2)}) collective-permute-start(bf16[256,1024]{1,0:T(8,128)(2,1)} %get-tuple-element.36), channel_id=1, source_target_pairs={{0,128},{64,192},{128,0},{192,64},{1,129},{65,193},{129,1},{193,65... | collective-permute-start | bytes 1572872 | tf_op jit(solution)/shard_map/ppermute | solution.py:222
  53.3 35.6 %all-to-all-start.1 = ((bf16[32,8,1024]{2,1,0:T(8,128)(2,1)}), bf16[32,8,1024]{2,1,0:T(8,128)(2,1)S(1)}, u32[]{:S(2)}, u32[]{:S(2)}) async-start(bf16[32,8,1024]{2,1,0:T(8,128)(2,1)} %fusion), calls=%async_computation.1 | async-start | bytes 1048576 | tf_op jit(solution)/shard_map/all_to_all | solution.py:247
  63.1 14.9 %collective-permute-start.2 = (bf16[256,1024]{1,0:T(8,128)(2,1)S(1)}, bf16[256,1024]{1,0:T(8,128)(2,1)S(1)}, u32[]{:S(2)}, u32[]{:S(2)}) collective-permute-start(bf16[256,1024]{1,0:T(8,128)(2,1)S(1)} %bitcast.14), channel_id=1, source_target_pairs={{0,192},{64,0},{128,64},{192,128},{1,193},{65,1},{129,65},{193,129... | collective-permute-start | bytes 1572872 | tf_op jit(solution)/shard_map/ppermute | solution.py:222
  65.3 16.4 %collective-permute-start.1 = (bf16[256,1024]{1,0:T(8,128)(2,1)S(1)}, bf16[256,1024]{1,0:T(8,128)(2,1)S(1)}, u32[]{:S(2)}, u32[]{:S(2)}) collective-permute-start(bf16[256,1024]{1,0:T(8,128)(2,1)S(1)} %bitcast.15), channel_id=1, source_target_pairs={{0,128},{64,192},{128,0},{192,64},{1,129},{65,193},{129,1},{193,65... | collective-permute-start | bytes 1572872 | tf_op jit(solution)/shard_map/ppermute | solution.py:222
  66.6 22.3 %collective-permute-start = (bf16[256,1024]{1,0:T(8,128)(2,1)S(1)}, bf16[256,1024]{1,0:T(8,128)(2,1)S(1)}, u32[]{:S(2)}, u32[]{:S(2)}) collective-permute-start(bf16[256,1024]{1,0:T(8,128)(2,1)S(1)} %bitcast.16), channel_id=1, source_target_pairs={{0,64},{64,128},{128,192},{192,0},{1,65},{65,129},{129,193},{193,1... | collective-permute-start | bytes 1572872 | tf_op jit(solution)/shard_map/ppermute | solution.py:222
  78.0 10.9 %copy-start.11 = (bf16[256,1024]{1,0:T(8,128)(2,1)}, bf16[256,1024]{1,0:T(8,128)(2,1)S(1)}, u32[]{:S(2)}) copy-start(bf16[256,1024]{1,0:T(8,128)(2,1)S(1)} %collective-permute-done.2.r3_ref) | copy-start | bytes 1572868
  81.7 7.2 %copy-start.12 = (bf16[256,1024]{1,0:T(8,128)(2,1)}, bf16[256,1024]{1,0:T(8,128)(2,1)S(1)}, u32[]{:S(2)}) copy-start(bf16[256,1024]{1,0:T(8,128)(2,1)S(1)} %collective-permute-done.1.r2_ref) | copy-start | bytes 1572868
  88.9 0.8 copy-start.13
  88.9 1.0 copy-start.10

commit v2 on v1

v2 whole, which is shorter than its diff:
```python
import math

import jax
import jax.numpy as jnp
from jax import lax
from jax.experimental import pallas as pl
from jax.experimental.pallas import tpu as pltpu
from jax.sharding import Mesh, PartitionSpec as P

EPSILON = 1e-05
F32 = jnp.float32
BF16 = jnp.bfloat16
S = 32
I = 8
C = 32
H = 256
Z = 128
J = 1024
NX, NZ, NY = 4, 8, 4
ND = NX * NZ * NY
Q = J // NX
SCALE = 1.0 / (math.sqrt(J) * S)
ROOT = 1.0 / math.sqrt(J)
NT = (((1,), (1,)), ((), ()))
TN = (((0,), (0,)), ((), ()))
MIB = 1024 * 1024


def dot(a, b, dims=(((1,), (0,)), ((), ()))):
    return lax.dot_general(a, b, dims, preferred_element_type=F32)


def iota(shape, dim):
    return lax.broadcasted_iota(jnp.int32, shape, dim)


def one_hot(condition):
    return jnp.where(condition, 1.0, 0.0).astype(BF16)


def to_residue_major():
    row, col = iota((I * S, I * S), 0), iota((I * S, I * S), 1)
    return one_hot((row // S == col % I) & (row % S == col // I))


def split(value):
    high = value.astype(BF16)
    return high, (value - high.astype(F32)).astype(BF16)


def layer_norm_parts(x_ref):
    features = x_ref[...].astype(F32)
    average = jnp.mean(features, axis=-1, keepdims=True)
    centred = features - average
    spread = jnp.mean(centred * centred, axis=-1, keepdims=True)
    inverse = lax.rsqrt(spread + EPSILON)
    return centred, inverse


def rows_of(g_ref, quarter):
    start = pl.multiple_of(quarter * Q, Q)
    return jnp.concatenate([g_ref[i, pl.ds(start, Q), :] for i in range(I)], axis=1)


def copies_between(sources, targets, sems):
    return [pltpu.make_async_copy(a, b, sems.at[n]) for n, (a, b) in enumerate(zip(sources, targets))]


def first_kernel(*refs):
    inputs, outputs, held, (made, w_scratch, in_sems, out_sems) = (
        refs[:9], refs[9:17], refs[17:26], (refs[26:30], *refs[30:])
    )
    x_ref, gain_ref, shift_ref, k1_ref, b1_ref, k2_ref, b2_ref, w_ref, g_ref = held
    left_ref, copies_ref, wd_ref, t_ref = made
    partial_refs = outputs[4:]
    plane = lax.axis_index("x")
    loads = copies_between(inputs, held, in_sems)
    stores = copies_between(made, outputs, out_sems)
    for load in loads:
        load.start()
    for load in loads[:7]:
        load.wait()
    centred, inverse = layer_norm_parts(x_ref)
    normed = (centred * inverse * gain_ref[...] + shift_ref[...]).astype(BF16)
    left = (dot(normed, k1_ref[...], NT) + b1_ref[...]).astype(BF16)
    right = (dot(normed, k2_ref[...], NT) + b2_ref[...]).astype(BF16)
    left = dot(to_residue_major(), left).astype(BF16)
    left_ref[...] = left
    stores[0].start()
    spread = dot(right, one_hot(iota((C, C * S), 0) == iota((C, C * S), 1) // S))
    keep = iota((S * I, C * S), 0) // I == iota((S * I, C * S), 1) % S
    kept = jnp.where(keep, spread, 0.0).astype(BF16)
    gather = one_hot(iota((Q, S * I), 0) % I == iota((Q, S * I), 1) % I)
    copies_ref[...] = dot(gather, kept).astype(BF16)
    stores[1].start()
    loads[7].wait()
    w_scratch[...] = w_ref[...].astype(F32)
    for d in range(C):
        wd_ref[:, d * Z : (d + 1) * Z] = w_scratch[pl.ds(d, C, stride=C), :].astype(BF16)
    stores[2].start()
    for d in range(0, C, 2):
        block = dot(left, wd_ref[:, d * Z : (d + 2) * Z]).astype(BF16)
        for e in range(2):
            for i in range(I):
                t_ref[(d + e) * S : (d + e + 1) * S, i * Z : (i + 1) * Z] = block[
                    i * S : (i + 1) * S, e * Z : (e + 1) * Z
                ]
    stores[3].start()
    loads[8].wait()
    for k in (1, 3, 2, 0):
        rows = rows_of(g_ref, (plane + k) % NX)
        partial_refs[k][...] = (dot(rows, t_ref[...], NT) * SCALE).astype(BF16)
    for store in stores:
        store.wait()


def fold_kernel(a_ref, b_ref, c_ref, d_ref, out_ref):
    step = 16
    for n in range(0, Q, step):
        rows = pl.ds(n, step)
        total = a_ref[rows, :].astype(F32) + b_ref[rows, :].astype(F32)
        total = total + (c_ref[rows, :].astype(F32) + d_ref[rows, :].astype(F32))
        out_ref[rows, :] = total.astype(BF16)


def quarters_of():
    plane = lax.axis_index("x")
    return [(plane + NX - k) % NX for k in range(NX)]


def update_kernel(*refs):
    inputs, bias_ref, update_hbm, (held, update_ref, in_sems, out_sems) = (
        refs[:5], refs[5], refs[6], (refs[7:12], *refs[12:])
    )
    loads = copies_between(inputs, held, in_sems)
    for n in (4, 0, 1, 2, 3):
        loads[n].start()
    loads[4].wait()
    stores = []
    bias = jnp.concatenate([bias_ref[...]] * I, axis=1)
    for k, quarter in enumerate(quarters_of()):
        loads[k].wait()
        block = (dot(held[k][...], held[4][...]) * (1.0 / S) + bias).astype(BF16)
        rows = pl.ds(pl.multiple_of(quarter * Q, Q), Q)
        for i in range(I):
            update_ref[k, i] = block[:, i * Z : (i + 1) * Z]
        stores.append(pltpu.make_async_copy(update_ref.at[k], update_hbm.at[:, rows, :], out_sems.at[k]))
        stores[-1].start()
    for store in stores:
        store.wait()


def second_kernel(
    r0_any, r1_any, r2_any, r3_any, g_hbm, wd_hbm, left_ref,
    left_grad_ref, w_part_ref, bias_grad_ref,
    r0_ref, r1_ref, r2_ref, r3_ref, g_ref, wd_ref, rt_scratch, m_scratch, sems,
):
    quarters = quarters_of()
    sources = (r0_any, r1_any, r2_any, r3_any, g_hbm, wd_hbm)
    held = (r0_ref, r1_ref, r2_ref, r3_ref, g_ref, wd_ref)
    loads = copies_between(sources, held, sems)
    for load in loads:
        load.start()
    for k in range(NX):
        loads[k].wait()
        rt_scratch[:, k * Q : (k + 1) * Q] = held[k][...].T
    loads[4].wait()
    bias_grad = jnp.zeros((1, Z), F32)
    for i in range(0, I, 2):
        pair = []
        for n in (i, i + 1):
            parts = [g_ref[n, pl.ds(pl.multiple_of(q * Q, Q), Q), :] for q in quarters]
            pair.append(jnp.concatenate(parts, axis=0))
            bias_grad = bias_grad + jnp.sum(pair[-1].astype(F32), axis=0, keepdims=True)
        u = dot(rt_scratch[...], jnp.concatenate(pair, axis=1)).astype(BF16)
        for e in range(2):
            for d in range(C):
                m_scratch[(i + e) * S : (i + e + 1) * S, d * Z : (d + 1) * Z] = u[
                    d * S : (d + 1) * S, e * Z : (e + 1) * Z
                ]
    bias_grad_ref[...] = bias_grad
    loads[5].wait()
    left_grad_ref[...] = dot(m_scratch[...], wd_ref[...], NT) * SCALE
    w_part = dot(left_ref[...], m_scratch[...], TN) * SCALE
    for d in range(C):
        w_part_ref[d] = w_part[:, d * Z : (d + 1) * Z].astype(BF16)


def third_kernel(
    left_grad_ref, w_hbm, bias_grad_ref, x_ref, gain_ref, shift_ref, k1_ref, k2_ref, pieces_ref,
    align_ref, pack_ref, w_ref, sem,
):
    load = pltpu.make_async_copy(w_hbm, w_ref, sem)
    load.start()
    total = jnp.sum(pieces_ref[...].astype(F32).reshape(NZ * NY, I, C * S), axis=0)
    high, low = split(total)
    scatter = one_hot(iota((S * I, I), 0) % I == iota((S * I, I), 1))
    keep = iota((S * I, C * S), 0) // I == iota((S * I, C * S), 1) % S
    fold = one_hot(iota((C * S, C), 0) // S == iota((C * S, C), 1))
    rg_high, rg_low = [
        dot(jnp.where(keep, dot(scatter, part), 0.0).astype(BF16), fold) for part in (high, low)
    ]
    right_grad = rg_high + rg_low
    high, low = split(left_grad_ref[...])
    order = to_residue_major()
    left_grad = dot(order, high, TN) + dot(order, low, TN)
    lg_high, lg_low = split(left_grad)
    rg_high, rg_low = rg_high.astype(BF16), rg_low.astype(BF16)
    normed_grad = (
        dot(lg_high, k1_ref[...])
        + dot(lg_low, k1_ref[...])
        + dot(rg_high, k2_ref[...])
        + dot(rg_low, k2_ref[...])
    )
    centred, inverse = layer_norm_parts(x_ref)
    unit = centred * inverse
    normed = (unit * gain_ref[...] + shift_ref[...]).astype(BF16)
    unit_grad = normed_grad * gain_ref[...]
    mean_one = jnp.mean(unit_grad, axis=-1, keepdims=True)
    mean_two = jnp.mean(unit_grad * unit, axis=-1, keepdims=True)
    align_ref[...] = inverse * (unit_grad - mean_one - unit * mean_two)
    gain_grad = jnp.sum(normed_grad * unit, axis=0, keepdims=True)
    offset_grad = jnp.sum(normed_grad, axis=0, keepdims=True)
    both = jnp.concatenate([lg_high, rg_high, lg_low, rg_low], axis=1)
    weights = dot(both, normed, TN)
    weights = weights[: 2 * C] + weights[2 * C :]
    weights = jnp.concatenate([weights[:, :Z], weights[:, Z:]], axis=0)
    biases = jnp.sum(jnp.concatenate([left_grad, right_grad], axis=1), axis=0, keepdims=True)
    biases = jnp.concatenate([biases, jnp.zeros((1, Z - 2 * C), F32)], axis=1)
    halves = (gain_grad[:, :Z], gain_grad[:, Z:], offset_grad[:, :Z], offset_grad[:, Z:])
    rest = jnp.concatenate(halves + (biases, bias_grad_ref[...], jnp.zeros((2, Z), F32)), axis=0)
    tiles = weights.reshape(16, 1, 8, Z)
    small = jnp.concatenate([tiles, tiles], axis=1).reshape(32, 8, Z)
    block, row = iota(small.shape, 0), iota(small.shape, 1)
    rest = jnp.concatenate([rest[4:], rest[:4]], axis=0)[None]
    small = jnp.where(block % 2 == row // 4, small, jnp.where(block < 2, rest, 0.0))
    load.wait()
    pack_ref[...] = packed(w_ref[...].astype(F32), small)


def packed(w_rows, small):
    high = small.astype(BF16).astype(F32)
    return jnp.concatenate([w_rows, high, small - high], axis=1).astype(BF16)


def sum_kernel(in_ref, out_ref):
    total = jnp.sum(in_ref[...].astype(F32), axis=0)
    out_ref[...] = jnp.concatenate([total[:32], total[32:40] + total[40:]], axis=0)


def spread_kernel(a_ref, b_ref, c_ref, d_ref, out_ref):
    total = a_ref[...] + b_ref[...] + (c_ref[...] + d_ref[...])
    out_ref[...] = jnp.broadcast_to(packed(total[None, :32], total[None, 32:]), (32, 48, Z))


def last_kernel(
    in_ref, gain_ref, offset_ref, lw_ref, lb_ref, rw_ref, rb_ref, w_ref, wb_ref, w_scratch
):
    blocks = in_ref[...].astype(F32)
    w_scratch[...] = blocks[:, :32].reshape(C * C, Z)
    for c in range(C):
        w_ref[c * C : (c + 1) * C, :] = w_scratch[pl.ds(c, C, stride=C), :]
    small = blocks[:, 32:40] + blocks[:, 40:]
    pairs = small.reshape(16, 2, 8, Z)
    weights = jnp.where(iota((16, 8, Z), 1) < 4, pairs[:, 0], pairs[:, 1]).reshape(Z, Z)
    first, second = small[0], small[1]
    lw_ref[:, :Z] = weights[:C]
    lw_ref[:, Z:] = weights[2 * C : 3 * C]
    rw_ref[:, :Z] = weights[C : 2 * C]
    rw_ref[:, Z:] = weights[3 * C :]
    gain_ref[:, :Z] = first[4:5]
    gain_ref[:, Z:] = first[5:6]
    offset_ref[:, :Z] = first[6:7]
    offset_ref[:, Z:] = first[7:8]
    lb_ref[...] = second[0:1, :C]
    rb_ref[...] = second[0:1, C : 2 * C]
    wb_ref[...] = second[1:2] * ROOT


def shape(dims, dtype):
    return jax.ShapeDtypeStruct(dims, dtype)


HBM = pl.BlockSpec(memory_space=pltpu.HBM)
VMEM = pl.BlockSpec(memory_space=pltpu.VMEM)


def in_hbm(array):
    return pltpu.with_memory_space_constraint(array, pltpu.HBM)


def in_vmem(*arrays):
    return [pltpu.with_memory_space_constraint(v, pltpu.VMEM) for v in arrays]


def shifted(array, step):
    return lax.ppermute(array, "x", [(n, (n + step) % NX) for n in range(NX)])


def call(body, name, mib, out_shape, scratch=(), **more):
    params = pltpu.CompilerParams(vmem_limit_bytes=mib * MIB)
    return pl.pallas_call(
        body, out_shape=out_shape, scratch_shapes=list(scratch), compiler_params=params, name=name, **more
    )


def exchange(array):
    return lax.all_to_all(array, ("z", "y"), 0, 0, tiled=True)


def blocking_exchange(array):
    return lax.cond(lax.axis_index("x") < NX, exchange, jnp.zeros_like, array)


def per_device(x, gain, shift, k1, b1, k2, b2, w, bias, g):
    gain, shift, b1, b2, bias = [v.reshape(1, -1) for v in (gain, shift, b1, b2, bias)]
    x, k1, k2 = x.reshape(S * I, H), k1.T, k2.T
    inputs = (x, gain, shift, k1, b1, k2, b2, w, g)
    made = (
        ((I * S, C), BF16),
        ((Q, C * S), BF16),
        ((C, C * Z), BF16),
        ((C * S, I * Z), BF16),
    )
    left, copies, wd, t, p0, p1, p2, p3 = call(
        first_kernel,
        "first",
        16,
        tuple(pltpu.HBM(*v) for v in made) + (pltpu.VMEM((Q, C * S), BF16),) * NX,
        [pltpu.VMEM(v.shape, v.dtype) for v in inputs]
        + [pltpu.VMEM(*v) for v in made]
        + [pltpu.VMEM((C * C, Z), F32), pltpu.SemaphoreType.DMA((len(inputs),))]
        + [pltpu.SemaphoreType.DMA((len(made),))],
        in_specs=[HBM] * len(inputs),
        out_specs=[HBM] * len(made) + [VMEM] * NX,
    )(*[in_hbm(v) for v in inputs])
    arrived = [shifted(p, k) for k, p in ((1, p1), (3, p3), (2, p2))]
    r0 = blocking_exchange(copies)
    r1, r3, r2 = [shifted(r0, k) for k in (1, 3, 2)]
    quarter = ((Q, C * S), BF16)
    own = call(fold_kernel, "fold", 8, shape(*quarter))(*in_vmem(p0, *arrived))
    pieces = exchange(own)
    r0, r1, r2, r3 = [in_hbm(v) for v in (r0, r1, r2, r3)]
    left_grad, w_part, bias_grad = call(
        second_kernel,
        "second",
        16,
        (shape((I * S, C), F32), pltpu.HBM((C, C, Z), BF16), shape((1, Z), F32)),
        [pltpu.VMEM(*quarter)] * NX
        + [pltpu.VMEM(g.shape, BF16), pltpu.VMEM(wd.shape, BF16)]
        + [pltpu.VMEM((C * S, J), BF16), pltpu.VMEM((I * S, C * Z), BF16), pltpu.SemaphoreType.DMA((6,))],
        in_specs=[HBM] * (NX + 2) + [VMEM],
        cost_estimate=pl.CostEstimate(flops=100_000_000_000, bytes_accessed=0, transcendentals=0),
    )(r0, r1, r2, r3, in_hbm(g), in_hbm(wd), left)
    align, pack = call(
        third_kernel,
        "third",
        12,
        (shape((S * I, H), F32), shape((32, 48, Z), BF16)),
        [pltpu.VMEM((C, C, Z), BF16), pltpu.SemaphoreType.DMA],
        in_specs=[VMEM, HBM] + [VMEM] * 7,
    )(left_grad, in_hbm(w_part), bias_grad, x, gain, shift, k1, k2, pieces)
    parts = exchange(pack)
    update = call(
        update_kernel,
        "update",
        12,
        pltpu.HBM((I, J, Z), BF16),
        [pltpu.VMEM(*quarter)] * NX
        + [pltpu.VMEM(t.shape, BF16), pltpu.VMEM((NX, I, Q, Z), BF16)]
        + [pltpu.SemaphoreType.DMA((5,)), pltpu.SemaphoreType.DMA((NX,))],
        in_specs=[HBM] * (NX + 1) + [VMEM],
        out_specs=HBM,
    )(r0, r1, r2, r3, in_hbm(t), bias)
    mine = call(sum_kernel, "sum", 8, shape((40, Z), F32))(parts)
    others = [shifted(mine, k) for k in (1, 3, 2)]
    block = call(spread_kernel, "spread", 8, shape((32, 48, Z), BF16))(mine, *others)
    sums = exchange(block)
    gain_g, offset_g, lw, lb, rw, rb, w_g, wb = call(
        last_kernel,
        "last",
        8,
        (
            shape((1, H), F32),
            shape((1, H), F32),
            shape((C, H), F32),
            shape((1, C), F32),
            shape((C, H), F32),
            shape((1, C), F32),
            shape((C * C, Z), F32),
            shape((1, Z), F32),
        ),
        [pltpu.VMEM((C * C, Z), F32)],
    )(sums)
    return (
        update,
        align.reshape(S, I, H),
        gain_g.reshape(H),
        offset_g.reshape(H),
        lw.T,
        lb.reshape(C),
        rw.T,
        rb.reshape(C),
        w_g,
        wb.reshape(Z),
    )


def solution(mesh):
    grid = Mesh(mesh.devices.reshape(NX, NZ, NY, 2), ("x", "z", "y", "dp"))
    dap = ("x", "z", "y")
    in_specs = (P("dp", dap, None),) + (P(),) * 8 + (P(("dp",) + dap, None, None),)
    out_specs = (
        P(("dp",) + dap, None, None),
        P("dp", dap, None),
        P("dp"),
        P("dp"),
        P("dp", None),
        P("dp"),
        P("dp", None),
        P("dp"),
        P("dp", None),
        P("dp"),
    )
    return jax.shard_map(
        per_device, mesh=grid, in_specs=in_specs, out_specs=out_specs, check_vma=False
    )
```

time: 160 us -> 123 us (0.77)
  waiting for transfers between devices: 43.8 us -> 23.6 us
  local copies, waits for them, and re-layouts: 9.42 us -> 0.03 us
  blocking collectives: 55.7 us -> 48.2 us
  Pallas kernels: 18.3 us -> 23.7 us
  starting transfers between devices: 30.1 us -> 25.8 us
    ppermute x6 -> x9, waiting for transfers between devices: 43.8 us -> 17.2 us  [shifted(): return lax.ppermute(array, 'x', [(n, (n + step) % NX) for n in range(NX)])]
    all_to_all x2, starting transfers between devices: 21.5 us -> 11.1 us  [exchange(): return lax.all_to_all(array, ('z', 'y'), 0, 0, tiled=True)]
    unnamed x32 -> x14, local copies, waits for them, and re-layouts: 8.55 us -> 0.03 us
    all_to_all x2, blocking collectives: 55.7 us -> 48.2 us  [exchange(): return lax.all_to_all(array, ('z', 'y'), 0, 0, tiled=True)]
    all_to_all x2, waiting for transfers between devices: 0.01 us -> 6.42 us  [exchange(): return lax.all_to_all(array, ('z', 'y'), 0, 0, tiled=True)]
    ppermute x6 -> x9, starting transfers between devices: 8.62 us -> 14.7 us  [shifted(): return lax.ppermute(array, 'x', [(n, (n + step) % NX) for n in range(NX)])]
    pallas_call x4 -> x8, Pallas kernels: 18.3 us -> 23.7 us  [the longest x1 6.37 us: per_device(): call(second_kernel, 'second', 16, (shape((I * S, C), F32), pltpu.HBM((C,...]
  transfers between devices with their start and end apart: 8 -> 11, of which waited for: 6 -> 6; matrix products, arithmetic and copies ran while one was open for 1% -> 0% of each run, Pallas kernels for 0% -> 10%
where the time goes in v2:
time: 123 us; the launch traced here: 122 us
  blocking collectives  48.2 us (39%)
  starting transfers between devices  25.8 us (21%)
  Pallas kernels  23.7 us (19%)
  waiting for transfers between devices  23.6 us (19%)
    all_to_all x2, blocking collectives, exchange(): return lax.all_to_all(array, ('z', 'y'), 0, 0, tiled=True)  48.2 us
    ppermute x9, waiting for transfers between devices, shifted(): return lax.ppermute(array, 'x', [(n, (n + step) % NX) for n in range(NX)])  17.2 us
    ppermute x9, starting transfers between devices, shifted(): return lax.ppermute(array, 'x', [(n, (n + step) % NX) for n in range(NX)])  14.7 us
    all_to_all x2, starting transfers between devices, exchange(): return lax.all_to_all(array, ('z', 'y'), 0, 0, tiled=True)  11.1 us
    all_to_all x2, waiting for transfers between devices, exchange(): return lax.all_to_all(array, ('z', 'y'), 0, 0, tiled=True)  6.42 us
    pallas_call x1, Pallas kernels, per_device(): call(second_kernel, 'second', 16, (shape((I * S, C), F32), pltpu.HBM((C,...  6.37 us
    pallas_call x1, Pallas kernels, per_device(): call(first_kernel, 'first', 16, tuple((pltpu.HBM(*v) for v in made)) + (p...  5.92 us
    pallas_call x1, Pallas kernels, per_device(): call(update_kernel, 'update', 12, pltpu.HBM((I, J, Z), BF16), [pltpu.VMEM...  5.4 us
  transfers between devices with their start and end apart: 11, of which 6 were waited for; matrix products, arithmetic and copies ran while one was open for 0% of the time, Pallas kernels for 10%

profile of v2, /device:TPU:8, one launch (start us, length us, event | category | flops | bytes accessed | tf_op | source)
XLA Modules:
  0.0 122.2 jit_solution(11143285859488599703)
XLA Ops:
  0.6 5.9 %first.1 = (bf16[256,32]{1,0:T(8,128)(2,1)}, bf16[256,1024]{1,0:T(8,128)(2,1)}, bf16[32,4096]{1,0:T(8,128)(2,1)}, bf16[1024,1024]{1,0:T(8,128)(2,1)}, bf16[256,1...) custom-call(bf16[256,256]{1,0:T(8,128)(2,1)} %bitcast.21, ...), custom_call_target="tpu_custom_call" | custom-call | tf_op jit(solution)/shard_map/first/pallas_call | solution.py:325
  6.6 1.6 %collective-permute-start.3 = (bf16[256,1024]{1,0:T(8,128)(2,1)}, bf16[256,1024]{1,0:T(8,128)(2,1)S(1)}, u32[]{:S(2)}, u32[]{:S(2)}) collective-permute-start(bf16[256,1024]{1,0:T(8,128)(2,1)} %get-tuple-element.43), channel_id=1, source_target_pairs={{0,64},{64,128},{128,192},{192,0},{1,65},{65,129},{129,193},{193,1... | collective-permute-start | bytes 1572872 | tf_op jit(solution)/shard_map/ppermute | solution.py:297
  8.1 1.7 %collective-permute-start.4 = (bf16[256,1024]{1,0:T(8,128)(2,1)S(1)}, bf16[256,1024]{1,0:T(8,128)(2,1)S(1)}, u32[]{:S(2)}, u32[]{:S(2)}) collective-permute-start(bf16[256,1024]{1,0:T(8,128)(2,1)S(1)} %get-tuple-element.44), channel_id=1, source_target_pairs={{0,192},{64,0},{128,64},{192,128},{1,193},{65,1},{129,65},{193,129... | collective-permute-start | bytes 1572872 | tf_op jit(solution)/shard_map/ppermute | solution.py:297
  9.9 1.8 %collective-permute-start.5 = (bf16[256,1024]{1,0:T(8,128)(2,1)S(1)}, bf16[256,1024]{1,0:T(8,128)(2,1)S(1)}, u32[]{:S(2)}, u32[]{:S(2)}) collective-permute-start(bf16[256,1024]{1,0:T(8,128)(2,1)S(1)} %get-tuple-element.45), channel_id=1, source_target_pairs={{0,128},{64,192},{128,0},{192,64},{1,129},{65,193},{129,1},{193,65... | collective-permute-start | bytes 1572872 | tf_op jit(solution)/shard_map/ppermute | solution.py:297
  11.7 27.8 %conditional.1 = (bf16[256,1024]{1,0:T(8,128)(2,1)}) conditional(s32[]{:T(128)} %convert_element_type.3, () %tuple.14, bf16[256,1024]{1,0:T(8,128)(2,1)} %get-tuple-element.35), branch_computations={%region_0.0_spmd, %region_1.0_spmd} | conditional | bytes 1048584 | solution.py:312
  11.7 27.8 %all_to_all.30 = bf16[32,8,1024]{2,1,0:T(8,128)(2,1)} all-to-all(bf16[32,8,1024]{2,1,0:T(8,128)(2,1)} %bitcast.33), channel_id=1, replica_groups=mesh['x'=4,'z'=8,'y'=4,'dp'=2] {'z','y'}, dimensions={0} | all-to-all | bytes 1048576 | tf_op jit(solution)/shard_map/cond/branch_1_fun/all_to_all | solution.py:308
  39.5 0.0 copy-start.6
  39.5 0.6 collective-permute-start
  40.1 2.0 %collective-permute-start.1 = (bf16[256,1024]{1,0:T(8,128)(2,1)}, bf16[256,1024]{1,0:T(8,128)(2,1)}, u32[]{:S(2)}, u32[]{:S(2)}) collective-permute-start(bf16[256,1024]{1,0:T(8,128)(2,1)} %get-tuple-element.56.refs_0_.r0_any), channel_id=1, source_target_pairs={{0,128},{64,192},{128,0},{192,64},{1,129},{65,193},{129,1},{193,65... | collective-permute-start | bytes 1572872 | tf_op jit(solution)/shard_map/ppermute | solution.py:297
  42.1 0.0 collective-permute-done.3.b_ref
  42.1 1.7 %collective-permute-start.2 = (bf16[256,1024]{1,0:T(8,128)(2,1)}, bf16[256,1024]{1,0:T(8,128)(2,1)}, u32[]{:S(2)}, u32[]{:S(2)}) collective-permute-start(bf16[256,1024]{1,0:T(8,128)(2,1)} %get-tuple-element.56.refs_0_.r0_any), channel_id=1, source_target_pairs={{0,192},{64,0},{128,64},{192,128},{1,193},{65,1},{129,65},{193,129... | collective-permute-start | bytes 1572872 | tf_op jit(solution)/shard_map/ppermute | solution.py:297
  43.8 0.0 collective-permute-done.4.c_ref
  43.8 0.0 collective-permute-done.5.d_ref
  43.8 1.1 fold.1
  44.9 5.6 %all-to-all-start.1 = ((bf16[32,8,1024]{2,1,0:T(8,128)(2,1)}), bf16[32,8,1024]{2,1,0:T(8,128)(2,1)S(1)}, u32[]{:S(2)}, u32[]{:S(2)}) async-start(bf16[32,8,1024]{2,1,0:T(8,128)(2,1)} %bitcast.10), calls=%async_computation.1 | async-start | bytes 1048576 | tf_op jit(solution)/shard_map/all_to_all | solution.py:308
  50.5 12.6 %collective-permute-done.refs_1_.r1_any = bf16[256,1024]{1,0:T(8,128)(2,1)} collective-permute-done((bf16[256,1024]{1,0:T(8,128)(2,1)}, bf16[256,1024]{1,0:T(8,128)(2,1)}, u32[]{:S(2)}, u32[]{:S(2)}) %collective-permute-start) | collective-permute-done | bytes 524320 | tf_op jit(solution)/shard_map/ppermute | solution.py:297
  63.1 0.0 collective-permute-done.1.refs_2_.r2_any
  63.1 0.6 collective-permute-done.2.refs_3_.r3_any
  63.7 0.0 copy-done.6
  63.7 0.0 copy-start
  63.7 0.0 copy-start.1
  63.7 0.0 copy-start.2
  63.7 0.0 copy-start.3
  63.8 0.0 copy-start.4
  63.8 6.4 %second.1 = (f32[256,32]{1,0:T(8,128)S(1)}, bf16[32,32,128]{2,1,0:T(8,128)(2,1)}, f32[1,128]{1,0:T(1,128)S(1)}) custom-call(bf16[256,1024]{1,0:T(8,128)(2,1)} %get-tuple-element.56.refs_0_.r0_any, bf16[256,1024]{1,0:T(8,128)(2,1)} %collective-permute-done.refs_1_.r1_any, bf16[256,1024]{1,0:T(8,128)(2,1)} %collective-permute-done.1.refs_2_.r2_any, ...), custom_call_target="tpu_custom_call" | custom-call | flops 99999997952 | tf_op jit(solution)/shard_map/second/pallas_call | solution.py:344
  70.2 0.0 copy-start.5
  70.2 0.0 all-to-all-done.1
  70.2 0.0 copy-done
  70.2 0.0 copy-done.1
  70.2 0.0 copy-done.2
  70.2 0.0 copy-done.3
  70.2 0.0 copy-done.4
  70.2 3.0 %third.1 = (f32[256,256]{1,0:T(8,128)}, bf16[32,48,128]{2,1,0:T(8,128)(2,1)S(1)}) custom-call(f32[256,32]{1,0:T(8,128)S(1)} %get-tuple-element.39.left_grad_ref, bf16[32,32,128]{2,1,0:T(8,128)(2,1)} %get-tuple-element.40.w_hbm, f32[1,128]{1,0:T(1,128)S(1)} %get-tuple-element.41.bias_grad_ref, bf16[256,256]{1,0:T(8,128)(2,1)S(1)} %bitcast.22, ...), custom_call_target="tpu_custom_call" | custom-call | tf_op jit(solution)/shard_map/third/pallas_call | solution.py:355
  73.2 20.4 %all_to_all.31.in_ref = bf16[32,48,128]{2,1,0:T(8,128)(2,1)S(1)} all-to-all(bf16[32,48,128]{2,1,0:T(8,128)(2,1)S(1)} %get-tuple-element.47), channel_id=1, replica_groups=mesh['x'=4,'z'=8,'y'=4,'dp'=2] {'z','y'}, dimensions={0} | all-to-all | bytes 786432 | tf_op jit(solution)/shard_map/all_to_all | solution.py:308
  93.6 0.1 sum.1.a_ref
  93.6 2.2 %collective-permute-start.6 = (f32[40,128]{1,0:T(8,128)S(1)}, f32[40,128]{1,0:T(8,128)S(1)}, u32[]{:S(2)}, u32[]{:S(2)}) collective-permute-start(f32[40,128]{1,0:T(8,128)S(1)} %sum.1.a_ref), channel_id=1, source_target_pairs={{0,64},{64,128},{128,192},{192,0},{1,65},{65,129},{129,193},{193,1... | collective-permute-start | bytes 61448 | tf_op jit(solution)/shard_map/ppermute | solution.py:297
  95.8 1.7 %collective-permute-start.7 = (f32[40,128]{1,0:T(8,128)S(1)}, f32[40,128]{1,0:T(8,128)S(1)}, u32[]{:S(2)}, u32[]{:S(2)}) collective-permute-start(f32[40,128]{1,0:T(8,128)S(1)} %sum.1.a_ref), channel_id=1, source_target_pairs={{0,192},{64,0},{128,64},{192,128},{1,193},{65,1},{129,65},{193,129... | collective-permute-start | bytes 61448 | tf_op jit(solution)/shard_map/ppermute | solution.py:297
  97.5 1.4 %collective-permute-start.8 = (f32[40,128]{1,0:T(8,128)S(1)}, f32[40,128]{1,0:T(8,128)S(1)}, u32[]{:S(2)}, u32[]{:S(2)}) collective-permute-start(f32[40,128]{1,0:T(8,128)S(1)} %sum.1.a_ref), channel_id=1, source_target_pairs={{0,128},{64,192},{128,0},{192,64},{1,129},{65,193},{129,1},{193,65... | collective-permute-start | bytes 61448 | tf_op jit(solution)/shard_map/ppermute | solution.py:297
  98.9 0.3 collective-permute-done.6.b_ref
  99.2 0.5 collective-permute-done.7.c_ref
  99.6 3.2 %collective-permute-done.8.d_ref = f32[40,128]{1,0:T(8,128)S(1)} collective-permute-done((f32[40,128]{1,0:T(8,128)S(1)}, f32[40,128]{1,0:T(8,128)S(1)}, u32[]{:S(2)}, u32[]{:S(2)}) %collective-permute-start.8) | collective-permute-done | bytes 20512 | tf_op jit(solution)/shard_map/ppermute | solution.py:297
  102.8 0.8 spread.1
  103.5 5.6 %all-to-all-start.3 = ((bf16[32,48,128]{2,1,0:T(8,128)(2,1)}), bf16[32,48,128]{2,1,0:T(8,128)(2,1)S(1)}, u32[]{:S(2)}, u32[]{:S(2)}) async-start(bf16[32,48,128]{2,1,0:T(8,128)(2,1)} %spread.1), calls=%async_computation.3 | async-start | bytes 786432 | tf_op jit(solution)/shard_map/all_to_all | solution.py:308
  109.1 0.0 copy-done.5
  109.1 5.4 %update.1 = bf16[8,1024,128]{2,1,0:T(8,128)(2,1)} custom-call(bf16[256,1024]{1,0:T(8,128)(2,1)} %get-tuple-element.56.refs_0_.r0_any, bf16[256,1024]{1,0:T(8,128)(2,1)} %collective-permute-done.refs_1_.r1_any, bf16[256,1024]{1,0:T(8,128)(2,1)} %collective-permute-done.1.refs_2_.r2_any, bf16[256,1024]{1,0:T(8,128)(2,1)} %collective-permute-done.2.refs_3_.r3_any, ...), custom_call_target="tpu_custom_call" | custom-call | tf_op jit(solution)/shard_map/update/pallas_call | solution.py:364
  114.5 6.4 %all-to-all-done.3.in_ref = bf16[32,48,128]{2,1,0:T(8,128)(2,1)S(1)} async-done(((bf16[32,48,128]{2,1,0:T(8,128)(2,1)}), bf16[32,48,128]{2,1,0:T(8,128)(2,1)S(1)}, u32[]{:S(2)}, u32[]{:S(2)}) %all-to-all-start.3) | async-done | bytes 393248 | tf_op jit(solution)/shard_map/all_to_all | solution.py:308
  121.0 1.2 last.1
Async XLA Ops:
  6.6 35.5 %collective-permute-start.3 = (bf16[256,1024]{1,0:T(8,128)(2,1)}, bf16[256,1024]{1,0:T(8,128)(2,1)S(1)}, u32[]{:S(2)}, u32[]{:S(2)}) collective-permute-start(bf16[256,1024]{1,0:T(8,128)(2,1)} %get-tuple-element.43), channel_id=1, source_target_pairs={{0,64},{64,128},{128,192},{192,0},{1,65},{65,129},{129,193},{193,1... | collective-permute-start | bytes 1572872 | tf_op jit(solution)/shard_map/ppermute | solution.py:297
  8.1 35.7 %collective-permute-start.4 = (bf16[256,1024]{1,0:T(8,128)(2,1)S(1)}, bf16[256,1024]{1,0:T(8,128)(2,1)S(1)}, u32[]{:S(2)}, u32[]{:S(2)}) collective-permute-start(bf16[256,1024]{1,0:T(8,128)(2,1)S(1)} %get-tuple-element.44), channel_id=1, source_target_pairs={{0,192},{64,0},{128,64},{192,128},{1,193},{65,1},{129,65},{193,129... | collective-permute-start | bytes 1572872 | tf_op jit(solution)/shard_map/ppermute | solution.py:297
  9.9 34.0 %collective-permute-start.5 = (bf16[256,1024]{1,0:T(8,128)(2,1)S(1)}, bf16[256,1024]{1,0:T(8,128)(2,1)S(1)}, u32[]{:S(2)}, u32[]{:S(2)}) collective-permute-start(bf16[256,1024]{1,0:T(8,128)(2,1)S(1)} %get-tuple-element.45), channel_id=1, source_target_pairs={{0,128},{64,192},{128,0},{192,64},{1,129},{65,193},{129,1},{193,65... | collective-permute-start | bytes 1572872 | tf_op jit(solution)/shard_map/ppermute | solution.py:297
  39.5 24.2 %copy-start.6 = (bf16[256,32]{1,0:T(8,128)(2,1)S(1)}, bf16[256,32]{1,0:T(8,128)(2,1)}, u32[]{:S(2)}) copy-start(bf16[256,32]{1,0:T(8,128)(2,1)} %get-tuple-element.38.left_ref) | copy-start | bytes 49156
  39.5 23.6 %collective-permute-start = (bf16[256,1024]{1,0:T(8,128)(2,1)}, bf16[256,1024]{1,0:T(8,128)(2,1)}, u32[]{:S(2)}, u32[]{:S(2)}) collective-permute-start(bf16[256,1024]{1,0:T(8,128)(2,1)} %get-tuple-element.56.refs_0_.r0_any), channel_id=1, source_target_pairs={{0,64},{64,128},{128,192},{192,0},{1,65},{65,129},{129,193},{193,1... | collective-permute-start | bytes 1572872 | tf_op jit(solution)/shard_map/ppermute | solution.py:297
  40.1 23.0 %collective-permute-start.1 = (bf16[256,1024]{1,0:T(8,128)(2,1)}, bf16[256,1024]{1,0:T(8,128)(2,1)}, u32[]{:S(2)}, u32[]{:S(2)}) collective-permute-start(bf16[256,1024]{1,0:T(8,128)(2,1)} %get-tuple-element.56.refs_0_.r0_any), channel_id=1, source_target_pairs={{0,128},{64,192},{128,0},{192,64},{1,129},{65,193},{129,1},{193,65... | collective-permute-start | bytes 1572872 | tf_op jit(solution)/shard_map/ppermute | solution.py:297
  42.1 21.6 %collective-permute-start.2 = (bf16[256,1024]{1,0:T(8,128)(2,1)}, bf16[256,1024]{1,0:T(8,128)(2,1)}, u32[]{:S(2)}, u32[]{:S(2)}) collective-permute-start(bf16[256,1024]{1,0:T(8,128)(2,1)} %get-tuple-element.56.refs_0_.r0_any), channel_id=1, source_target_pairs={{0,192},{64,0},{128,64},{192,128},{1,193},{65,1},{129,65},{193,129... | collective-permute-start | bytes 1572872 | tf_op jit(solution)/shard_map/ppermute | solution.py:297
  44.9 25.3 %all-to-all-start.1 = ((bf16[32,8,1024]{2,1,0:T(8,128)(2,1)}), bf16[32,8,1024]{2,1,0:T(8,128)(2,1)S(1)}, u32[]{:S(2)}, u32[]{:S(2)}) async-start(bf16[32,8,1024]{2,1,0:T(8,128)(2,1)} %bitcast.10), calls=%async_computation.1 | async-start | bytes 1048576 | tf_op jit(solution)/shard_map/all_to_all | solution.py:308
  63.7 6.4 %copy-start = (bf16[32,8,256]{2,1,0:T(8,128)(2,1)S(1)}, bf16[32,8,256]{2,1,0:T(8,128)(2,1)}, u32[]{:S(2)}) copy-start(bf16[32,8,256]{2,1,0:T(8,128)(2,1)} %param.12) | copy-start | bytes 393220
  63.7 6.4 %copy-start.1 = (bf16[256,32]{0,1:T(8,128)(2,1)S(1)}, bf16[256,32]{0,1:T(8,128)(2,1)}, u32[]{:S(2)}) copy-start(bf16[256,32]{0,1:T(8,128)(2,1)} %param.15) | copy-start | bytes 49156
  63.7 6.5 %copy-start.2 = (bf16[256,32]{0,1:T(8,128)(2,1)S(1)}, bf16[256,32]{0,1:T(8,128)(2,1)}, u32[]{:S(2)}) copy-start(bf16[256,32]{0,1:T(8,128)(2,1)} %param.17) | copy-start | bytes 49156
  63.7 6.5 %copy-start.3 = (f32[256]{0:T(256)S(1)}, f32[256]{0:T(256)}, u32[]{:S(2)}) copy-start(f32[256]{0:T(256)} %param.13) | copy-start | bytes 3076
  63.8 6.5 %copy-start.4 = (f32[256]{0:T(256)S(1)}, f32[256]{0:T(256)}, u32[]{:S(2)}) copy-start(f32[256]{0:T(256)} %param.14) | copy-start | bytes 3076
  70.2 39.0 %copy-start.5 = (f32[128]{0:T(128)S(1)}, f32[128]{0:T(128)}, u32[]{:S(2)}) copy-start(f32[128]{0:T(128)} %param.20) | copy-start | bytes 1540
  93.6 5.5 %collective-permute-start.6 = (f32[40,128]{1,0:T(8,128)S(1)}, f32[40,128]{1,0:T(8,128)S(1)}, u32[]{:S(2)}, u32[]{:S(2)}) collective-permute-start(f32[40,128]{1,0:T(8,128)S(1)} %sum.1.a_ref), channel_id=1, source_target_pairs={{0,64},{64,128},{128,192},{192,0},{1,65},{65,129},{129,193},{193,1... | collective-permute-start | bytes 61448 | tf_op jit(solution)/shard_map/ppermute | solution.py:297
  95.8 3.8 %collective-permute-start.7 = (f32[40,128]{1,0:T(8,128)S(1)}, f32[40,128]{1,0:T(8,128)S(1)}, u32[]{:S(2)}, u32[]{:S(2)}) collective-permute-start(f32[40,128]{1,0:T(8,128)S(1)} %sum.1.a_ref), channel_id=1, source_target_pairs={{0,192},{64,0},{128,64},{192,128},{1,193},{65,1},{129,65},{193,129... | collective-permute-start | bytes 61448 | tf_op jit(solution)/shard_map/ppermute | solution.py:297
  97.5 5.3 %collective-permute-start.8 = (f32[40,128]{1,0:T(8,128)S(1)}, f32[40,128]{1,0:T(8,128)S(1)}, u32[]{:S(2)}, u32[]{:S(2)}) collective-permute-start(f32[40,128]{1,0:T(8,128)S(1)} %sum.1.a_ref), channel_id=1, source_target_pairs={{0,128},{64,192},{128,0},{192,64},{1,129},{65,193},{129,1},{193,65... | collective-permute-start | bytes 61448 | tf_op jit(solution)/shard_map/ppermute | solution.py:297
  103.5 17.4 %all-to-all-start.3 = ((bf16[32,48,128]{2,1,0:T(8,128)(2,1)}), bf16[32,48,128]{2,1,0:T(8,128)(2,1)S(1)}, u32[]{:S(2)}, u32[]{:S(2)}) async-start(bf16[32,48,128]{2,1,0:T(8,128)(2,1)} %spread.1), calls=%async_computation.3 | async-start | bytes 786432 | tf_op jit(solution)/shard_map/all_to_all | solution.py:308

commit v3 on v2

v3 whole, which is shorter than its diff:
```python
import itertools
import math

import jax
import jax.numpy as jnp
from jax import lax
from jax.experimental import pallas as pl
from jax.experimental.pallas import tpu as pltpu
from jax.sharding import Mesh, PartitionSpec as P

EPSILON = 1e-05
F32 = jnp.float32
BF16 = jnp.bfloat16
S = 32
I = 8
C = 32
H = 256
Z = 128
J = 1024
NX, NZ, NY = 4, 8, 4
NP = NX * NY
WR = C * C // NP
G = NZ * I
Q = J // NX
SCALE = 1.0 / (math.sqrt(J) * S)
ROOT = 1.0 / math.sqrt(J)
NT = (((1,), (1,)), ((), ()))
TN = (((0,), (0,)), ((), ()))
MIB = 1024 * 1024


def dot(a, b, dims=(((1,), (0,)), ((), ()))):
    return lax.dot_general(a, b, dims, preferred_element_type=F32)


def iota(shape, dim):
    return lax.broadcasted_iota(jnp.int32, shape, dim)


def one_hot(condition):
    return jnp.where(condition, 1.0, 0.0).astype(BF16)


def to_residue_major():
    row, col = iota((I * S, I * S), 0), iota((I * S, I * S), 1)
    return one_hot((row // S == col % I) & (row % S == col // I))


def split(value):
    high = value.astype(BF16)
    return high, (value - high.astype(F32)).astype(BF16)


def layer_norm_parts(x_ref):
    features = x_ref[...].astype(F32)
    average = jnp.mean(features, axis=-1, keepdims=True)
    centred = features - average
    spread = jnp.mean(centred * centred, axis=-1, keepdims=True)
    inverse = lax.rsqrt(spread + EPSILON)
    return centred, inverse


def places():
    core, x, y = lax.axis_index("dp"), lax.axis_index("x"), lax.axis_index("y")
    across = Q - I
    return x + (y - x) * core, y + (x - y) * core, Q - across * core, I + across * core


def block_rows(k, n):
    own, _, long_stride, short_stride = places()
    start = (own + NX - k) % NX * long_stride + n // NY * (NY * I) + n % NY * short_stride
    return pl.ds(pl.multiple_of(start, I), I)


def rows_of(g_ref, k):
    return jnp.concatenate([g_ref[i, k * Q : (k + 1) * Q, :] for i in range(I)], axis=1)


def copies_between(sources, targets, sems):
    return [pltpu.make_async_copy(a, b, sems.at[n]) for n, (a, b) in enumerate(zip(sources, targets))]


def first_kernel(*refs):
    inputs, outputs, held, (made, w_scratch, g_scratch, in_sems, out_sems) = (
        refs[:9], refs[9:18], refs[18:27], (refs[27:32], *refs[32:])
    )
    x_ref, gain_ref, shift_ref, k1_ref, b1_ref, k2_ref, b2_ref, w_ref, g_ref = held
    left_ref, copies_ref, wd_ref, t_ref, ordered_ref = made
    partial_refs = outputs[5:]
    loads = copies_between(inputs, held, in_sems)
    stores = copies_between(made, outputs, out_sems)
    for load in loads:
        load.start()
    for load in loads[:7]:
        load.wait()
    centred, inverse = layer_norm_parts(x_ref)
    normed = (centred * inverse * gain_ref[...] + shift_ref[...]).astype(BF16)
    left = (dot(normed, k1_ref[...], NT) + b1_ref[...]).astype(BF16)
    right = (dot(normed, k2_ref[...], NT) + b2_ref[...]).astype(BF16)
    left = dot(to_residue_major(), left).astype(BF16)
    left_ref[...] = left
    stores[0].start()
    spread = dot(right, one_hot(iota((C, C * S), 0) == iota((C, C * S), 1) // S))
    keep = iota((S * I, C * S), 0) // I == iota((S * I, C * S), 1) % S
    kept = jnp.where(keep, spread, 0.0).astype(BF16)
    gather = one_hot(iota((G, S * I), 0) % I == iota((G, S * I), 1) % I)
    copies_ref[...] = dot(gather, kept).astype(BF16)
    stores[1].start()
    loads[7].wait()
    w_scratch[...] = w_ref[...].astype(F32)
    for d in range(C):
        wd_ref[:, d * Z : (d + 1) * Z] = w_scratch[pl.ds(d, C, stride=C), :].astype(BF16)
    stores[2].start()
    for d in range(0, C, 2):
        block = dot(left, wd_ref[:, d * Z : (d + 2) * Z]).astype(BF16)
        for e in range(2):
            for i in range(I):
                t_ref[(d + e) * S : (d + e + 1) * S, i * Z : (i + 1) * Z] = block[
                    i * S : (i + 1) * S, e * Z : (e + 1) * Z
                ]
    stores[3].start()
    loads[8].wait()
    g_scratch[...] = g_ref[...].astype(F32)
    for k in range(NX):
        for n in range(0, NZ * NY, 2):
            pair = [g_scratch[:, block_rows(k, m), :] for m in (n, n + 1)]
            start = k * Q + n * I
            ordered_ref[:, start : start + 2 * I, :] = jnp.concatenate(pair, axis=1).astype(BF16)
    stores[4].start()
    for k in range(NX):
        rows = rows_of(ordered_ref, (NX - k) % NX)
        partial_refs[k][...] = (dot(rows, t_ref[...], NT) * SCALE).astype(BF16)
    for store in stores:
        store.wait()


def added(refs, rows):
    a, b, c, d = [ref[rows, :].astype(F32) for ref in refs]
    return (a + b) + (c + d)


def fold_kernel(*refs):
    inputs, outputs, total = refs[:4], refs[4:8], refs[8]
    line = places()[1]
    for n in range(0, Q, 16):
        rows = pl.ds(n, 16)
        total[rows, :] = added(inputs, rows)
    for k, out in enumerate(outputs):
        first = (line + k) % NY * I
        for z in range(0, NZ, 2):
            pair = [total[pl.ds(pl.multiple_of(n * NY * I + first, I), I), :] for n in (z, z + 1)]
            out[z * I : (z + 2) * I, :] = jnp.concatenate(pair, axis=0).astype(BF16)


def add_kernel(*refs):
    for n in range(0, G, 16):
        rows = pl.ds(n, 16)
        refs[4][rows, :] = added(refs[:4], rows)


def arrange_kernel(*refs):
    inputs, out_ref, total = refs[:4], refs[5], refs[6]
    line = places()[1]
    for k, ref in enumerate(inputs):
        first = (line + NY - k) % NY * I
        for z in range(0, NZ, 2):
            rows = ref[z * I : (z + 2) * I, :].astype(F32)
            for e in range(2):
                start = pl.multiple_of((z + e) * NY * I + first, I)
                total[pl.ds(start, I), :] = rows[e * I : (e + 1) * I]
    for n in range(0, Q, 16):
        out_ref[pl.ds(n, 16), :] = total[pl.ds(n, 16), :].astype(BF16)


def update_kernel(
    r0_ref, r1_ref, r2_ref, r3_ref, t_hbm, bias_ref, update_hbm, t_ref, update_ref, scratch, sem, sems
):
    load = pltpu.make_async_copy(t_hbm, t_ref, sem)
    load.start()
    load.wait()
    bias = jnp.concatenate([bias_ref[...]] * I, axis=1)
    for k, right in enumerate((r0_ref, r1_ref, r2_ref, r3_ref)):
        block = dot(right[...], t_ref[...]) * (1.0 / S) + bias
        for n in range(NZ * NY):
            scratch[block_rows(k, n), :] = block[n * I : (n + 1) * I]
    stores = []
    for k in range(NX):
        rows = pl.ds(k * Q, Q)
        for i in range(I):
            update_ref[i, rows, :] = scratch[rows, i * Z : (i + 1) * Z].astype(BF16)
        stores.append(pltpu.make_async_copy(update_ref.at[:, rows, :], update_hbm.at[:, rows, :], sems.at[k]))
        stores[-1].start()
    for store in stores:
        store.wait()


def second_kernel(
    r0_ref, r1_ref, r2_ref, r3_ref, g_hbm, wd_hbm, left_ref,
    left_grad_ref, w_part_ref, bias_grad_ref,
    g_ref, wd_ref, rt_scratch, m_scratch, sems,
):
    loads = copies_between((g_hbm, wd_hbm), (g_ref, wd_ref), sems)
    for load in loads:
        load.start()
    for k, right in enumerate((r0_ref, r1_ref, r2_ref, r3_ref)):
        rt_scratch[:, k * Q : (k + 1) * Q] = right[...].T
    loads[0].wait()
    bias_grad = jnp.zeros((1, Z), F32)
    for i in range(0, I, 2):
        pair = []
        for n in (i, i + 1):
            pair.append(g_ref[n])
            bias_grad = bias_grad + jnp.sum(pair[-1].astype(F32), axis=0, keepdims=True)
        u = dot(rt_scratch[...], jnp.concatenate(pair, axis=1)).astype(BF16)
        for e in range(2):
            for d in range(C):
                m_scratch[(i + e) * S : (i + e + 1) * S, d * Z : (d + 1) * Z] = u[
                    d * S : (d + 1) * S, e * Z : (e + 1) * Z
                ]
    bias_grad_ref[...] = bias_grad
    loads[1].wait()
    left_grad_ref[...] = dot(m_scratch[...], wd_ref[...], NT) * SCALE
    w_part = dot(left_ref[...], m_scratch[...], TN) * SCALE
    for d in range(C):
        w_part_ref[d] = w_part[:, d * Z : (d + 1) * Z].astype(BF16)


def third_kernel(
    left_grad_ref, w_hbm, bias_grad_ref, x_ref, gain_ref, shift_ref, k1_ref, k2_ref, pieces_ref,
    align_ref, pack_ref, w_ref, sem,
):
    load = pltpu.make_async_copy(w_hbm, w_ref, sem)
    load.start()
    total = jnp.sum(pieces_ref[...].astype(F32).reshape(NZ, I, C * S), axis=0)
    high, low = split(total)
    scatter = one_hot(iota((S * I, I), 0) % I == iota((S * I, I), 1))
    keep = iota((S * I, C * S), 0) // I == iota((S * I, C * S), 1) % S
    fold = one_hot(iota((C * S, C), 0) // S == iota((C * S, C), 1))
    rg_high, rg_low = [
        dot(jnp.where(keep, dot(scatter, part), 0.0).astype(BF16), fold) for part in (high, low)
    ]
    right_grad = rg_high + rg_low
    high, low = split(left_grad_ref[...])
    order = to_residue_major()
    left_grad = dot(order, high, TN) + dot(order, low, TN)
    lg_high, lg_low = split(left_grad)
    rg_high, rg_low = rg_high.astype(BF16), rg_low.astype(BF16)
    normed_grad = (
        dot(lg_high, k1_ref[...])
        + dot(lg_low, k1_ref[...])
        + dot(rg_high, k2_ref[...])
        + dot(rg_low, k2_ref[...])
    )
    centred, inverse = layer_norm_parts(x_ref)
    unit = centred * inverse
    normed = (unit * gain_ref[...] + shift_ref[...]).astype(BF16)
    unit_grad = normed_grad * gain_ref[...]
    mean_one = jnp.mean(unit_grad, axis=-1, keepdims=True)
    mean_two = jnp.mean(unit_grad * unit, axis=-1, keepdims=True)
    align_ref[...] = inverse * (unit_grad - mean_one - unit * mean_two)
    gain_grad = jnp.sum(normed_grad * unit, axis=0, keepdims=True)
    offset_grad = jnp.sum(normed_grad, axis=0, keepdims=True)
    both = jnp.concatenate([lg_high, rg_high, lg_low, rg_low], axis=1)
    weights = dot(both, normed, TN)
    weights = weights[: 2 * C] + weights[2 * C :]
    weights = jnp.concatenate([weights[:, :Z], weights[:, Z:]], axis=0)
    biases = jnp.sum(jnp.concatenate([left_grad, right_grad], axis=1), axis=0, keepdims=True)
    biases = jnp.concatenate([biases, jnp.zeros((1, Z - 2 * C), F32)], axis=1)
    halves = (gain_grad[:, :Z], gain_grad[:, Z:], offset_grad[:, :Z], offset_grad[:, Z:])
    rest = jnp.concatenate(halves + (biases, bias_grad_ref[...], jnp.zeros((2, Z), F32)), axis=0)
    rest = jnp.where(iota((NP, 8, Z), 0) == 0, rest[None], 0.0)
    small = jnp.concatenate([weights.reshape(NP, 8, Z), rest], axis=1)
    load.wait()
    pack_ref[...] = packed(w_ref[...].astype(F32).reshape(NP, WR, Z), small)


def packed(w_rows, small):
    high = small.astype(BF16).astype(F32)
    return jnp.concatenate([w_rows, high, small - high], axis=1).astype(BF16)


def sum_kernel(in_ref, out_ref):
    total = jnp.sum(in_ref[...].astype(F32), axis=0)
    total = jnp.concatenate([total[:WR], total[WR : WR + 16] + total[WR + 16 :]], axis=0)
    out_ref[...] = jnp.broadcast_to(total[None], out_ref.shape)


def spread_kernel(in_ref, out_ref):
    total = jnp.sum(in_ref[...], axis=0)[None]
    out_ref[...] = jnp.broadcast_to(packed(total[:, :WR], total[:, WR:]), out_ref.shape)


def last_kernel(
    in_ref, gain_ref, offset_ref, lw_ref, lb_ref, rw_ref, rb_ref, w_ref, wb_ref, w_scratch
):
    blocks = in_ref[...].astype(F32)
    w_scratch[...] = blocks[:, :WR].reshape(C * C, Z)
    for c in range(C):
        w_ref[c * C : (c + 1) * C, :] = w_scratch[pl.ds(c, C, stride=C), :]
    small = blocks[:, WR : WR + 16] + blocks[:, WR + 16 :]
    weights = small[:, :8].reshape(Z, Z)
    rest = small[0, 8:]
    lw_ref[:, :Z] = weights[:C]
    lw_ref[:, Z:] = weights[2 * C : 3 * C]
    rw_ref[:, :Z] = weights[C : 2 * C]
    rw_ref[:, Z:] = weights[3 * C :]
    gain_ref[:, :Z] = rest[0:1]
    gain_ref[:, Z:] = rest[1:2]
    offset_ref[:, :Z] = rest[2:3]
    offset_ref[:, Z:] = rest[3:4]
    lb_ref[...] = rest[4:5, :C]
    rb_ref[...] = rest[4:5, C : 2 * C]
    wb_ref[...] = rest[5:6] * ROOT


def shape(dims, dtype):
    return jax.ShapeDtypeStruct(dims, dtype)


LATE = pl.CostEstimate(flops=100_000_000_000, bytes_accessed=0, transcendentals=0)
HBM = pl.BlockSpec(memory_space=pltpu.HBM)
VMEM = pl.BlockSpec(memory_space=pltpu.VMEM)


def in_hbm(array):
    return pltpu.with_memory_space_constraint(array, pltpu.HBM)


def in_vmem(*arrays):
    return [pltpu.with_memory_space_constraint(v, pltpu.VMEM) for v in arrays]


def ring(step, long):
    def number(x, z, y, core):
        return ((x % NX * NZ + z) * NY + y % NY) * 2 + core

    pairs = []
    for x, z, y, core in itertools.product(range(NX), range(NZ), range(NY), range(2)):
        by_x = long == (core == 0)
        target = number(x + step * by_x, z, y + step * (not by_x), core)
        pairs.append((number(x, z, y, core), target))
    return pairs


def shifted(arrays, long):
    return [arrays[0]] + [
        lax.ppermute(arrays[k], ("x", "z", "y", "dp"), ring(k, long)) for k in (1, 2, 3)
    ]


def call(body, name, mib, out_shape, scratch=(), **more):
    params = pltpu.CompilerParams(vmem_limit_bytes=mib * MIB)
    return pl.pallas_call(
        body, out_shape=out_shape, scratch_shapes=list(scratch), compiler_params=params, name=name, **more
    )


def exchange(array, axes):
    return lax.all_to_all(array, axes, 0, 0, tiled=True)


def blocking_exchange(array, axes):
    return lax.cond(lax.axis_index("x") < NX, lambda v: exchange(v, axes), jnp.zeros_like, array)


def per_device(x, gain, shift, k1, b1, k2, b2, w, bias, g):
    gain, shift, b1, b2, bias = [v.reshape(1, -1) for v in (gain, shift, b1, b2, bias)]
    x, k1, k2 = x.reshape(S * I, H), k1.T, k2.T
    inputs = (x, gain, shift, k1, b1, k2, b2, w, g)
    made = (
        ((I * S, C), BF16),
        ((G, C * S), BF16),
        ((C, C * Z), BF16),
        ((C * S, I * Z), BF16),
        (g.shape, BF16),
    )
    left, copies, wd, t, ordered, p0, p1, p2, p3 = call(
        first_kernel,
        "first",
        24,
        tuple(pltpu.HBM(*v) for v in made) + (pltpu.VMEM((Q, C * S), BF16),) * NX,
        [pltpu.VMEM(v.shape, v.dtype) for v in inputs]
        + [pltpu.VMEM(*v) for v in made]
        + [pltpu.VMEM((C * C, Z), F32), pltpu.VMEM(g.shape, F32), pltpu.SemaphoreType.DMA((len(inputs),))]
        + [pltpu.SemaphoreType.DMA((len(made),))],
        in_specs=[HBM] * len(inputs),
        out_specs=[HBM] * len(made) + [VMEM] * NX,
    )(*[in_hbm(v) for v in inputs])
    quarter = ((Q, C * S), BF16)
    column = ((G, C * S), BF16)
    planes = shifted((p0, p1, p2, p3), True)
    near = blocking_exchange(copies, "z")
    lines = shifted([near] * NY, False)
    parts = call(
        fold_kernel, "fold", 8, (pltpu.VMEM(*column),) * NY, [pltpu.VMEM((Q, C * S), F32)]
    )(*in_vmem(*planes))
    sums = shifted(parts, False)
    r0 = call(arrange_kernel, "arrange", 8, pltpu.VMEM(*quarter), [pltpu.VMEM((Q, C * S), F32)])(
        *in_vmem(*lines, parts[0])
    )
    r0, r1, r2, r3 = in_vmem(*shifted([r0] * NX, True))
    own = call(add_kernel, "add", 8, shape((G, C * S), F32), cost_estimate=LATE)(*in_vmem(*sums))
    pieces = exchange(own, "z")
    left_grad, w_part, bias_grad = call(
        second_kernel,
        "second",
        16,
        (shape((I * S, C), F32), pltpu.HBM((C, C, Z), BF16), shape((1, Z), F32)),
        [pltpu.VMEM(g.shape, BF16), pltpu.VMEM(wd.shape, BF16)]
        + [pltpu.VMEM((C * S, J), BF16), pltpu.VMEM((I * S, C * Z), BF16), pltpu.SemaphoreType.DMA((2,))],
        in_specs=[VMEM] * NX + [HBM] * 2 + [VMEM],
        cost_estimate=LATE,
    )(r0, r1, r2, r3, in_hbm(ordered), in_hbm(wd), left)
    align, pack = call(
        third_kernel,
        "third",
        12,
        (shape((S * I, H), F32), shape((NP, WR + 32, Z), BF16)),
        [pltpu.VMEM((C, C, Z), BF16), pltpu.SemaphoreType.DMA],
        in_specs=[VMEM, HBM] + [VMEM] * 7,
    )(left_grad, in_hbm(w_part), bias_grad, x, gain, shift, k1, k2, pieces)
    parts = exchange(pack, ("x", "y"))
    update = call(
        update_kernel,
        "update",
        20,
        pltpu.HBM((I, J, Z), BF16),
        [pltpu.VMEM(t.shape, BF16), pltpu.VMEM((I, J, Z), BF16), pltpu.VMEM((J, I * Z), F32)]
        + [pltpu.SemaphoreType.DMA, pltpu.SemaphoreType.DMA((NX,))],
        in_specs=[VMEM] * NX + [HBM] + [VMEM],
        out_specs=HBM,
    )(r0, r1, r2, r3, in_hbm(t), bias)
    plane = call(sum_kernel, "sum", 8, shape((NZ, WR + 16, Z), F32))(parts)
    column = exchange(plane, "z")
    block = call(spread_kernel, "spread", 8, shape((NP, WR + 32, Z), BF16))(column)
    sums = exchange(block, ("x", "y"))
    gain_g, offset_g, lw, lb, rw, rb, w_g, wb = call(
        last_kernel,
        "last",
        8,
        (
            shape((1, H), F32),
            shape((1, H), F32),
            shape((C, H), F32),
            shape((1, C), F32),
            shape((C, H), F32),
            shape((1, C), F32),
            shape((C * C, Z), F32),
            shape((1, Z), F32),
        ),
        [pltpu.VMEM((C * C, Z), F32)],
    )(sums)
    return (
        update,
        align.reshape(S, I, H),
        gain_g.reshape(H),
        offset_g.reshape(H),
        lw.T,
        lb.reshape(C),
        rw.T,
        rb.reshape(C),
        w_g,
        wb.reshape(Z),
    )


def solution(mesh):
    grid = Mesh(mesh.devices.reshape(NX, NZ, NY, 2), ("x", "z", "y", "dp"))
    dap = ("x", "z", "y")
    in_specs = (P("dp", dap, None),) + (P(),) * 8 + (P(("dp",) + dap, None, None),)
    out_specs = (
        P(("dp",) + dap, None, None),
        P("dp", dap, None),
        P("dp"),
        P("dp"),
        P("dp", None),
        P("dp"),
        P("dp", None),
        P("dp"),
        P("dp", None),
        P("dp"),
    )
    return jax.shard_map(
        per_device, mesh=grid, in_specs=in_specs, out_specs=out_specs, check_vma=False
    )
```

time: 123 us -> 110 us (0.89)
  waiting for transfers between devices: 23.6 us -> 13.3 us
  blocking collectives: 48.2 us -> 46 us
    ppermute x9 -> x12, waiting for transfers between devices: 17.2 us -> 11.2 us  [shifted(): lax.ppermute(arrays[k], ('x', 'z', 'y', 'dp'), ring(k, long))]
    all_to_all x2, waiting for transfers between devices: 6.42 us -> 2.14 us  [exchange(): return lax.all_to_all(array, axes, 0, 0, tiled=True)]
    all_to_all x2, starting transfers between devices: 11.1 us -> 8.73 us  [exchange(): return lax.all_to_all(array, axes, 0, 0, tiled=True)]
    all_to_all x2 -> x3, blocking collectives: 48.2 us -> 46 us  [exchange(): return lax.all_to_all(array, axes, 0, 0, tiled=True)]
    ppermute x9 -> x12, starting transfers between devices: 14.7 us -> 15.9 us  [shifted(): lax.ppermute(arrays[k], ('x', 'z', 'y', 'dp'), ring(k, long))]
    pallas_call x6 -> x8, Pallas kernels: 16.2 us -> 17.3 us  [the longest x1 6.95 us: per_device(): call(first_kernel, 'first', 24, tuple((pltpu.HBM(*v) for v in made)) + (p...]
  transfers between devices with their start and end apart: 11 -> 14, of which waited for: 6 -> 6; matrix products, arithmetic and copies ran while one was open for 0% -> 0% of each run, Pallas kernels for 10% -> 11%
where the time goes in v3:
time: 110 us; the launch traced here: 109 us
  blocking collectives  46 us (42%)
  starting transfers between devices  24.7 us (22%)
  Pallas kernels  24.1 us (22%)
  waiting for transfers between devices  13.3 us (12%)
    all_to_all x3, blocking collectives, exchange(): return lax.all_to_all(array, axes, 0, 0, tiled=True)  46 us
    ppermute x12, starting transfers between devices, shifted(): lax.ppermute(arrays[k], ('x', 'z', 'y', 'dp'), ring(k, long))  15.9 us
    ppermute x12, waiting for transfers between devices, shifted(): lax.ppermute(arrays[k], ('x', 'z', 'y', 'dp'), ring(k, long))  11.2 us
    all_to_all x2, starting transfers between devices, exchange(): return lax.all_to_all(array, axes, 0, 0, tiled=True)  8.73 us
    pallas_call x1, Pallas kernels, per_device(): call(first_kernel, 'first', 24, tuple((pltpu.HBM(*v) for v in made)) + (p...  6.95 us
    pallas_call x1, Pallas kernels, per_device(): call(second_kernel, 'second', 16, (shape((I * S, C), F32), pltpu.HBM((C,...  5.7 us
    pallas_call x1, Pallas kernels, per_device(): call(update_kernel, 'update', 20, pltpu.HBM((I, J, Z), BF16), [pltpu.VMEM...  5.38 us
    pallas_call x1, Pallas kernels, per_device(): call(third_kernel, 'third', 12, (shape((S * I, H), F32), shape((NP, WR +...  2.92 us
  transfers between devices with their start and end apart: 14, of which 6 were waited for; matrix products, arithmetic and copies ran while one was open for 0% of the time, Pallas kernels for 11%

profile of v3, /device:TPU:8, one launch (start us, length us, event | category | flops | bytes accessed | tf_op | source)
XLA Modules:
  0.0 109.0 jit_solution(10682754559820034719)
XLA Ops:
  0.6 7.0 %first.1 = (bf16[256,32]{1,0:T(8,128)(2,1)}, bf16[64,1024]{1,0:T(8,128)(2,1)}, bf16[32,4096]{1,0:T(8,128)(2,1)}, bf16[1024,1024]{1,0:T(8,128)(2,1)}, bf16[8,1024...) custom-call(bf16[256,256]{1,0:T(8,128)(2,1)} %bitcast.22, ...), custom_call_target="tpu_custom_call" | custom-call | tf_op jit(solution)/shard_map/first/pallas_call | solution.py:377
  7.6 1.6 %collective-permute-start.3 = (bf16[256,1024]{1,0:T(8,128)(2,1)}, bf16[256,1024]{1,0:T(8,128)(2,1)S(1)}, u32[]{:S(2)}, u32[]{:S(2)}) collective-permute-start(bf16[256,1024]{1,0:T(8,128)(2,1)} %get-tuple-element.42), channel_id=1, source_target_pairs={{0,64},{1,3},{2,66},{3,5},{4,68},{5,7},{6,70},{7,1},{8,72},{9,11},... | collective-permute-start | bytes 1572872 | tf_op jit(solution)/shard_map/ppermute | solution.py:347
  9.2 2.7 %collective-permute-start.4 = (bf16[256,1024]{1,0:T(8,128)(2,1)S(1)}, bf16[256,1024]{1,0:T(8,128)(2,1)S(1)}, u32[]{:S(2)}, u32[]{:S(2)}) collective-permute-start(bf16[256,1024]{1,0:T(8,128)(2,1)S(1)} %get-tuple-element.43), channel_id=1, source_target_pairs={{0,128},{1,5},{2,130},{3,7},{4,132},{5,1},{6,134},{7,3},{8,136},{9... | collective-permute-start | bytes 1572872 | tf_op jit(solution)/shard_map/ppermute | solution.py:347
  11.9 1.4 %collective-permute-start.5 = (bf16[256,1024]{1,0:T(8,128)(2,1)S(1)}, bf16[256,1024]{1,0:T(8,128)(2,1)S(1)}, u32[]{:S(2)}, u32[]{:S(2)}) collective-permute-start(bf16[256,1024]{1,0:T(8,128)(2,1)S(1)} %get-tuple-element.44), channel_id=1, source_target_pairs={{0,192},{1,7},{2,194},{3,1},{4,196},{5,3},{6,198},{7,5},{8,200},{9... | collective-permute-start | bytes 1572872 | tf_op jit(solution)/shard_map/ppermute | solution.py:347
  13.3 17.5 %conditional.1 = (bf16[64,1024]{1,0:T(8,128)(2,1)S(1)}) conditional(s32[]{:T(128)} %convert_element_type.3, () %tuple.14, bf16[64,1024]{1,0:T(8,128)(2,1)} %get-tuple-element.40), branch_computations={%region_0.0_spmd, %region_1.0_spmd} | conditional | bytes 262152 | solution.py:363
  13.3 17.5 %all_to_all.35 = bf16[8,8,1024]{2,1,0:T(8,128)(2,1)S(1)} all-to-all(bf16[8,8,1024]{2,1,0:T(8,128)(2,1)} %bitcast.33), channel_id=1, replica_groups=mesh['x'=4,'z'=8,'y'=4,'dp'=2] {'z'}, dimensions={0} | all-to-all | bytes 262144 | tf_op jit(solution)/shard_map/cond/branch_1_fun/all_to_all | solution.py:359
  30.9 1.6 %collective-permute-start = (bf16[64,1024]{1,0:T(8,128)(2,1)S(1)}, bf16[64,1024]{1,0:T(8,128)(2,1)S(1)}, u32[]{:S(2)}, u32[]{:S(2)}) collective-permute-start(bf16[64,1024]{1,0:T(8,128)(2,1)S(1)} %get-tuple-element.66.refs_0_), channel_id=1, source_target_pairs={{0,2},{1,65},{2,4},{3,67},{4,6},{5,69},{6,0},{7,71},{8,10},{9,73},... | collective-permute-start | bytes 393224 | tf_op jit(solution)/shard_map/ppermute | solution.py:347
  32.5 0.9 collective-permute-start.1
  33.4 0.0 collective-permute-done.3.refs_1_
  33.4 2.4 %collective-permute-start.2 = (bf16[64,1024]{1,0:T(8,128)(2,1)S(1)}, bf16[64,1024]{1,0:T(8,128)(2,1)S(1)}, u32[]{:S(2)}, u32[]{:S(2)}) collective-permute-start(bf16[64,1024]{1,0:T(8,128)(2,1)S(1)} %get-tuple-element.66.refs_0_), channel_id=1, source_target_pairs={{0,6},{1,193},{2,0},{3,195},{4,2},{5,197},{6,4},{7,199},{8,14},{9,... | collective-permute-start | bytes 393224 | tf_op jit(solution)/shard_map/ppermute | solution.py:347
  35.8 0.0 collective-permute-done.4.refs_2_
  35.8 0.0 collective-permute-done.5.refs_3_
  35.8 0.3 fold.1
  36.1 0.3 collective-permute-start.10
  36.4 1.5 %collective-permute-start.11 = (bf16[64,1024]{1,0:T(8,128)(2,1)S(1)}, bf16[64,1024]{1,0:T(8,128)(2,1)S(1)}, u32[]{:S(2)}, u32[]{:S(2)}) collective-permute-start(bf16[64,1024]{1,0:T(8,128)(2,1)S(1)} %get-tuple-element.55), channel_id=1, source_target_pairs={{0,6},{1,193},{2,0},{3,195},{4,2},{5,197},{6,4},{7,199},{8,14},{9,... | collective-permute-start | bytes 393224 | tf_op jit(solution)/shard_map/ppermute | solution.py:347
  37.9 0.0 collective-permute-done.refs_1_
  37.9 1.1 %collective-permute-start.9 = (bf16[64,1024]{1,0:T(8,128)(2,1)S(1)}, bf16[64,1024]{1,0:T(8,128)(2,1)S(1)}, u32[]{:S(2)}, u32[]{:S(2)}) collective-permute-start(bf16[64,1024]{1,0:T(8,128)(2,1)S(1)} %get-tuple-element.53), channel_id=1, source_target_pairs={{0,2},{1,65},{2,4},{3,67},{4,6},{5,69},{6,0},{7,71},{8,10},{9,73},... | collective-permute-start | bytes 393224 | tf_op jit(solution)/shard_map/ppermute | solution.py:347
  39.0 0.0 collective-permute-done.1.refs_2_
  39.0 0.7 collective-permute-done.2.refs_3_
  39.8 0.1 arrange.1.r0_ref
  39.9 0.0 copy-start.6
  39.9 1.1 %collective-permute-start.6 = (bf16[256,1024]{1,0:T(8,128)(2,1)S(1)}, bf16[256,1024]{1,0:T(8,128)(2,1)S(1)}, u32[]{:S(2)}, u32[]{:S(2)}) collective-permute-start(bf16[256,1024]{1,0:T(8,128)(2,1)S(1)} %arrange.1.r0_ref), channel_id=1, source_target_pairs={{0,64},{1,3},{2,66},{3,5},{4,68},{5,7},{6,70},{7,1},{8,72},{9,11},... | collective-permute-start | bytes 1572872 | tf_op jit(solution)/shard_map/ppermute | solution.py:347
  41.1 0.9 collective-permute-start.7
  41.9 1.5 %collective-permute-done.10.refs_2_ = bf16[64,1024]{1,0:T(8,128)(2,1)S(1)} collective-permute-done((bf16[64,1024]{1,0:T(8,128)(2,1)S(1)}, bf16[64,1024]{1,0:T(8,128)(2,1)S(1)}, u32[]{:S(2)}, u32[]{:S(2)}) %collective-permute-start.10) | collective-permute-done | bytes 131104 | tf_op jit(solution)/shard_map/ppermute | solution.py:347
  43.5 0.4 collective-permute-start.8
  43.8 1.9 %collective-permute-done.11.refs_3_ = bf16[64,1024]{1,0:T(8,128)(2,1)S(1)} collective-permute-done((bf16[64,1024]{1,0:T(8,128)(2,1)S(1)}, bf16[64,1024]{1,0:T(8,128)(2,1)S(1)}, u32[]{:S(2)}, u32[]{:S(2)}) %collective-permute-start.11) | collective-permute-done | bytes 131104 | tf_op jit(solution)/shard_map/ppermute | solution.py:347
  45.7 0.0 collective-permute-done.9.refs_1_
  45.7 0.8 add.1
  46.5 3.4 %all-to-all-start.1 = ((f32[8,8,1024]{2,1,0:T(8,128)}), f32[8,8,1024]{2,1,0:T(8,128)S(1)}, u32[]{:S(2)}, u32[]{:S(2)}) async-start(f32[8,8,1024]{2,1,0:T(8,128)} %bitcast.10), calls=%async_computation.1 | async-start | bytes 524288 | tf_op jit(solution)/shard_map/all_to_all | solution.py:359
  49.9 6.1 %collective-permute-done.6.r1_ref = bf16[256,1024]{1,0:T(8,128)(2,1)S(1)} collective-permute-done((bf16[256,1024]{1,0:T(8,128)(2,1)S(1)}, bf16[256,1024]{1,0:T(8,128)(2,1)S(1)}, u32[]{:S(2)}, u32[]{:S(2)}) %collective-permute-start.6) | collective-permute-done | bytes 524320 | tf_op jit(solution)/shard_map/ppermute | solution.py:347
  56.0 0.0 collective-permute-done.7.r2_ref
  56.0 0.9 collective-permute-done.8.r3_ref
  56.9 0.0 copy-done.6
  56.9 0.0 copy-start
  56.9 0.0 copy-start.1
  56.9 0.0 copy-start.2
  56.9 0.0 copy-start.3
  56.9 0.0 copy-start.4
  56.9 5.7 %second.1 = (f32[256,32]{1,0:T(8,128)S(1)}, bf16[32,32,128]{2,1,0:T(8,128)(2,1)}, f32[1,128]{1,0:T(1,128)S(1)}) custom-call(bf16[256,1024]{1,0:T(8,128)(2,1)S(1)} %arrange.1.r0_ref, bf16[256,1024]{1,0:T(8,128)(2,1)S(1)} %collective-permute-done.6.r1_ref, bf16[256,1024]{1,0:T(8,128)(2,1)S(1)} %collective-permute-done.7.r2_ref, ...), custom_call_target="tpu_custom_call" | custom-call | flops 99999997952 | tf_op jit(solution)/shard_map/second/pallas_call | solution.py:404
  62.7 0.0 all-to-all-done.1
  62.7 0.0 copy-done
  62.7 0.0 copy-done.1
  62.7 0.0 copy-done.2
  62.7 0.0 copy-done.3
  62.7 0.0 copy-done.4
  62.7 0.0 copy-start.5
  62.7 2.9 %third.1 = (f32[256,256]{1,0:T(8,128)}, bf16[16,96,128]{2,1,0:T(8,128)(2,1)S(1)}) custom-call(f32[256,32]{1,0:T(8,128)S(1)} %get-tuple-element.50.left_grad_ref, bf16[32,32,128]{2,1,0:T(8,128)(2,1)} %get-tuple-element.51.w_hbm, f32[1,128]{1,0:T(1,128)S(1)} %get-tuple-element.52.bias_grad_ref, bf16[256,256]{1,0:T(8,128)(2,1)S(1)} %bitcast.23, ...), custom_call_target="tpu_custom_call" | custom-call | tf_op jit(solution)/shard_map/third/pallas_call | solution.py:414
  65.7 14.9 %all_to_all.36.in_ref = bf16[16,96,128]{2,1,0:T(8,128)(2,1)S(1)} all-to-all(bf16[16,96,128]{2,1,0:T(8,128)(2,1)S(1)} %get-tuple-element.57), channel_id=1, replica_groups=mesh['x'=4,'z'=8,'y'=4,'dp'=2] {'x','y'}, dimensions={0} | all-to-all | bytes 786432 | tf_op jit(solution)/shard_map/all_to_all | solution.py:359
  80.6 0.1 sum.1
  80.6 13.6 %all_to_all.37.in_ref = f32[8,80,128]{2,1,0:T(8,128)S(1)} all-to-all(f32[8,80,128]{2,1,0:T(8,128)S(1)} %sum.1), channel_id=1, replica_groups=mesh['x'=4,'z'=8,'y'=4,'dp'=2] {'z'}, dimensions={0} | all-to-all | bytes 655360 | tf_op jit(solution)/shard_map/all_to_all | solution.py:359
  94.2 0.8 spread.1
  95.0 5.3 %all-to-all-start.4 = ((bf16[16,96,128]{2,1,0:T(8,128)(2,1)}), bf16[16,96,128]{2,1,0:T(8,128)(2,1)S(1)}, u32[]{:S(2)}, u32[]{:S(2)}) async-start(bf16[16,96,128]{2,1,0:T(8,128)(2,1)} %spread.1), calls=%async_computation.4 | async-start | bytes 786432 | tf_op jit(solution)/shard_map/all_to_all | solution.py:359
  100.3 0.0 copy-done.5
  100.3 5.4 %update.1 = bf16[8,1024,128]{2,1,0:T(8,128)(2,1)} custom-call(bf16[256,1024]{1,0:T(8,128)(2,1)S(1)} %arrange.1.r0_ref, bf16[256,1024]{1,0:T(8,128)(2,1)S(1)} %collective-permute-done.6.r1_ref, bf16[256,1024]{1,0:T(8,128)(2,1)S(1)} %collective-permute-done.7.r2_ref, bf16[256,1024]{1,0:T(8,128)(2,1)S(1)} %collective-permute-done.8.r3_ref, ...), custom_call_target="tpu_custom_call" | custom-call | tf_op jit(solution)/shard_map/update/pallas_call | solution.py:423
  105.7 2.1 %all-to-all-done.4.in_ref = bf16[16,96,128]{2,1,0:T(8,128)(2,1)S(1)} async-done(((bf16[16,96,128]{2,1,0:T(8,128)(2,1)}), bf16[16,96,128]{2,1,0:T(8,128)(2,1)S(1)}, u32[]{:S(2)}, u32[]{:S(2)}) %all-to-all-start.4) | async-done | bytes 393248 | tf_op jit(solution)/shard_map/all_to_all | solution.py:359
  107.8 1.2 %last.1 = (f32[1,256]{1,0:T(1,128)}, f32[1,256]{1,0:T(1,128)}, f32[32,256]{1,0:T(8,128)}, f32[1,32]{1,0:T(1,128)}, f32[32,256]{1,0:T(8,128)}, /*index=5*/f32[1,3...) custom-call(bf16[16,96,128]{2,1,0:T(8,128)(2,1)S(1)} %all-to-all-done.4.in_ref), custom_call_target="tpu_custom_call" | custom-call | tf_op jit(solution)/shard_map/last/pallas_call | solution.py:437
Async XLA Ops:
  7.6 25.8 %collective-permute-start.3 = (bf16[256,1024]{1,0:T(8,128)(2,1)}, bf16[256,1024]{1,0:T(8,128)(2,1)S(1)}, u32[]{:S(2)}, u32[]{:S(2)}) collective-permute-start(bf16[256,1024]{1,0:T(8,128)(2,1)} %get-tuple-element.42), channel_id=1, source_target_pairs={{0,64},{1,3},{2,66},{3,5},{4,68},{5,7},{6,70},{7,1},{8,72},{9,11},... | collective-permute-start | bytes 1572872 | tf_op jit(solution)/shard_map/ppermute | solution.py:347
  9.2 26.6 %collective-permute-start.4 = (bf16[256,1024]{1,0:T(8,128)(2,1)S(1)}, bf16[256,1024]{1,0:T(8,128)(2,1)S(1)}, u32[]{:S(2)}, u32[]{:S(2)}) collective-permute-start(bf16[256,1024]{1,0:T(8,128)(2,1)S(1)} %get-tuple-element.43), channel_id=1, source_target_pairs={{0,128},{1,5},{2,130},{3,7},{4,132},{5,1},{6,134},{7,3},{8,136},{9... | collective-permute-start | bytes 1572872 | tf_op jit(solution)/shard_map/ppermute | solution.py:347
  11.9 23.9 %collective-permute-start.5 = (bf16[256,1024]{1,0:T(8,128)(2,1)S(1)}, bf16[256,1024]{1,0:T(8,128)(2,1)S(1)}, u32[]{:S(2)}, u32[]{:S(2)}) collective-permute-start(bf16[256,1024]{1,0:T(8,128)(2,1)S(1)} %get-tuple-element.44), channel_id=1, source_target_pairs={{0,192},{1,7},{2,194},{3,1},{4,196},{5,3},{6,198},{7,5},{8,200},{9... | collective-permute-start | bytes 1572872 | tf_op jit(solution)/shard_map/ppermute | solution.py:347
  30.9 7.0 %collective-permute-start = (bf16[64,1024]{1,0:T(8,128)(2,1)S(1)}, bf16[64,1024]{1,0:T(8,128)(2,1)S(1)}, u32[]{:S(2)}, u32[]{:S(2)}) collective-permute-start(bf16[64,1024]{1,0:T(8,128)(2,1)S(1)} %get-tuple-element.66.refs_0_), channel_id=1, source_target_pairs={{0,2},{1,65},{2,4},{3,67},{4,6},{5,69},{6,0},{7,71},{8,10},{9,73},... | collective-permute-start | bytes 393224 | tf_op jit(solution)/shard_map/ppermute | solution.py:347
  32.5 6.6 %collective-permute-start.1 = (bf16[64,1024]{1,0:T(8,128)(2,1)S(1)}, bf16[64,1024]{1,0:T(8,128)(2,1)S(1)}, u32[]{:S(2)}, u32[]{:S(2)}) collective-permute-start(bf16[64,1024]{1,0:T(8,128)(2,1)S(1)} %get-tuple-element.66.refs_0_), channel_id=1, source_target_pairs={{0,4},{1,129},{2,6},{3,131},{4,0},{5,133},{6,2},{7,135},{8,12},{9,... | collective-permute-start | bytes 393224 | tf_op jit(solution)/shard_map/ppermute | solution.py:347
  33.4 6.4 %collective-permute-start.2 = (bf16[64,1024]{1,0:T(8,128)(2,1)S(1)}, bf16[64,1024]{1,0:T(8,128)(2,1)S(1)}, u32[]{:S(2)}, u32[]{:S(2)}) collective-permute-start(bf16[64,1024]{1,0:T(8,128)(2,1)S(1)} %get-tuple-element.66.refs_0_), channel_id=1, source_target_pairs={{0,6},{1,193},{2,0},{3,195},{4,2},{5,197},{6,4},{7,199},{8,14},{9,... | collective-permute-start | bytes 393224 | tf_op jit(solution)/shard_map/ppermute | solution.py:347
  36.1 7.4 %collective-permute-start.10 = (bf16[64,1024]{1,0:T(8,128)(2,1)S(1)}, bf16[64,1024]{1,0:T(8,128)(2,1)S(1)}, u32[]{:S(2)}, u32[]{:S(2)}) collective-permute-start(bf16[64,1024]{1,0:T(8,128)(2,1)S(1)} %get-tuple-element.54), channel_id=1, source_target_pairs={{0,4},{1,129},{2,6},{3,131},{4,0},{5,133},{6,2},{7,135},{8,12},{9,... | collective-permute-start | bytes 393224 | tf_op jit(solution)/shard_map/ppermute | solution.py:347
  36.4 9.3 %collective-permute-start.11 = (bf16[64,1024]{1,0:T(8,128)(2,1)S(1)}, bf16[64,1024]{1,0:T(8,128)(2,1)S(1)}, u32[]{:S(2)}, u32[]{:S(2)}) collective-permute-start(bf16[64,1024]{1,0:T(8,128)(2,1)S(1)} %get-tuple-element.55), channel_id=1, source_target_pairs={{0,6},{1,193},{2,0},{3,195},{4,2},{5,197},{6,4},{7,199},{8,14},{9,... | collective-permute-start | bytes 393224 | tf_op jit(solution)/shard_map/ppermute | solution.py:347
  37.9 7.9 %collective-permute-start.9 = (bf16[64,1024]{1,0:T(8,128)(2,1)S(1)}, bf16[64,1024]{1,0:T(8,128)(2,1)S(1)}, u32[]{:S(2)}, u32[]{:S(2)}) collective-permute-start(bf16[64,1024]{1,0:T(8,128)(2,1)S(1)} %get-tuple-element.53), channel_id=1, source_target_pairs={{0,2},{1,65},{2,4},{3,67},{4,6},{5,69},{6,0},{7,71},{8,10},{9,73},... | collective-permute-start | bytes 393224 | tf_op jit(solution)/shard_map/ppermute | solution.py:347
  39.9 17.0 %copy-start.6 = (bf16[256,32]{1,0:T(8,128)(2,1)S(1)}, bf16[256,32]{1,0:T(8,128)(2,1)}, u32[]{:S(2)}) copy-start(bf16[256,32]{1,0:T(8,128)(2,1)} %get-tuple-element.49.left_ref) | copy-start | bytes 49156
  39.9 16.1 %collective-permute-start.6 = (bf16[256,1024]{1,0:T(8,128)(2,1)S(1)}, bf16[256,1024]{1,0:T(8,128)(2,1)S(1)}, u32[]{:S(2)}, u32[]{:S(2)}) collective-permute-start(bf16[256,1024]{1,0:T(8,128)(2,1)S(1)} %arrange.1.r0_ref), channel_id=1, source_target_pairs={{0,64},{1,3},{2,66},{3,5},{4,68},{5,7},{6,70},{7,1},{8,72},{9,11},... | collective-permute-start | bytes 1572872 | tf_op jit(solution)/shard_map/ppermute | solution.py:347
  41.1 14.9 %collective-permute-start.7 = (bf16[256,1024]{1,0:T(8,128)(2,1)S(1)}, bf16[256,1024]{1,0:T(8,128)(2,1)S(1)}, u32[]{:S(2)}, u32[]{:S(2)}) collective-permute-start(bf16[256,1024]{1,0:T(8,128)(2,1)S(1)} %arrange.1.r0_ref), channel_id=1, source_target_pairs={{0,128},{1,5},{2,130},{3,7},{4,132},{5,1},{6,134},{7,3},{8,136},{9... | collective-permute-start | bytes 1572872 | tf_op jit(solution)/shard_map/ppermute | solution.py:347
  43.5 13.4 %collective-permute-start.8 = (bf16[256,1024]{1,0:T(8,128)(2,1)S(1)}, bf16[256,1024]{1,0:T(8,128)(2,1)S(1)}, u32[]{:S(2)}, u32[]{:S(2)}) collective-permute-start(bf16[256,1024]{1,0:T(8,128)(2,1)S(1)} %arrange.1.r0_ref), channel_id=1, source_target_pairs={{0,192},{1,7},{2,194},{3,1},{4,196},{5,3},{6,198},{7,5},{8,200},{9... | collective-permute-start | bytes 1572872 | tf_op jit(solution)/shard_map/ppermute | solution.py:347
  46.5 16.1 %all-to-all-start.1 = ((f32[8,8,1024]{2,1,0:T(8,128)}), f32[8,8,1024]{2,1,0:T(8,128)S(1)}, u32[]{:S(2)}, u32[]{:S(2)}) async-start(f32[8,8,1024]{2,1,0:T(8,128)} %bitcast.10), calls=%async_computation.1 | async-start | bytes 524288 | tf_op jit(solution)/shard_map/all_to_all | solution.py:359
  56.9 5.8 %copy-start = (bf16[32,8,256]{2,1,0:T(8,128)(2,1)S(1)}, bf16[32,8,256]{2,1,0:T(8,128)(2,1)}, u32[]{:S(2)}) copy-start(bf16[32,8,256]{2,1,0:T(8,128)(2,1)} %param.12) | copy-start | bytes 393220
  56.9 5.8 %copy-start.1 = (bf16[256,32]{0,1:T(8,128)(2,1)S(1)}, bf16[256,32]{0,1:T(8,128)(2,1)}, u32[]{:S(2)}) copy-start(bf16[256,32]{0,1:T(8,128)(2,1)} %param.15) | copy-start | bytes 49156
  56.9 5.8 %copy-start.2 = (bf16[256,32]{0,1:T(8,128)(2,1)S(1)}, bf16[256,32]{0,1:T(8,128)(2,1)}, u32[]{:S(2)}) copy-start(bf16[256,32]{0,1:T(8,128)(2,1)} %param.17) | copy-start | bytes 49156
  56.9 5.8 %copy-start.3 = (f32[256]{0:T(256)S(1)}, f32[256]{0:T(256)}, u32[]{:S(2)}) copy-start(f32[256]{0:T(256)} %param.13) | copy-start | bytes 3076
  56.9 5.8 %copy-start.4 = (f32[256]{0:T(256)S(1)}, f32[256]{0:T(256)}, u32[]{:S(2)}) copy-start(f32[256]{0:T(256)} %param.14) | copy-start | bytes 3076
  62.7 37.6 %copy-start.5 = (f32[128]{0:T(128)S(1)}, f32[128]{0:T(128)}, u32[]{:S(2)}) copy-start(f32[128]{0:T(128)} %param.20) | copy-start | bytes 1540
  95.0 12.9 %all-to-all-start.4 = ((bf16[16,96,128]{2,1,0:T(8,128)(2,1)}), bf16[16,96,128]{2,1,0:T(8,128)(2,1)S(1)}, u32[]{:S(2)}, u32[]{:S(2)}) async-start(bf16[16,96,128]{2,1,0:T(8,128)(2,1)} %spread.1), calls=%async_computation.4 | async-start | bytes 786432 | tf_op jit(solution)/shard_map/all_to_all | solution.py:359

commit v4 on v3

--- a/solution.py
+++ b/solution.py
@@ -70,10 +70,6 @@
     own, _, long_stride, short_stride = places()
     start = (own + NX - k) % NX * long_stride + n // NY * (NY * I) + n % NY * short_stride
     return pl.ds(pl.multiple_of(start, I), I)
-
-
-def rows_of(g_ref, k):
-    return jnp.concatenate([g_ref[i, k * Q : (k + 1) * Q, :] for i in range(I)], axis=1)
 
 
 def copies_between(sources, targets, sems):
@@ -127,9 +123,11 @@
             start = k * Q + n * I
             ordered_ref[:, start : start + 2 * I, :] = jnp.concatenate(pair, axis=1).astype(BF16)
     stores[4].start()
+    rows = jnp.concatenate([ordered_ref[i] for i in range(I)], axis=1)
+    whole = dot(rows, t_ref[...], NT) * SCALE
     for k in range(NX):
-        rows = rows_of(ordered_ref, (NX - k) % NX)
-        partial_refs[k][...] = (dot(rows, t_ref[...], NT) * SCALE).astype(BF16)
+        start = (NX - k) % NX * Q
+        partial_refs[k][...] = whole[start : start + Q].astype(BF16)
     for store in stores:
         store.wait()
 
@@ -203,15 +201,17 @@
     for load in loads:
         load.start()
     for k, right in enumerate((r0_ref, r1_ref, r2_ref, r3_ref)):
-        rt_scratch[:, k * Q : (k + 1) * Q] = right[...].T
+        rt_scratch[: C * S, k * Q : (k + 1) * Q] = right[...].T
     loads[0].wait()
+    rt_scratch[C * S :, :] = jnp.ones((16, J), BF16)
     bias_grad = jnp.zeros((1, Z), F32)
     for i in range(0, I, 2):
         pair = []
         for n in (i, i + 1):
             pair.append(g_ref[n])
-            bias_grad = bias_grad + jnp.sum(pair[-1].astype(F32), axis=0, keepdims=True)
-        u = dot(rt_scratch[...], jnp.concatenate(pair, axis=1)).astype(BF16)
+        u = dot(rt_scratch[...], jnp.concatenate(pair, axis=1))
+        bias_grad = bias_grad + (u[C * S : C * S + 1, :Z] + u[C * S : C * S + 1, Z:])
+        u = u[: C * S].astype(BF16)
         for e in range(2):
             for d in range(C):
                 m_scratch[(i + e) * S : (i + e + 1) * S, d * Z : (d + 1) * Z] = u[
@@ -281,13 +281,8 @@
 
 def sum_kernel(in_ref, out_ref):
     total = jnp.sum(in_ref[...].astype(F32), axis=0)
-    total = jnp.concatenate([total[:WR], total[WR : WR + 16] + total[WR + 16 :]], axis=0)
-    out_ref[...] = jnp.broadcast_to(total[None], out_ref.shape)
-
-
-def spread_kernel(in_ref, out_ref):
-    total = jnp.sum(in_ref[...], axis=0)[None]
-    out_ref[...] = jnp.broadcast_to(packed(total[:, :WR], total[:, WR:]), out_ref.shape)
+    block = packed(total[None, :WR], total[None, WR : WR + 16] + total[None, WR + 16 :])
+    out_ref[...] = jnp.broadcast_to(block, out_ref.shape)
 
 
 def last_kernel(
@@ -407,7 +402,7 @@
         16,
         (shape((I * S, C), F32), pltpu.HBM((C, C, Z), BF16), shape((1, Z), F32)),
         [pltpu.VMEM(g.shape, BF16), pltpu.VMEM(wd.shape, BF16)]
-        + [pltpu.VMEM((C * S, J), BF16), pltpu.VMEM((I * S, C * Z), BF16), pltpu.SemaphoreType.DMA((2,))],
+        + [pltpu.VMEM((C * S + 16, J), BF16), pltpu.VMEM((I * S, C * Z), BF16), pltpu.SemaphoreType.DMA((2,))],
         in_specs=[VMEM] * NX + [HBM] * 2 + [VMEM],
         cost_estimate=LATE,
     )(r0, r1, r2, r3, in_hbm(ordered), in_hbm(wd), left)
@@ -430,9 +425,9 @@
         in_specs=[VMEM] * NX + [HBM] + [VMEM],
         out_specs=HBM,
     )(r0, r1, r2, r3, in_hbm(t), bias)
-    plane = call(sum_kernel, "sum", 8, shape((NZ, WR + 16, Z), F32))(parts)
+    plane = call(sum_kernel, "sum", 8, shape((NZ, WR + 32, Z), BF16))(parts)
     column = exchange(plane, "z")
-    block = call(spread_kernel, "spread", 8, shape((NP, WR + 32, Z), BF16))(column)
+    block = call(sum_kernel, "spread", 8, shape((NP, WR + 32, Z), BF16))(column)
     sums = exchange(block, ("x", "y"))
     gain_g, offset_g, lw, lb, rw, rb, w_g, wb = call(
         last_kernel,

time: 110 us -> 107 us (0.973)
  blocking collectives: 46 us -> 44.6 us
    all_to_all x3, blocking collectives: 46 us -> 44.6 us  [exchange(): return lax.all_to_all(array, axes, 0, 0, tiled=True)]
  transfers between devices with their start and end apart: 14 -> 14, of which waited for: 6 -> 6; matrix products, arithmetic and copies ran while one was open for 0% -> 0% of each run, Pallas kernels for 11% -> 12%
where the time goes in v4:
time: 107 us
  blocking collectives  44.6 us (42%)
  starting transfers between devices  24.7 us (23%)
  Pallas kernels  23.4 us (22%)
  waiting for transfers between devices  13.3 us (12%)
    all_to_all x3, blocking collectives, exchange(): return lax.all_to_all(array, axes, 0, 0, tiled=True)  44.6 us
    ppermute x12, starting transfers between devices, shifted(): lax.ppermute(arrays[k], ('x', 'z', 'y', 'dp'), ring(k, long))  15.8 us
    ppermute x12, waiting for transfers between devices, shifted(): lax.ppermute(arrays[k], ('x', 'z', 'y', 'dp'), ring(k, long))  11.2 us
    all_to_all x2, starting transfers between devices, exchange(): return lax.all_to_all(array, axes, 0, 0, tiled=True)  8.91 us
    pallas_call x1, Pallas kernels, per_device(): call(first_kernel, 'first', 24, tuple((pltpu.HBM(*v) for v in made)) + (p...  6.18 us
    pallas_call x1, Pallas kernels, per_device(): call(second_kernel, 'second', 16, (shape((I * S, C), F32), pltpu.HBM((C,...  5.74 us
    pallas_call x1, Pallas kernels, per_device(): call(update_kernel, 'update', 20, pltpu.HBM((I, J, Z), BF16), [pltpu.VMEM...  5.38 us
    pallas_call x1, Pallas kernels, per_device(): call(third_kernel, 'third', 12, (shape((S * I, H), F32), shape((NP, WR +...  2.91 us
  transfers between devices with their start and end apart: 14, of which 6 were waited for; matrix products, arithmetic and copies ran while one was open for 0% of the time, Pallas kernels for 12%

profile of v4, /device:TPU:8, one launch (start us, length us, event | category | flops | bytes accessed | tf_op | source)
XLA Modules:
  0.0 106.9 jit_solution(7179501545550783296)
XLA Ops:
  0.6 6.2 %first.1 = (bf16[256,32]{1,0:T(8,128)(2,1)}, bf16[64,1024]{1,0:T(8,128)(2,1)}, bf16[32,4096]{1,0:T(8,128)(2,1)}, bf16[1024,1024]{1,0:T(8,128)(2,1)}, bf16[8,1024...) custom-call(bf16[256,256]{1,0:T(8,128)(2,1)} %bitcast.22, ...), custom_call_target="tpu_custom_call" | custom-call | tf_op jit(solution)/shard_map/first/pallas_call | solution.py:372
  6.8 1.6 %collective-permute-start.3 = (bf16[256,1024]{1,0:T(8,128)(2,1)}, bf16[256,1024]{1,0:T(8,128)(2,1)S(1)}, u32[]{:S(2)}, u32[]{:S(2)}) collective-permute-start(bf16[256,1024]{1,0:T(8,128)(2,1)} %get-tuple-element.42), channel_id=1, source_target_pairs={{0,64},{1,3},{2,66},{3,5},{4,68},{5,7},{6,70},{7,1},{8,72},{9,11},... | collective-permute-start | bytes 1572872 | tf_op jit(solution)/shard_map/ppermute | solution.py:342
  8.4 2.7 %collective-permute-start.4 = (bf16[256,1024]{1,0:T(8,128)(2,1)S(1)}, bf16[256,1024]{1,0:T(8,128)(2,1)S(1)}, u32[]{:S(2)}, u32[]{:S(2)}) collective-permute-start(bf16[256,1024]{1,0:T(8,128)(2,1)S(1)} %get-tuple-element.43), channel_id=1, source_target_pairs={{0,128},{1,5},{2,130},{3,7},{4,132},{5,1},{6,134},{7,3},{8,136},{9... | collective-permute-start | bytes 1572872 | tf_op jit(solution)/shard_map/ppermute | solution.py:342
  11.1 1.4 %collective-permute-start.5 = (bf16[256,1024]{1,0:T(8,128)(2,1)S(1)}, bf16[256,1024]{1,0:T(8,128)(2,1)S(1)}, u32[]{:S(2)}, u32[]{:S(2)}) collective-permute-start(bf16[256,1024]{1,0:T(8,128)(2,1)S(1)} %get-tuple-element.44), channel_id=1, source_target_pairs={{0,192},{1,7},{2,194},{3,1},{4,196},{5,3},{6,198},{7,5},{8,200},{9... | collective-permute-start | bytes 1572872 | tf_op jit(solution)/shard_map/ppermute | solution.py:342
  12.6 17.5 %conditional.1 = (bf16[64,1024]{1,0:T(8,128)(2,1)S(1)}) conditional(s32[]{:T(128)} %convert_element_type.3, () %tuple.14, bf16[64,1024]{1,0:T(8,128)(2,1)} %get-tuple-element.40), branch_computations={%region_0.0_spmd, %region_1.0_spmd} | conditional | bytes 262152 | solution.py:358
  12.6 17.5 %all_to_all.35 = bf16[8,8,1024]{2,1,0:T(8,128)(2,1)S(1)} all-to-all(bf16[8,8,1024]{2,1,0:T(8,128)(2,1)} %bitcast.33), channel_id=1, replica_groups=mesh['x'=4,'z'=8,'y'=4,'dp'=2] {'z'}, dimensions={0} | all-to-all | bytes 262144 | tf_op jit(solution)/shard_map/cond/branch_1_fun/all_to_all | solution.py:354
  30.1 1.6 %collective-permute-start = (bf16[64,1024]{1,0:T(8,128)(2,1)S(1)}, bf16[64,1024]{1,0:T(8,128)(2,1)S(1)}, u32[]{:S(2)}, u32[]{:S(2)}) collective-permute-start(bf16[64,1024]{1,0:T(8,128)(2,1)S(1)} %get-tuple-element.66.refs_0_), channel_id=1, source_target_pairs={{0,2},{1,65},{2,4},{3,67},{4,6},{5,69},{6,0},{7,71},{8,10},{9,73},... | collective-permute-start | bytes 393224 | tf_op jit(solution)/shard_map/ppermute | solution.py:342
  31.7 0.9 collective-permute-start.1
  32.6 0.0 collective-permute-done.3.refs_1_
  32.6 2.4 %collective-permute-start.2 = (bf16[64,1024]{1,0:T(8,128)(2,1)S(1)}, bf16[64,1024]{1,0:T(8,128)(2,1)S(1)}, u32[]{:S(2)}, u32[]{:S(2)}) collective-permute-start(bf16[64,1024]{1,0:T(8,128)(2,1)S(1)} %get-tuple-element.66.refs_0_), channel_id=1, source_target_pairs={{0,6},{1,193},{2,0},{3,195},{4,2},{5,197},{6,4},{7,199},{8,14},{9,... | collective-permute-start | bytes 393224 | tf_op jit(solution)/shard_map/ppermute | solution.py:342
  35.0 0.0 collective-permute-done.4.refs_2_
  35.0 0.0 collective-permute-done.5.refs_3_
  35.0 0.3 fold.1
  35.3 0.3 collective-permute-start.10
  35.6 1.5 %collective-permute-start.11 = (bf16[64,1024]{1,0:T(8,128)(2,1)S(1)}, bf16[64,1024]{1,0:T(8,128)(2,1)S(1)}, u32[]{:S(2)}, u32[]{:S(2)}) collective-permute-start(bf16[64,1024]{1,0:T(8,128)(2,1)S(1)} %get-tuple-element.55), channel_id=1, source_target_pairs={{0,6},{1,193},{2,0},{3,195},{4,2},{5,197},{6,4},{7,199},{8,14},{9,... | collective-permute-start | bytes 393224 | tf_op jit(solution)/shard_map/ppermute | solution.py:342
  37.1 0.0 collective-permute-done.refs_1_
  37.1 1.1 %collective-permute-start.9 = (bf16[64,1024]{1,0:T(8,128)(2,1)S(1)}, bf16[64,1024]{1,0:T(8,128)(2,1)S(1)}, u32[]{:S(2)}, u32[]{:S(2)}) collective-permute-start(bf16[64,1024]{1,0:T(8,128)(2,1)S(1)} %get-tuple-element.53), channel_id=1, source_target_pairs={{0,2},{1,65},{2,4},{3,67},{4,6},{5,69},{6,0},{7,71},{8,10},{9,73},... | collective-permute-start | bytes 393224 | tf_op jit(solution)/shard_map/ppermute | solution.py:342
  38.2 0.0 collective-permute-done.1.refs_2_
  38.3 0.7 collective-permute-done.2.refs_3_
  39.0 0.1 arrange.1.r0_ref
  39.1 0.0 copy-start.6
  39.1 1.0 collective-permute-start.6
  40.2 1.0 collective-permute-start.7
  41.2 1.6 %collective-permute-done.10.refs_2_ = bf16[64,1024]{1,0:T(8,128)(2,1)S(1)} collective-permute-done((bf16[64,1024]{1,0:T(8,128)(2,1)S(1)}, bf16[64,1024]{1,0:T(8,128)(2,1)S(1)}, u32[]{:S(2)}, u32[]{:S(2)}) %collective-permute-start.10) | collective-permute-done | bytes 131104 | tf_op jit(solution)/shard_map/ppermute | solution.py:342
  42.8 0.2 collective-permute-start.8
  43.0 2.1 %collective-permute-done.11.refs_3_ = bf16[64,1024]{1,0:T(8,128)(2,1)S(1)} collective-permute-done((bf16[64,1024]{1,0:T(8,128)(2,1)S(1)}, bf16[64,1024]{1,0:T(8,128)(2,1)S(1)}, u32[]{:S(2)}, u32[]{:S(2)}) %collective-permute-start.11) | collective-permute-done | bytes 131104 | tf_op jit(solution)/shard_map/ppermute | solution.py:342
  45.1 0.0 collective-permute-done.9.refs_1_
  45.1 0.8 add.1
  45.8 3.6 %all-to-all-start.1 = ((f32[8,8,1024]{2,1,0:T(8,128)}), f32[8,8,1024]{2,1,0:T(8,128)S(1)}, u32[]{:S(2)}, u32[]{:S(2)}) async-start(f32[8,8,1024]{2,1,0:T(8,128)} %bitcast.10), calls=%async_computation.1 | async-start | bytes 524288 | tf_op jit(solution)/shard_map/all_to_all | solution.py:354
  49.4 5.8 %collective-permute-done.6.r1_ref = bf16[256,1024]{1,0:T(8,128)(2,1)S(1)} collective-permute-done((bf16[256,1024]{1,0:T(8,128)(2,1)S(1)}, bf16[256,1024]{1,0:T(8,128)(2,1)S(1)}, u32[]{:S(2)}, u32[]{:S(2)}) %collective-permute-start.6) | collective-permute-done | bytes 524320 | tf_op jit(solution)/shard_map/ppermute | solution.py:342
  55.2 0.0 collective-permute-done.7.r2_ref
  55.2 0.9 collective-permute-done.8.r3_ref
  56.1 0.0 copy-done.6
  56.1 0.0 copy-start
  56.1 0.0 copy-start.1
  56.1 0.0 copy-start.2
  56.1 0.0 copy-start.3
  56.2 0.0 copy-start.4
  56.2 5.7 %second.1 = (f32[256,32]{1,0:T(8,128)S(1)}, bf16[32,32,128]{2,1,0:T(8,128)(2,1)}, f32[1,128]{1,0:T(1,128)S(1)}) custom-call(bf16[256,1024]{1,0:T(8,128)(2,1)S(1)} %arrange.1.r0_ref, bf16[256,1024]{1,0:T(8,128)(2,1)S(1)} %collective-permute-done.6.r1_ref, bf16[256,1024]{1,0:T(8,128)(2,1)S(1)} %collective-permute-done.7.r2_ref, ...), custom_call_target="tpu_custom_call" | custom-call | flops 99999997952 | tf_op jit(solution)/shard_map/second/pallas_call | solution.py:399
  61.9 0.0 copy-start.5
  61.9 0.0 all-to-all-done.1
  61.9 0.0 copy-done
  62.0 0.0 copy-done.1
  62.0 0.0 copy-done.2
  62.0 0.0 copy-done.3
  62.0 0.0 copy-done.4
  62.0 2.9 %third.1 = (f32[256,256]{1,0:T(8,128)}, bf16[16,96,128]{2,1,0:T(8,128)(2,1)S(1)}) custom-call(f32[256,32]{1,0:T(8,128)S(1)} %get-tuple-element.50.left_grad_ref, bf16[32,32,128]{2,1,0:T(8,128)(2,1)} %get-tuple-element.51.w_hbm, f32[1,128]{1,0:T(1,128)S(1)} %get-tuple-element.52.bias_grad_ref, bf16[256,256]{1,0:T(8,128)(2,1)S(1)} %bitcast.23, ...), custom_call_target="tpu_custom_call" | custom-call | tf_op jit(solution)/shard_map/third/pallas_call | solution.py:409
  64.9 14.9 %all_to_all.36.in_ref = bf16[16,96,128]{2,1,0:T(8,128)(2,1)S(1)} all-to-all(bf16[16,96,128]{2,1,0:T(8,128)(2,1)S(1)} %get-tuple-element.57), channel_id=1, replica_groups=mesh['x'=4,'z'=8,'y'=4,'dp'=2] {'x','y'}, dimensions={0} | all-to-all | bytes 786432 | tf_op jit(solution)/shard_map/all_to_all | solution.py:354
  79.8 0.1 sum.1
  79.9 12.2 %all_to_all.37.in_ref = bf16[8,96,128]{2,1,0:T(8,128)(2,1)S(1)} all-to-all(bf16[8,96,128]{2,1,0:T(8,128)(2,1)S(1)} %sum.1), channel_id=1, replica_groups=mesh['x'=4,'z'=8,'y'=4,'dp'=2] {'z'}, dimensions={0} | all-to-all | bytes 393216 | tf_op jit(solution)/shard_map/all_to_all | solution.py:354
  92.1 0.8 spread.1
  92.8 5.3 %all-to-all-start.4 = ((bf16[16,96,128]{2,1,0:T(8,128)(2,1)}), bf16[16,96,128]{2,1,0:T(8,128)(2,1)S(1)}, u32[]{:S(2)}, u32[]{:S(2)}) async-start(bf16[16,96,128]{2,1,0:T(8,128)(2,1)} %spread.1), calls=%async_computation.4 | async-start | bytes 786432 | tf_op jit(solution)/shard_map/all_to_all | solution.py:354
  98.2 0.0 copy-done.5
  98.2 5.4 %update.1 = bf16[8,1024,128]{2,1,0:T(8,128)(2,1)} custom-call(bf16[256,1024]{1,0:T(8,128)(2,1)S(1)} %arrange.1.r0_ref, bf16[256,1024]{1,0:T(8,128)(2,1)S(1)} %collective-permute-done.6.r1_ref, bf16[256,1024]{1,0:T(8,128)(2,1)S(1)} %collective-permute-done.7.r2_ref, bf16[256,1024]{1,0:T(8,128)(2,1)S(1)} %collective-permute-done.8.r3_ref, ...), custom_call_target="tpu_custom_call" | custom-call | tf_op jit(solution)/shard_map/update/pallas_call | solution.py:418
  103.6 2.1 %all-to-all-done.4.in_ref = bf16[16,96,128]{2,1,0:T(8,128)(2,1)S(1)} async-done(((bf16[16,96,128]{2,1,0:T(8,128)(2,1)}), bf16[16,96,128]{2,1,0:T(8,128)(2,1)S(1)}, u32[]{:S(2)}, u32[]{:S(2)}) %all-to-all-start.4) | async-done | bytes 393248 | tf_op jit(solution)/shard_map/all_to_all | solution.py:354
  105.7 1.2 %last.1 = (f32[1,256]{1,0:T(1,128)}, f32[1,256]{1,0:T(1,128)}, f32[32,256]{1,0:T(8,128)}, f32[1,32]{1,0:T(1,128)}, f32[32,256]{1,0:T(8,128)}, /*index=5*/f32[1,3...) custom-call(bf16[16,96,128]{2,1,0:T(8,128)(2,1)S(1)} %all-to-all-done.4.in_ref), custom_call_target="tpu_custom_call" | custom-call | tf_op jit(solution)/shard_map/last/pallas_call | solution.py:432
Async XLA Ops:
  6.8 25.8 %collective-permute-start.3 = (bf16[256,1024]{1,0:T(8,128)(2,1)}, bf16[256,1024]{1,0:T(8,128)(2,1)S(1)}, u32[]{:S(2)}, u32[]{:S(2)}) collective-permute-start(bf16[256,1024]{1,0:T(8,128)(2,1)} %get-tuple-element.42), channel_id=1, source_target_pairs={{0,64},{1,3},{2,66},{3,5},{4,68},{5,7},{6,70},{7,1},{8,72},{9,11},... | collective-permute-start | bytes 1572872 | tf_op jit(solution)/shard_map/ppermute | solution.py:342
  8.4 26.6 %collective-permute-start.4 = (bf16[256,1024]{1,0:T(8,128)(2,1)S(1)}, bf16[256,1024]{1,0:T(8,128)(2,1)S(1)}, u32[]{:S(2)}, u32[]{:S(2)}) collective-permute-start(bf16[256,1024]{1,0:T(8,128)(2,1)S(1)} %get-tuple-element.43), channel_id=1, source_target_pairs={{0,128},{1,5},{2,130},{3,7},{4,132},{5,1},{6,134},{7,3},{8,136},{9... | collective-permute-start | bytes 1572872 | tf_op jit(solution)/shard_map/ppermute | solution.py:342
  11.1 23.9 %collective-permute-start.5 = (bf16[256,1024]{1,0:T(8,128)(2,1)S(1)}, bf16[256,1024]{1,0:T(8,128)(2,1)S(1)}, u32[]{:S(2)}, u32[]{:S(2)}) collective-permute-start(bf16[256,1024]{1,0:T(8,128)(2,1)S(1)} %get-tuple-element.44), channel_id=1, source_target_pairs={{0,192},{1,7},{2,194},{3,1},{4,196},{5,3},{6,198},{7,5},{8,200},{9... | collective-permute-start | bytes 1572872 | tf_op jit(solution)/shard_map/ppermute | solution.py:342
  30.1 7.0 %collective-permute-start = (bf16[64,1024]{1,0:T(8,128)(2,1)S(1)}, bf16[64,1024]{1,0:T(8,128)(2,1)S(1)}, u32[]{:S(2)}, u32[]{:S(2)}) collective-permute-start(bf16[64,1024]{1,0:T(8,128)(2,1)S(1)} %get-tuple-element.66.refs_0_), channel_id=1, source_target_pairs={{0,2},{1,65},{2,4},{3,67},{4,6},{5,69},{6,0},{7,71},{8,10},{9,73},... | collective-permute-start | bytes 393224 | tf_op jit(solution)/shard_map/ppermute | solution.py:342
  31.7 6.6 %collective-permute-start.1 = (bf16[64,1024]{1,0:T(8,128)(2,1)S(1)}, bf16[64,1024]{1,0:T(8,128)(2,1)S(1)}, u32[]{:S(2)}, u32[]{:S(2)}) collective-permute-start(bf16[64,1024]{1,0:T(8,128)(2,1)S(1)} %get-tuple-element.66.refs_0_), channel_id=1, source_target_pairs={{0,4},{1,129},{2,6},{3,131},{4,0},{5,133},{6,2},{7,135},{8,12},{9,... | collective-permute-start | bytes 393224 | tf_op jit(solution)/shard_map/ppermute | solution.py:342
  32.6 6.4 %collective-permute-start.2 = (bf16[64,1024]{1,0:T(8,128)(2,1)S(1)}, bf16[64,1024]{1,0:T(8,128)(2,1)S(1)}, u32[]{:S(2)}, u32[]{:S(2)}) collective-permute-start(bf16[64,1024]{1,0:T(8,128)(2,1)S(1)} %get-tuple-element.66.refs_0_), channel_id=1, source_target_pairs={{0,6},{1,193},{2,0},{3,195},{4,2},{5,197},{6,4},{7,199},{8,14},{9,... | collective-permute-start | bytes 393224 | tf_op jit(solution)/shard_map/ppermute | solution.py:342
  35.3 7.5 %collective-permute-start.10 = (bf16[64,1024]{1,0:T(8,128)(2,1)S(1)}, bf16[64,1024]{1,0:T(8,128)(2,1)S(1)}, u32[]{:S(2)}, u32[]{:S(2)}) collective-permute-start(bf16[64,1024]{1,0:T(8,128)(2,1)S(1)} %get-tuple-element.54), channel_id=1, source_target_pairs={{0,4},{1,129},{2,6},{3,131},{4,0},{5,133},{6,2},{7,135},{8,12},{9,... | collective-permute-start | bytes 393224 | tf_op jit(solution)/shard_map/ppermute | solution.py:342
  35.6 9.4 %collective-permute-start.11 = (bf16[64,1024]{1,0:T(8,128)(2,1)S(1)}, bf16[64,1024]{1,0:T(8,128)(2,1)S(1)}, u32[]{:S(2)}, u32[]{:S(2)}) collective-permute-start(bf16[64,1024]{1,0:T(8,128)(2,1)S(1)} %get-tuple-element.55), channel_id=1, source_target_pairs={{0,6},{1,193},{2,0},{3,195},{4,2},{5,197},{6,4},{7,199},{8,14},{9,... | collective-permute-start | bytes 393224 | tf_op jit(solution)/shard_map/ppermute | solution.py:342
  37.1 8.0 %collective-permute-start.9 = (bf16[64,1024]{1,0:T(8,128)(2,1)S(1)}, bf16[64,1024]{1,0:T(8,128)(2,1)S(1)}, u32[]{:S(2)}, u32[]{:S(2)}) collective-permute-start(bf16[64,1024]{1,0:T(8,128)(2,1)S(1)} %get-tuple-element.53), channel_id=1, source_target_pairs={{0,2},{1,65},{2,4},{3,67},{4,6},{5,69},{6,0},{7,71},{8,10},{9,73},... | collective-permute-start | bytes 393224 | tf_op jit(solution)/shard_map/ppermute | solution.py:342
  39.1 17.0 %copy-start.6 = (bf16[256,32]{1,0:T(8,128)(2,1)S(1)}, bf16[256,32]{1,0:T(8,128)(2,1)}, u32[]{:S(2)}) copy-start(bf16[256,32]{1,0:T(8,128)(2,1)} %get-tuple-element.49.left_ref) | copy-start | bytes 49156
  39.1 16.1 %collective-permute-start.6 = (bf16[256,1024]{1,0:T(8,128)(2,1)S(1)}, bf16[256,1024]{1,0:T(8,128)(2,1)S(1)}, u32[]{:S(2)}, u32[]{:S(2)}) collective-permute-start(bf16[256,1024]{1,0:T(8,128)(2,1)S(1)} %arrange.1.r0_ref), channel_id=1, source_target_pairs={{0,64},{1,3},{2,66},{3,5},{4,68},{5,7},{6,70},{7,1},{8,72},{9,11},... | collective-permute-start | bytes 1572872 | tf_op jit(solution)/shard_map/ppermute | solution.py:342
  40.2 15.0 %collective-permute-start.7 = (bf16[256,1024]{1,0:T(8,128)(2,1)S(1)}, bf16[256,1024]{1,0:T(8,128)(2,1)S(1)}, u32[]{:S(2)}, u32[]{:S(2)}) collective-permute-start(bf16[256,1024]{1,0:T(8,128)(2,1)S(1)} %arrange.1.r0_ref), channel_id=1, source_target_pairs={{0,128},{1,5},{2,130},{3,7},{4,132},{5,1},{6,134},{7,3},{8,136},{9... | collective-permute-start | bytes 1572872 | tf_op jit(solution)/shard_map/ppermute | solution.py:342
  42.8 13.3 %collective-permute-start.8 = (bf16[256,1024]{1,0:T(8,128)(2,1)S(1)}, bf16[256,1024]{1,0:T(8,128)(2,1)S(1)}, u32[]{:S(2)}, u32[]{:S(2)}) collective-permute-start(bf16[256,1024]{1,0:T(8,128)(2,1)S(1)} %arrange.1.r0_ref), channel_id=1, source_target_pairs={{0,192},{1,7},{2,194},{3,1},{4,196},{5,3},{6,198},{7,5},{8,200},{9... | collective-permute-start | bytes 1572872 | tf_op jit(solution)/shard_map/ppermute | solution.py:342
  45.8 16.1 %all-to-all-start.1 = ((f32[8,8,1024]{2,1,0:T(8,128)}), f32[8,8,1024]{2,1,0:T(8,128)S(1)}, u32[]{:S(2)}, u32[]{:S(2)}) async-start(f32[8,8,1024]{2,1,0:T(8,128)} %bitcast.10), calls=%async_computation.1 | async-start | bytes 524288 | tf_op jit(solution)/shard_map/all_to_all | solution.py:354
  56.1 5.8 %copy-start = (bf16[32,8,256]{2,1,0:T(8,128)(2,1)S(1)}, bf16[32,8,256]{2,1,0:T(8,128)(2,1)}, u32[]{:S(2)}) copy-start(bf16[32,8,256]{2,1,0:T(8,128)(2,1)} %param.12) | copy-start | bytes 393220
  56.1 5.8 %copy-start.1 = (bf16[256,32]{0,1:T(8,128)(2,1)S(1)}, bf16[256,32]{0,1:T(8,128)(2,1)}, u32[]{:S(2)}) copy-start(bf16[256,32]{0,1:T(8,128)(2,1)} %param.15) | copy-start | bytes 49156
  56.1 5.8 %copy-start.2 = (bf16[256,32]{0,1:T(8,128)(2,1)S(1)}, bf16[256,32]{0,1:T(8,128)(2,1)}, u32[]{:S(2)}) copy-start(bf16[256,32]{0,1:T(8,128)(2,1)} %param.17) | copy-start | bytes 49156
  56.1 5.8 %copy-start.3 = (f32[256]{0:T(256)S(1)}, f32[256]{0:T(256)}, u32[]{:S(2)}) copy-start(f32[256]{0:T(256)} %param.13) | copy-start | bytes 3076
  56.2 5.8 %copy-start.4 = (f32[256]{0:T(256)S(1)}, f32[256]{0:T(256)}, u32[]{:S(2)}) copy-start(f32[256]{0:T(256)} %param.14) | copy-start | bytes 3076
  61.9 36.2 %copy-start.5 = (f32[128]{0:T(128)S(1)}, f32[128]{0:T(128)}, u32[]{:S(2)}) copy-start(f32[128]{0:T(128)} %param.20) | copy-start | bytes 1540
  92.8 12.9 %all-to-all-start.4 = ((bf16[16,96,128]{2,1,0:T(8,128)(2,1)}), bf16[16,96,128]{2,1,0:T(8,128)(2,1)S(1)}, u32[]{:S(2)}, u32[]{:S(2)}) async-start(bf16[16,96,128]{2,1,0:T(8,128)(2,1)} %spread.1), calls=%async_computation.4 | async-start | bytes 786432 | tf_op jit(solution)/shard_map/all_to_all | solution.py:354

commit v5 on v4

--- a/solution.py
+++ b/solution.py
@@ -192,33 +192,58 @@
         store.wait()
 
 
-def second_kernel(
-    r0_ref, r1_ref, r2_ref, r3_ref, g_hbm, wd_hbm, left_ref,
-    left_grad_ref, w_part_ref, bias_grad_ref,
-    g_ref, wd_ref, rt_scratch, m_scratch, sems,
-):
-    loads = copies_between((g_hbm, wd_hbm), (g_ref, wd_ref), sems)
+HALF = J // 2
+EARLY, LATER = (0, 3), (1, 2)
+
+
+def half_product(quarters, rights, g_hbm, g_ref, rt_scratch, sems, finish):
+    loads = [
+        pltpu.make_async_copy(
+            g_hbm.at[:, pl.ds(k * Q, Q), :], g_ref.at[:, pl.ds(n * Q, Q), :], sems.at[n]
+        )
+        for n, k in enumerate(quarters)
+    ]
     for load in loads:
         load.start()
-    for k, right in enumerate((r0_ref, r1_ref, r2_ref, r3_ref)):
+    for k, right in enumerate(rights):
         rt_scratch[: C * S, k * Q : (k + 1) * Q] = right[...].T
-    loads[0].wait()
-    rt_scratch[C * S :, :] = jnp.ones((16, J), BF16)
-    bias_grad = jnp.zeros((1, Z), F32)
+    rt_scratch[C * S :, :] = jnp.ones((16, HALF), BF16)
+    for load in loads:
+        load.wait()
     for i in range(0, I, 2):
-        pair = []
-        for n in (i, i + 1):
-            pair.append(g_ref[n])
-        u = dot(rt_scratch[...], jnp.concatenate(pair, axis=1))
-        bias_grad = bias_grad + (u[C * S : C * S + 1, :Z] + u[C * S : C * S + 1, Z:])
+        finish(i, dot(rt_scratch[...], jnp.concatenate([g_ref[i], g_ref[i + 1]], axis=1)))
+
+
+def early_kernel(r0_ref, re_ref, g_hbm, u_ref, g_ref, rt_scratch, sem):
+    def finish(i, u):
+        u_ref[:, i * Z : (i + 2) * Z] = u
+
+    half_product(EARLY, (r0_ref, re_ref), g_hbm, g_ref, rt_scratch, sem, finish)
+
+
+def second_kernel(
+    ra_ref, rb_ref, u_ref, g_hbm, wd_hbm, left_ref,
+    left_grad_ref, w_part_ref, bias_grad_ref,
+    g_ref, wd_ref, rt_scratch, m_scratch, sem, wd_sem,
+):
+    load = pltpu.make_async_copy(wd_hbm, wd_ref, wd_sem)
+    load.start()
+    bias_grad = []
+
+    def finish(i, u):
+        u = u + u_ref[:, i * Z : (i + 2) * Z]
+        bias_grad.append(u[C * S : C * S + 1, :Z] + u[C * S : C * S + 1, Z:])
         u = u[: C * S].astype(BF16)
         for e in range(2):
             for d in range(C):
                 m_scratch[(i + e) * S : (i + e + 1) * S, d * Z : (d + 1) * Z] = u[
                     d * S : (d + 1) * S, e * Z : (e + 1) * Z
                 ]
+
+    half_product(LATER, (ra_ref, rb_ref), g_hbm, g_ref, rt_scratch, sem, finish)
+    bias_grad = sum(bias_grad)
     bias_grad_ref[...] = bias_grad
-    loads[1].wait()
+    load.wait()
     left_grad_ref[...] = dot(m_scratch[...], wd_ref[...], NT) * SCALE
     w_part = dot(left_ref[...], m_scratch[...], TN) * SCALE
     for d in range(C):
@@ -338,9 +363,10 @@
 
 
 def shifted(arrays, long):
-    return [arrays[0]] + [
-        lax.ppermute(arrays[k], ("x", "z", "y", "dp"), ring(k, long)) for k in (1, 2, 3)
-    ]
+    moved = {
+        k: lax.ppermute(arrays[k], ("x", "z", "y", "dp"), ring(k, long)) for k in (1, 3, 2)
+    }
+    return [arrays[0], moved[1], moved[2], moved[3]]
 
 
 def call(body, name, mib, out_shape, scratch=(), **more):
@@ -393,19 +419,29 @@
     r0 = call(arrange_kernel, "arrange", 8, pltpu.VMEM(*quarter), [pltpu.VMEM((Q, C * S), F32)])(
         *in_vmem(*lines, parts[0])
     )
-    r0, r1, r2, r3 = in_vmem(*shifted([r0] * NX, True))
+    rights = in_vmem(*shifted([r0] * NX, True))
     own = call(add_kernel, "add", 8, shape((G, C * S), F32), cost_estimate=LATE)(*in_vmem(*sums))
     pieces = exchange(own, "z")
+    rt_type = ((C * S + 16, HALF), BF16)
+    half = call(
+        early_kernel,
+        "early",
+        16,
+        pltpu.VMEM((C * S + 16, I * Z), F32),
+        [pltpu.VMEM((I, HALF, Z), BF16), pltpu.VMEM(*rt_type), pltpu.SemaphoreType.DMA((2,))],
+        in_specs=[VMEM] * 2 + [HBM],
+    )(*[rights[k] for k in EARLY], in_hbm(ordered))
     left_grad, w_part, bias_grad = call(
         second_kernel,
         "second",
         16,
         (shape((I * S, C), F32), pltpu.HBM((C, C, Z), BF16), shape((1, Z), F32)),
-        [pltpu.VMEM(g.shape, BF16), pltpu.VMEM(wd.shape, BF16)]
-        + [pltpu.VMEM((C * S + 16, J), BF16), pltpu.VMEM((I * S, C * Z), BF16), pltpu.SemaphoreType.DMA((2,))],
-        in_specs=[VMEM] * NX + [HBM] * 2 + [VMEM],
+        [pltpu.VMEM((I, HALF, Z), BF16), pltpu.VMEM(wd.shape, BF16)]
+        + [pltpu.VMEM(*rt_type), pltpu.VMEM((I * S, C * Z), BF16)]
+        + [pltpu.SemaphoreType.DMA((2,)), pltpu.SemaphoreType.DMA],
+        in_specs=[VMEM] * 3 + [HBM] * 2 + [VMEM],
         cost_estimate=LATE,
-    )(r0, r1, r2, r3, in_hbm(ordered), in_hbm(wd), left)
+    )(*[rights[k] for k in LATER], *in_vmem(half), in_hbm(ordered), in_hbm(wd), left)
     align, pack = call(
         third_kernel,
         "third",
@@ -424,7 +460,7 @@
         + [pltpu.SemaphoreType.DMA, pltpu.SemaphoreType.DMA((NX,))],
         in_specs=[VMEM] * NX + [HBM] + [VMEM],
         out_specs=HBM,
-    )(r0, r1, r2, r3, in_hbm(t), bias)
+    )(*rights, in_hbm(t), bias)
     plane = call(sum_kernel, "sum", 8, shape((NZ, WR + 32, Z), BF16))(parts)
     column = exchange(plane, "z")
     block = call(sum_kernel, "spread", 8, shape((NP, WR + 32, Z), BF16))(column)

time: 107 us -> 105 us (0.981)
  waiting for transfers between devices: 13.3 us -> 9.84 us
  blocking collectives: 44.6 us -> 42.5 us
  starting transfers between devices: 24.7 us -> 26.6 us
  Pallas kernels: 23.4 us -> 24.6 us
    ppermute x12, waiting for transfers between devices: 11.2 us -> 7.7 us  [shifted(): lax.ppermute(arrays[k], ('x', 'z', 'y', 'dp'), ring(k, long))]
    pallas_call x0 -> x1, Pallas kernels: none -> 2.53 us  [per_device(): call(early_kernel, 'early', 16, pltpu.VMEM((C * S + 16, I * Z), F32), [pl...]
    all_to_all x3, blocking collectives: 44.6 us -> 42.5 us  [exchange(): return lax.all_to_all(array, axes, 0, 0, tiled=True)]
    ppermute x12, starting transfers between devices: 15.8 us -> 17.7 us  [shifted(): lax.ppermute(arrays[k], ('x', 'z', 'y', 'dp'), ring(k, long))]
    pallas_call x1, Pallas kernels: 5.74 us -> 4.37 us  [per_device(): call(second_kernel, 'second', 16, (shape((I * S, C), F32), pltpu.HBM((C,...]
  transfers between devices with their start and end apart: 14 -> 14, of which waited for: 6 -> 4; matrix products, arithmetic and copies ran while one was open for 0% -> 0% of each run, Pallas kernels for 12% -> 13%
where the time goes in v5:
time: 105 us; the launch traced here: 104 us
  blocking collectives  42.5 us (40%)
  starting transfers between devices  26.6 us (25%)
  Pallas kernels  24.6 us (23%)
  waiting for transfers between devices  9.84 us (9%)
    all_to_all x3, blocking collectives, exchange(): return lax.all_to_all(array, axes, 0, 0, tiled=True)  42.5 us
    ppermute x12, starting transfers between devices, shifted(): lax.ppermute(arrays[k], ('x', 'z', 'y', 'dp'), ring(k, long))  17.7 us
    all_to_all x2, starting transfers between devices, exchange(): return lax.all_to_all(array, axes, 0, 0, tiled=True)  8.93 us
    ppermute x12, waiting for transfers between devices, shifted(): lax.ppermute(arrays[k], ('x', 'z', 'y', 'dp'), ring(k, long))  7.7 us
    pallas_call x1, Pallas kernels, per_device(): call(first_kernel, 'first', 24, tuple((pltpu.HBM(*v) for v in made)) + (p...  6.18 us
    pallas_call x1, Pallas kernels, per_device(): call(update_kernel, 'update', 20, pltpu.HBM((I, J, Z), BF16), [pltpu.VMEM...  5.38 us
    pallas_call x1, Pallas kernels, per_device(): call(second_kernel, 'second', 16, (shape((I * S, C), F32), pltpu.HBM((C,...  4.37 us
    pallas_call x1, Pallas kernels, per_device(): call(third_kernel, 'third', 12, (shape((S * I, H), F32), shape((NP, WR +...  2.92 us
  transfers between devices with their start and end apart: 14, of which 4 were waited for; matrix products, arithmetic and copies ran while one was open for 0% of the time, Pallas kernels for 13%

profile of v5, /device:TPU:8, one launch (start us, length us, event | category | flops | bytes accessed | tf_op | source)
XLA Modules:
  0.0 104.4 jit_solution(15087513335565986125)
XLA Ops:
  0.6 6.2 %first.1 = (bf16[256,32]{1,0:T(8,128)(2,1)}, bf16[64,1024]{1,0:T(8,128)(2,1)}, bf16[32,4096]{1,0:T(8,128)(2,1)}, bf16[1024,1024]{1,0:T(8,128)(2,1)}, bf16[8,1024...) custom-call(bf16[256,256]{1,0:T(8,128)(2,1)} %bitcast.22, ...), custom_call_target="tpu_custom_call" | custom-call | tf_op jit(solution)/shard_map/first/pallas_call | solution.py:398
  6.8 1.6 %collective-permute-start.3 = (bf16[256,1024]{1,0:T(8,128)(2,1)}, bf16[256,1024]{1,0:T(8,128)(2,1)S(1)}, u32[]{:S(2)}, u32[]{:S(2)}) collective-permute-start(bf16[256,1024]{1,0:T(8,128)(2,1)} %get-tuple-element.42), channel_id=1, source_target_pairs={{0,64},{1,3},{2,66},{3,5},{4,68},{5,7},{6,70},{7,1},{8,72},{9,11},... | collective-permute-start | bytes 1572872 | tf_op jit(solution)/shard_map/ppermute | solution.py:367
  8.4 2.7 %collective-permute-start.4 = (bf16[256,1024]{1,0:T(8,128)(2,1)S(1)}, bf16[256,1024]{1,0:T(8,128)(2,1)S(1)}, u32[]{:S(2)}, u32[]{:S(2)}) collective-permute-start(bf16[256,1024]{1,0:T(8,128)(2,1)S(1)} %get-tuple-element.43), channel_id=1, source_target_pairs={{0,128},{1,5},{2,130},{3,7},{4,132},{5,1},{6,134},{7,3},{8,136},{9... | collective-permute-start | bytes 1572872 | tf_op jit(solution)/shard_map/ppermute | solution.py:367
  11.1 1.4 %collective-permute-start.5 = (bf16[256,1024]{1,0:T(8,128)(2,1)S(1)}, bf16[256,1024]{1,0:T(8,128)(2,1)S(1)}, u32[]{:S(2)}, u32[]{:S(2)}) collective-permute-start(bf16[256,1024]{1,0:T(8,128)(2,1)S(1)} %get-tuple-element.44), channel_id=1, source_target_pairs={{0,192},{1,7},{2,194},{3,1},{4,196},{5,3},{6,198},{7,5},{8,200},{9... | collective-permute-start | bytes 1572872 | tf_op jit(solution)/shard_map/ppermute | solution.py:367
  12.6 17.5 %conditional.1 = (bf16[64,1024]{1,0:T(8,128)(2,1)S(1)}) conditional(s32[]{:T(128)} %convert_element_type.3, () %tuple.14, bf16[64,1024]{1,0:T(8,128)(2,1)} %get-tuple-element.40), branch_computations={%region_0.0_spmd, %region_1.0_spmd} | conditional | bytes 262152 | solution.py:384
  12.6 17.5 %all_to_all.35 = bf16[8,8,1024]{2,1,0:T(8,128)(2,1)S(1)} all-to-all(bf16[8,8,1024]{2,1,0:T(8,128)(2,1)} %bitcast.33), channel_id=1, replica_groups=mesh['x'=4,'z'=8,'y'=4,'dp'=2] {'z'}, dimensions={0} | all-to-all | bytes 262144 | tf_op jit(solution)/shard_map/cond/branch_1_fun/all_to_all | solution.py:380
  30.1 0.4 collective-permute-start.2
  30.6 2.6 %collective-permute-start.1 = (bf16[64,1024]{1,0:T(8,128)(2,1)S(1)}, bf16[64,1024]{1,0:T(8,128)(2,1)S(1)}, u32[]{:S(2)}, u32[]{:S(2)}) collective-permute-start(bf16[64,1024]{1,0:T(8,128)(2,1)S(1)} %get-tuple-element.66.refs_0_), channel_id=1, source_target_pairs={{0,4},{1,129},{2,6},{3,131},{4,0},{5,133},{6,2},{7,135},{8,12},{9,... | collective-permute-start | bytes 393224 | tf_op jit(solution)/shard_map/ppermute | solution.py:367
  33.1 0.0 collective-permute-done.3.refs_1_
  33.1 1.9 %collective-permute-start = (bf16[64,1024]{1,0:T(8,128)(2,1)S(1)}, bf16[64,1024]{1,0:T(8,128)(2,1)S(1)}, u32[]{:S(2)}, u32[]{:S(2)}) collective-permute-start(bf16[64,1024]{1,0:T(8,128)(2,1)S(1)} %get-tuple-element.66.refs_0_), channel_id=1, source_target_pairs={{0,2},{1,65},{2,4},{3,67},{4,6},{5,69},{6,0},{7,71},{8,10},{9,73},... | collective-permute-start | bytes 393224 | tf_op jit(solution)/shard_map/ppermute | solution.py:367
  35.0 0.0 collective-permute-done.4.refs_2_
  35.0 0.0 collective-permute-done.5.refs_3_
  35.0 0.3 fold.1
  35.3 0.1 collective-permute-start.9
  35.4 2.2 %collective-permute-start.10 = (bf16[64,1024]{1,0:T(8,128)(2,1)S(1)}, bf16[64,1024]{1,0:T(8,128)(2,1)S(1)}, u32[]{:S(2)}, u32[]{:S(2)}) collective-permute-start(bf16[64,1024]{1,0:T(8,128)(2,1)S(1)} %get-tuple-element.54), channel_id=1, source_target_pairs={{0,4},{1,129},{2,6},{3,131},{4,0},{5,133},{6,2},{7,135},{8,12},{9,... | collective-permute-start | bytes 393224 | tf_op jit(solution)/shard_map/ppermute | solution.py:367
  37.6 0.0 collective-permute-done.2.refs_3_
  37.6 1.7 %collective-permute-start.11 = (bf16[64,1024]{1,0:T(8,128)(2,1)S(1)}, bf16[64,1024]{1,0:T(8,128)(2,1)S(1)}, u32[]{:S(2)}, u32[]{:S(2)}) collective-permute-start(bf16[64,1024]{1,0:T(8,128)(2,1)S(1)} %get-tuple-element.55), channel_id=1, source_target_pairs={{0,6},{1,193},{2,0},{3,195},{4,2},{5,197},{6,4},{7,199},{8,14},{9,... | collective-permute-start | bytes 393224 | tf_op jit(solution)/shard_map/ppermute | solution.py:367
  39.3 0.0 collective-permute-done.1.refs_2_
  39.3 0.0 collective-permute-done.refs_1_
  39.3 0.1 arrange.1.r0_ref
  39.4 1.4 %collective-permute-start.8 = (bf16[256,1024]{1,0:T(8,128)(2,1)S(1)}, bf16[256,1024]{1,0:T(8,128)(2,1)S(1)}, u32[]{:S(2)}, u32[]{:S(2)}) collective-permute-start(bf16[256,1024]{1,0:T(8,128)(2,1)S(1)} %arrange.1.r0_ref), channel_id=1, source_target_pairs={{0,192},{1,7},{2,194},{3,1},{4,196},{5,3},{6,198},{7,5},{8,200},{9... | collective-permute-start | bytes 1572872 | tf_op jit(solution)/shard_map/ppermute | solution.py:367
  40.9 1.3 %collective-permute-start.7 = (bf16[256,1024]{1,0:T(8,128)(2,1)S(1)}, bf16[256,1024]{1,0:T(8,128)(2,1)S(1)}, u32[]{:S(2)}, u32[]{:S(2)}) collective-permute-start(bf16[256,1024]{1,0:T(8,128)(2,1)S(1)} %arrange.1.r0_ref), channel_id=1, source_target_pairs={{0,128},{1,5},{2,130},{3,7},{4,132},{5,1},{6,134},{7,3},{8,136},{9... | collective-permute-start | bytes 1572872 | tf_op jit(solution)/shard_map/ppermute | solution.py:367
  42.2 0.0 collective-permute-done.9.refs_1_
  42.2 0.4 collective-permute-start.6
  42.6 0.9 collective-permute-done.10.refs_2_
  43.5 1.7 %collective-permute-done.11.refs_3_ = bf16[64,1024]{1,0:T(8,128)(2,1)S(1)} collective-permute-done((bf16[64,1024]{1,0:T(8,128)(2,1)S(1)}, bf16[64,1024]{1,0:T(8,128)(2,1)S(1)}, u32[]{:S(2)}, u32[]{:S(2)}) %collective-permute-start.11) | collective-permute-done | bytes 131104 | tf_op jit(solution)/shard_map/ppermute | solution.py:367
  45.1 0.8 add.1
  45.9 3.6 %all-to-all-start.1 = ((f32[8,8,1024]{2,1,0:T(8,128)}), f32[8,8,1024]{2,1,0:T(8,128)S(1)}, u32[]{:S(2)}, u32[]{:S(2)}) async-start(f32[8,8,1024]{2,1,0:T(8,128)} %bitcast.10), calls=%async_computation.1 | async-start | bytes 524288 | tf_op jit(solution)/shard_map/all_to_all | solution.py:380
  49.5 0.0 collective-permute-done.8.r3_ref.re_ref
  49.5 0.0 copy-start.6
  49.5 2.5 %early.1.u_ref = f32[1040,1024]{1,0:T(8,128)S(1)} custom-call(bf16[256,1024]{1,0:T(8,128)(2,1)S(1)} %arrange.1.r0_ref, bf16[256,1024]{1,0:T(8,128)(2,1)S(1)} %collective-permute-done.8.r3_ref.re_ref, bf16[8,1024,128]{2,1,0:T(8,128)(2,1)} %get-tuple-element.47.g_hbm), custom_call_target="tpu_custom_call" | custom-call | tf_op jit(solution)/shard_map/early/pallas_call | solution.py:426
  52.1 0.0 collective-permute-done.7.r2_ref.rb_ref
  52.1 5.1 %collective-permute-done.6.r1_ref.ra_ref = bf16[256,1024]{1,0:T(8,128)(2,1)S(1)} collective-permute-done((bf16[256,1024]{1,0:T(8,128)(2,1)S(1)}, bf16[256,1024]{1,0:T(8,128)(2,1)S(1)}, u32[]{:S(2)}, u32[]{:S(2)}) %collective-permute-start.6) | collective-permute-done | bytes 524320 | tf_op jit(solution)/shard_map/ppermute | solution.py:367
  57.2 0.0 copy-done.6
  57.2 0.0 copy-start
  57.2 0.0 copy-start.1
  57.2 0.0 copy-start.2
  57.2 0.0 copy-start.3
  57.2 0.0 copy-start.4
  57.2 4.4 %second.1 = (f32[256,32]{1,0:T(8,128)S(1)}, bf16[32,32,128]{2,1,0:T(8,128)(2,1)}, f32[1,128]{1,0:T(1,128)S(1)}) custom-call(bf16[256,1024]{1,0:T(8,128)(2,1)S(1)} %collective-permute-done.6.r1_ref.ra_ref, bf16[256,1024]{1,0:T(8,128)(2,1)S(1)} %collective-permute-done.7.r2_ref.rb_ref, f32[1040,1024]{1,0:T(8,128)S(1)} %early.1.u_ref, ...), custom_call_target="tpu_custom_call" | custom-call | flops 99999997952 | tf_op jit(solution)/shard_map/second/pallas_call | solution.py:434
  61.6 0.0 copy-start.5
  61.6 0.0 all-to-all-done.1
  61.6 0.0 copy-done
  61.6 0.0 copy-done.1
  61.6 0.0 copy-done.2
  61.6 0.0 copy-done.3
  61.6 0.0 copy-done.4
  61.7 2.9 %third.1 = (f32[256,256]{1,0:T(8,128)}, bf16[16,96,128]{2,1,0:T(8,128)(2,1)S(1)}) custom-call(f32[256,32]{1,0:T(8,128)S(1)} %get-tuple-element.50.left_grad_ref, bf16[32,32,128]{2,1,0:T(8,128)(2,1)} %get-tuple-element.51.w_hbm, f32[1,128]{1,0:T(1,128)S(1)} %get-tuple-element.52.bias_grad_ref, bf16[256,256]{1,0:T(8,128)(2,1)S(1)} %bitcast.23, ...), custom_call_target="tpu_custom_call" | custom-call | tf_op jit(solution)/shard_map/third/pallas_call | solution.py:445
  64.6 12.1 %all_to_all.36.in_ref = bf16[16,96,128]{2,1,0:T(8,128)(2,1)S(1)} all-to-all(bf16[16,96,128]{2,1,0:T(8,128)(2,1)S(1)} %get-tuple-element.57), channel_id=1, replica_groups=mesh['x'=4,'z'=8,'y'=4,'dp'=2] {'x','y'}, dimensions={0} | all-to-all | bytes 786432 | tf_op jit(solution)/shard_map/all_to_all | solution.py:380
  76.7 0.1 sum.1
  76.7 12.8 %all_to_all.37.in_ref = bf16[8,96,128]{2,1,0:T(8,128)(2,1)S(1)} all-to-all(bf16[8,96,128]{2,1,0:T(8,128)(2,1)S(1)} %sum.1), channel_id=1, replica_groups=mesh['x'=4,'z'=8,'y'=4,'dp'=2] {'z'}, dimensions={0} | all-to-all | bytes 393216 | tf_op jit(solution)/shard_map/all_to_all | solution.py:380
  89.6 0.8 spread.1
  90.3 5.3 %all-to-all-start.4 = ((bf16[16,96,128]{2,1,0:T(8,128)(2,1)}), bf16[16,96,128]{2,1,0:T(8,128)(2,1)S(1)}, u32[]{:S(2)}, u32[]{:S(2)}) async-start(bf16[16,96,128]{2,1,0:T(8,128)(2,1)} %spread.1), calls=%async_computation.4 | async-start | bytes 786432 | tf_op jit(solution)/shard_map/all_to_all | solution.py:380
  95.7 0.0 copy-done.5
  95.7 5.4 %update.1 = bf16[8,1024,128]{2,1,0:T(8,128)(2,1)} custom-call(bf16[256,1024]{1,0:T(8,128)(2,1)S(1)} %arrange.1.r0_ref, bf16[256,1024]{1,0:T(8,128)(2,1)S(1)} %collective-permute-done.6.r1_ref.ra_ref, bf16[256,1024]{1,0:T(8,128)(2,1)S(1)} %collective-permute-done.7.r2_ref.rb_ref, bf16[256,1024]{1,0:T(8,128)(2,1)S(1)} %collective-permute-done.8.r3_ref.re_ref, ...), custom_call_target="tpu_custom_call" | custom-call | tf_op jit(solution)/shard_map/update/pallas_call | solution.py:454
  101.1 2.1 %all-to-all-done.4.in_ref = bf16[16,96,128]{2,1,0:T(8,128)(2,1)S(1)} async-done(((bf16[16,96,128]{2,1,0:T(8,128)(2,1)}), bf16[16,96,128]{2,1,0:T(8,128)(2,1)S(1)}, u32[]{:S(2)}, u32[]{:S(2)}) %all-to-all-start.4) | async-done | bytes 393248 | tf_op jit(solution)/shard_map/all_to_all | solution.py:380
  103.2 1.2 %last.1 = (f32[1,256]{1,0:T(1,128)}, f32[1,256]{1,0:T(1,128)}, f32[32,256]{1,0:T(8,128)}, f32[1,32]{1,0:T(1,128)}, f32[32,256]{1,0:T(8,128)}, /*index=5*/f32[1,3...) custom-call(bf16[16,96,128]{2,1,0:T(8,128)(2,1)S(1)} %all-to-all-done.4.in_ref), custom_call_target="tpu_custom_call" | custom-call | tf_op jit(solution)/shard_map/last/pallas_call | solution.py:468
Async XLA Ops:
  6.8 26.3 %collective-permute-start.3 = (bf16[256,1024]{1,0:T(8,128)(2,1)}, bf16[256,1024]{1,0:T(8,128)(2,1)S(1)}, u32[]{:S(2)}, u32[]{:S(2)}) collective-permute-start(bf16[256,1024]{1,0:T(8,128)(2,1)} %get-tuple-element.42), channel_id=1, source_target_pairs={{0,64},{1,3},{2,66},{3,5},{4,68},{5,7},{6,70},{7,1},{8,72},{9,11},... | collective-permute-start | bytes 1572872 | tf_op jit(solution)/shard_map/ppermute | solution.py:367
  8.4 26.6 %collective-permute-start.4 = (bf16[256,1024]{1,0:T(8,128)(2,1)S(1)}, bf16[256,1024]{1,0:T(8,128)(2,1)S(1)}, u32[]{:S(2)}, u32[]{:S(2)}) collective-permute-start(bf16[256,1024]{1,0:T(8,128)(2,1)S(1)} %get-tuple-element.43), channel_id=1, source_target_pairs={{0,128},{1,5},{2,130},{3,7},{4,132},{5,1},{6,134},{7,3},{8,136},{9... | collective-permute-start | bytes 1572872 | tf_op jit(solution)/shard_map/ppermute | solution.py:367
  11.1 23.9 %collective-permute-start.5 = (bf16[256,1024]{1,0:T(8,128)(2,1)S(1)}, bf16[256,1024]{1,0:T(8,128)(2,1)S(1)}, u32[]{:S(2)}, u32[]{:S(2)}) collective-permute-start(bf16[256,1024]{1,0:T(8,128)(2,1)S(1)} %get-tuple-element.44), channel_id=1, source_target_pairs={{0,192},{1,7},{2,194},{3,1},{4,196},{5,3},{6,198},{7,5},{8,200},{9... | collective-permute-start | bytes 1572872 | tf_op jit(solution)/shard_map/ppermute | solution.py:367
  30.1 7.5 %collective-permute-start.2 = (bf16[64,1024]{1,0:T(8,128)(2,1)S(1)}, bf16[64,1024]{1,0:T(8,128)(2,1)S(1)}, u32[]{:S(2)}, u32[]{:S(2)}) collective-permute-start(bf16[64,1024]{1,0:T(8,128)(2,1)S(1)} %get-tuple-element.66.refs_0_), channel_id=1, source_target_pairs={{0,6},{1,193},{2,0},{3,195},{4,2},{5,197},{6,4},{7,199},{8,14},{9,... | collective-permute-start | bytes 393224 | tf_op jit(solution)/shard_map/ppermute | solution.py:367
  30.6 8.7 %collective-permute-start.1 = (bf16[64,1024]{1,0:T(8,128)(2,1)S(1)}, bf16[64,1024]{1,0:T(8,128)(2,1)S(1)}, u32[]{:S(2)}, u32[]{:S(2)}) collective-permute-start(bf16[64,1024]{1,0:T(8,128)(2,1)S(1)} %get-tuple-element.66.refs_0_), channel_id=1, source_target_pairs={{0,4},{1,129},{2,6},{3,131},{4,0},{5,133},{6,2},{7,135},{8,12},{9,... | collective-permute-start | bytes 393224 | tf_op jit(solution)/shard_map/ppermute | solution.py:367
  33.1 6.1 %collective-permute-start = (bf16[64,1024]{1,0:T(8,128)(2,1)S(1)}, bf16[64,1024]{1,0:T(8,128)(2,1)S(1)}, u32[]{:S(2)}, u32[]{:S(2)}) collective-permute-start(bf16[64,1024]{1,0:T(8,128)(2,1)S(1)} %get-tuple-element.66.refs_0_), channel_id=1, source_target_pairs={{0,2},{1,65},{2,4},{3,67},{4,6},{5,69},{6,0},{7,71},{8,10},{9,73},... | collective-permute-start | bytes 393224 | tf_op jit(solution)/shard_map/ppermute | solution.py:367
  35.3 6.8 %collective-permute-start.9 = (bf16[64,1024]{1,0:T(8,128)(2,1)S(1)}, bf16[64,1024]{1,0:T(8,128)(2,1)S(1)}, u32[]{:S(2)}, u32[]{:S(2)}) collective-permute-start(bf16[64,1024]{1,0:T(8,128)(2,1)S(1)} %get-tuple-element.53), channel_id=1, source_target_pairs={{0,2},{1,65},{2,4},{3,67},{4,6},{5,69},{6,0},{7,71},{8,10},{9,73},... | collective-permute-start | bytes 393224 | tf_op jit(solution)/shard_map/ppermute | solution.py:367
  35.4 8.0 %collective-permute-start.10 = (bf16[64,1024]{1,0:T(8,128)(2,1)S(1)}, bf16[64,1024]{1,0:T(8,128)(2,1)S(1)}, u32[]{:S(2)}, u32[]{:S(2)}) collective-permute-start(bf16[64,1024]{1,0:T(8,128)(2,1)S(1)} %get-tuple-element.54), channel_id=1, source_target_pairs={{0,4},{1,129},{2,6},{3,131},{4,0},{5,133},{6,2},{7,135},{8,12},{9,... | collective-permute-start | bytes 393224 | tf_op jit(solution)/shard_map/ppermute | solution.py:367
  37.6 7.5 %collective-permute-start.11 = (bf16[64,1024]{1,0:T(8,128)(2,1)S(1)}, bf16[64,1024]{1,0:T(8,128)(2,1)S(1)}, u32[]{:S(2)}, u32[]{:S(2)}) collective-permute-start(bf16[64,1024]{1,0:T(8,128)(2,1)S(1)} %get-tuple-element.55), channel_id=1, source_target_pairs={{0,6},{1,193},{2,0},{3,195},{4,2},{5,197},{6,4},{7,199},{8,14},{9,... | collective-permute-start | bytes 393224 | tf_op jit(solution)/shard_map/ppermute | solution.py:367
  39.4 10.1 %collective-permute-start.8 = (bf16[256,1024]{1,0:T(8,128)(2,1)S(1)}, bf16[256,1024]{1,0:T(8,128)(2,1)S(1)}, u32[]{:S(2)}, u32[]{:S(2)}) collective-permute-start(bf16[256,1024]{1,0:T(8,128)(2,1)S(1)} %arrange.1.r0_ref), channel_id=1, source_target_pairs={{0,192},{1,7},{2,194},{3,1},{4,196},{5,3},{6,198},{7,5},{8,200},{9... | collective-permute-start | bytes 1572872 | tf_op jit(solution)/shard_map/ppermute | solution.py:367
  40.9 11.2 %collective-permute-start.7 = (bf16[256,1024]{1,0:T(8,128)(2,1)S(1)}, bf16[256,1024]{1,0:T(8,128)(2,1)S(1)}, u32[]{:S(2)}, u32[]{:S(2)}) collective-permute-start(bf16[256,1024]{1,0:T(8,128)(2,1)S(1)} %arrange.1.r0_ref), channel_id=1, source_target_pairs={{0,128},{1,5},{2,130},{3,7},{4,132},{5,1},{6,134},{7,3},{8,136},{9... | collective-permute-start | bytes 1572872 | tf_op jit(solution)/shard_map/ppermute | solution.py:367
  42.2 15.0 %collective-permute-start.6 = (bf16[256,1024]{1,0:T(8,128)(2,1)S(1)}, bf16[256,1024]{1,0:T(8,128)(2,1)S(1)}, u32[]{:S(2)}, u32[]{:S(2)}) collective-permute-start(bf16[256,1024]{1,0:T(8,128)(2,1)S(1)} %arrange.1.r0_ref), channel_id=1, source_target_pairs={{0,64},{1,3},{2,66},{3,5},{4,68},{5,7},{6,70},{7,1},{8,72},{9,11},... | collective-permute-start | bytes 1572872 | tf_op jit(solution)/shard_map/ppermute | solution.py:367
  45.9 15.7 %all-to-all-start.1 = ((f32[8,8,1024]{2,1,0:T(8,128)}), f32[8,8,1024]{2,1,0:T(8,128)S(1)}, u32[]{:S(2)}, u32[]{:S(2)}) async-start(f32[8,8,1024]{2,1,0:T(8,128)} %bitcast.10), calls=%async_computation.1 | async-start | bytes 524288 | tf_op jit(solution)/shard_map/all_to_all | solution.py:380
  49.5 7.7 %copy-start.6 = (bf16[256,32]{1,0:T(8,128)(2,1)S(1)}, bf16[256,32]{1,0:T(8,128)(2,1)}, u32[]{:S(2)}) copy-start(bf16[256,32]{1,0:T(8,128)(2,1)} %get-tuple-element.49.left_ref) | copy-start | bytes 49156
  57.2 4.4 %copy-start = (bf16[32,8,256]{2,1,0:T(8,128)(2,1)S(1)}, bf16[32,8,256]{2,1,0:T(8,128)(2,1)}, u32[]{:S(2)}) copy-start(bf16[32,8,256]{2,1,0:T(8,128)(2,1)} %param.12) | copy-start | bytes 393220
  57.2 4.4 %copy-start.1 = (bf16[256,32]{0,1:T(8,128)(2,1)S(1)}, bf16[256,32]{0,1:T(8,128)(2,1)}, u32[]{:S(2)}) copy-start(bf16[256,32]{0,1:T(8,128)(2,1)} %param.15) | copy-start | bytes 49156
  57.2 4.5 %copy-start.2 = (bf16[256,32]{0,1:T(8,128)(2,1)S(1)}, bf16[256,32]{0,1:T(8,128)(2,1)}, u32[]{:S(2)}) copy-start(bf16[256,32]{0,1:T(8,128)(2,1)} %param.17) | copy-start | bytes 49156
  57.2 4.5 %copy-start.3 = (f32[256]{0:T(256)S(1)}, f32[256]{0:T(256)}, u32[]{:S(2)}) copy-start(f32[256]{0:T(256)} %param.13) | copy-start | bytes 3076
  57.2 4.5 %copy-start.4 = (f32[256]{0:T(256)S(1)}, f32[256]{0:T(256)}, u32[]{:S(2)}) copy-start(f32[256]{0:T(256)} %param.14) | copy-start | bytes 3076
  61.6 34.1 %copy-start.5 = (f32[128]{0:T(128)S(1)}, f32[128]{0:T(128)}, u32[]{:S(2)}) copy-start(f32[128]{0:T(128)} %param.20) | copy-start | bytes 1540
  90.3 12.9 %all-to-all-start.4 = ((bf16[16,96,128]{2,1,0:T(8,128)(2,1)}), bf16[16,96,128]{2,1,0:T(8,128)(2,1)S(1)}, u32[]{:S(2)}, u32[]{:S(2)}) async-start(bf16[16,96,128]{2,1,0:T(8,128)(2,1)} %spread.1), calls=%async_computation.4 | async-start | bytes 786432 | tf_op jit(solution)/shard_map/all_to_all | solution.py:380

commit v6 on v5

--- a/solution.py
+++ b/solution.py
@@ -223,8 +223,8 @@
 
 def second_kernel(
     ra_ref, rb_ref, u_ref, g_hbm, wd_hbm, left_ref,
-    left_grad_ref, w_part_ref, bias_grad_ref,
-    g_ref, wd_ref, rt_scratch, m_scratch, sem, wd_sem,
+    left_grad_ref, w_part_hbm, bias_grad_ref,
+    g_ref, wd_ref, w_part_ref, rt_scratch, m_scratch, sem, wd_sem, w_sem,
 ):
     load = pltpu.make_async_copy(wd_hbm, wd_ref, wd_sem)
     load.start()
@@ -243,16 +243,19 @@
     half_product(LATER, (ra_ref, rb_ref), g_hbm, g_ref, rt_scratch, sem, finish)
     bias_grad = sum(bias_grad)
     bias_grad_ref[...] = bias_grad
-    load.wait()
-    left_grad_ref[...] = dot(m_scratch[...], wd_ref[...], NT) * SCALE
     w_part = dot(left_ref[...], m_scratch[...], TN) * SCALE
     for d in range(C):
         w_part_ref[d] = w_part[:, d * Z : (d + 1) * Z].astype(BF16)
+    store = pltpu.make_async_copy(w_part_ref, w_part_hbm, w_sem)
+    store.start()
+    load.wait()
+    left_grad_ref[...] = dot(m_scratch[...], wd_ref[...], NT) * SCALE
+    store.wait()
 
 
 def third_kernel(
     left_grad_ref, w_hbm, bias_grad_ref, x_ref, gain_ref, shift_ref, k1_ref, k2_ref, pieces_ref,
-    align_ref, pack_ref, w_ref, sem,
+    align_hbm, pack_ref, w_ref, align_ref, sem, align_sem,
 ):
     load = pltpu.make_async_copy(w_hbm, w_ref, sem)
     load.start()
@@ -283,6 +286,8 @@
     mean_one = jnp.mean(unit_grad, axis=-1, keepdims=True)
     mean_two = jnp.mean(unit_grad * unit, axis=-1, keepdims=True)
     align_ref[...] = inverse * (unit_grad - mean_one - unit * mean_two)
+    store = pltpu.make_async_copy(align_ref, align_hbm, align_sem)
+    store.start()
     gain_grad = jnp.sum(normed_grad * unit, axis=0, keepdims=True)
     offset_grad = jnp.sum(normed_grad, axis=0, keepdims=True)
     both = jnp.concatenate([lg_high, rg_high, lg_low, rg_low], axis=1)
@@ -297,6 +302,7 @@
     small = jnp.concatenate([weights.reshape(NP, 8, Z), rest], axis=1)
     load.wait()
     pack_ref[...] = packed(w_ref[...].astype(F32).reshape(NP, WR, Z), small)
+    store.wait()
 
 
 def packed(w_rows, small):
@@ -380,10 +386,6 @@
     return lax.all_to_all(array, axes, 0, 0, tiled=True)
 
 
-def blocking_exchange(array, axes):
-    return lax.cond(lax.axis_index("x") < NX, lambda v: exchange(v, axes), jnp.zeros_like, array)
-
-
 def per_device(x, gain, shift, k1, b1, k2, b2, w, bias, g):
     gain, shift, b1, b2, bias = [v.reshape(1, -1) for v in (gain, shift, b1, b2, bias)]
     x, k1, k2 = x.reshape(S * I, H), k1.T, k2.T
@@ -410,7 +412,7 @@
     quarter = ((Q, C * S), BF16)
     column = ((G, C * S), BF16)
     planes = shifted((p0, p1, p2, p3), True)
-    near = blocking_exchange(copies, "z")
+    near = exchange(copies, "z")
     lines = shifted([near] * NY, False)
     parts = call(
         fold_kernel, "fold", 8, (pltpu.VMEM(*column),) * NY, [pltpu.VMEM((Q, C * S), F32)]
@@ -436,18 +438,21 @@
         "second",
         16,
         (shape((I * S, C), F32), pltpu.HBM((C, C, Z), BF16), shape((1, Z), F32)),
-        [pltpu.VMEM((I, HALF, Z), BF16), pltpu.VMEM(wd.shape, BF16)]
+        [pltpu.VMEM((I, HALF, Z), BF16), pltpu.VMEM(wd.shape, BF16), pltpu.VMEM((C, C, Z), BF16)]
         + [pltpu.VMEM(*rt_type), pltpu.VMEM((I * S, C * Z), BF16)]
-        + [pltpu.SemaphoreType.DMA((2,)), pltpu.SemaphoreType.DMA],
+        + [pltpu.SemaphoreType.DMA((2,)), pltpu.SemaphoreType.DMA, pltpu.SemaphoreType.DMA],
         in_specs=[VMEM] * 3 + [HBM] * 2 + [VMEM],
+        out_specs=[VMEM, HBM, VMEM],
         cost_estimate=LATE,
     )(*[rights[k] for k in LATER], *in_vmem(half), in_hbm(ordered), in_hbm(wd), left)
     align, pack = call(
         third_kernel,
         "third",
         12,
-        (shape((S * I, H), F32), shape((NP, WR + 32, Z), BF16)),
-        [pltpu.VMEM((C, C, Z), BF16), pltpu.SemaphoreType.DMA],
+        (pltpu.HBM((S * I, H), F32), shape((NP, WR + 32, Z), BF16)),
+        [pltpu.VMEM((C, C, Z), BF16), pltpu.VMEM((S * I, H), F32)]
+        + [pltpu.SemaphoreType.DMA, pltpu.SemaphoreType.DMA],
+        out_specs=[HBM, VMEM],
         in_specs=[VMEM, HBM] + [VMEM] * 7,
     )(left_grad, in_hbm(w_part), bias_grad, x, gain, shift, k1, k2, pieces)
     parts = exchange(pack, ("x", "y"))

time: 105 us -> 104 us (level)
  Pallas kernels: 24.6 us -> 23.5 us
where the time goes in v6:
time: 104 us; the launch traced here: 103 us
  blocking collectives  42.4 us (41%)
  starting transfers between devices  26.6 us (26%)
  Pallas kernels  23.5 us (23%)
  waiting for transfers between devices  9.85 us (9%)
    all_to_all x3, blocking collectives, exchange(): return lax.all_to_all(array, axes, 0, 0, tiled=True)  42.4 us
    ppermute x12, starting transfers between devices, shifted(): lax.ppermute(arrays[k], ('x', 'z', 'y', 'dp'), ring(k, long))  17.7 us
    all_to_all x2, starting transfers between devices, exchange(): return lax.all_to_all(array, axes, 0, 0, tiled=True)  8.93 us
    ppermute x12, waiting for transfers between devices, shifted(): lax.ppermute(arrays[k], ('x', 'z', 'y', 'dp'), ring(k, long))  7.71 us
    pallas_call x1, Pallas kernels, per_device(): call(first_kernel, 'first', 24, tuple((pltpu.HBM(*v) for v in made)) + (p...  5.39 us
    pallas_call x1, Pallas kernels, per_device(): call(update_kernel, 'update', 20, pltpu.HBM((I, J, Z), BF16), [pltpu.VMEM...  5.38 us
    pallas_call x1, Pallas kernels, per_device(): call(second_kernel, 'second', 16, (shape((I * S, C), F32), pltpu.HBM((C,...  4.77 us
    pallas_call x1, Pallas kernels, per_device(): call(early_kernel, 'early', 16, pltpu.VMEM((C * S + 16, I * Z), F32), [pl...  2.53 us
  transfers between devices with their start and end apart: 14, of which 4 were waited for; matrix products, arithmetic and copies ran while one was open for 0% of the time, Pallas kernels for 13%

profile of v6, /device:TPU:8, one launch (start us, length us, event | category | flops | bytes accessed | tf_op | source)
XLA Modules:
  0.0 103.3 jit_solution(10308186640072099425)
XLA Ops:
  0.6 5.4 %first.1 = (bf16[256,32]{1,0:T(8,128)(2,1)}, bf16[64,1024]{1,0:T(8,128)(2,1)}, bf16[32,4096]{1,0:T(8,128)(2,1)}, bf16[1024,1024]{1,0:T(8,128)(2,1)}, bf16[8,1024...) custom-call(bf16[256,256]{1,0:T(8,128)(2,1)} %bitcast.25, ...), custom_call_target="tpu_custom_call" | custom-call | tf_op jit(solution)/shard_map/first/pallas_call | solution.py:400
  6.0 1.6 %collective-permute-start.3 = (bf16[256,1024]{1,0:T(8,128)(2,1)S(1)}, bf16[256,1024]{1,0:T(8,128)(2,1)S(1)}, u32[]{:S(2)}, u32[]{:S(2)}) collective-permute-start(bf16[256,1024]{1,0:T(8,128)(2,1)S(1)} %get-tuple-element.38), channel_id=1, source_target_pairs={{0,64},{1,3},{2,66},{3,5},{4,68},{5,7},{6,70},{7,1},{8,72},{9,11},... | collective-permute-start | bytes 1572872 | tf_op jit(solution)/shard_map/ppermute | solution.py:373
  7.6 2.7 %collective-permute-start.4 = (bf16[256,1024]{1,0:T(8,128)(2,1)S(1)}, bf16[256,1024]{1,0:T(8,128)(2,1)S(1)}, u32[]{:S(2)}, u32[]{:S(2)}) collective-permute-start(bf16[256,1024]{1,0:T(8,128)(2,1)S(1)} %get-tuple-element.39), channel_id=1, source_target_pairs={{0,128},{1,5},{2,130},{3,7},{4,132},{5,1},{6,134},{7,3},{8,136},{9... | collective-permute-start | bytes 1572872 | tf_op jit(solution)/shard_map/ppermute | solution.py:373
  10.3 1.4 %collective-permute-start.5 = (bf16[256,1024]{1,0:T(8,128)(2,1)S(1)}, bf16[256,1024]{1,0:T(8,128)(2,1)S(1)}, u32[]{:S(2)}, u32[]{:S(2)}) collective-permute-start(bf16[256,1024]{1,0:T(8,128)(2,1)S(1)} %get-tuple-element.40), channel_id=1, source_target_pairs={{0,192},{1,7},{2,194},{3,1},{4,196},{5,3},{6,198},{7,5},{8,200},{9... | collective-permute-start | bytes 1572872 | tf_op jit(solution)/shard_map/ppermute | solution.py:373
  11.8 17.5 %all_to_all.37 = bf16[8,8,1024]{2,1,0:T(8,128)(2,1)S(1)} all-to-all(bf16[8,8,1024]{2,1,0:T(8,128)(2,1)} %bitcast.36), channel_id=1, replica_groups=mesh['x'=4,'z'=8,'y'=4,'dp'=2] {'z'}, dimensions={0} | all-to-all | bytes 262144 | tf_op jit(solution)/shard_map/all_to_all | solution.py:386
  29.3 0.4 collective-permute-start.2
  29.8 2.6 %collective-permute-start.1 = (bf16[64,1024]{1,0:T(8,128)(2,1)S(1)}, bf16[64,1024]{1,0:T(8,128)(2,1)S(1)}, u32[]{:S(2)}, u32[]{:S(2)}) collective-permute-start(bf16[64,1024]{1,0:T(8,128)(2,1)S(1)} %bitcast.22), channel_id=1, source_target_pairs={{0,4},{1,129},{2,6},{3,131},{4,0},{5,133},{6,2},{7,135},{8,12},{9,... | collective-permute-start | bytes 393224 | tf_op jit(solution)/shard_map/ppermute | solution.py:373
  32.4 0.0 collective-permute-done.3.refs_1_
  32.4 1.9 %collective-permute-start = (bf16[64,1024]{1,0:T(8,128)(2,1)S(1)}, bf16[64,1024]{1,0:T(8,128)(2,1)S(1)}, u32[]{:S(2)}, u32[]{:S(2)}) collective-permute-start(bf16[64,1024]{1,0:T(8,128)(2,1)S(1)} %bitcast.23), channel_id=1, source_target_pairs={{0,2},{1,65},{2,4},{3,67},{4,6},{5,69},{6,0},{7,71},{8,10},{9,73},... | collective-permute-start | bytes 393224 | tf_op jit(solution)/shard_map/ppermute | solution.py:373
  34.2 0.0 collective-permute-done.4.refs_2_
  34.2 0.0 collective-permute-done.5.refs_3_
  34.3 0.3 fold.1
  34.6 0.1 collective-permute-start.9
  34.6 2.2 %collective-permute-start.10 = (bf16[64,1024]{1,0:T(8,128)(2,1)S(1)}, bf16[64,1024]{1,0:T(8,128)(2,1)S(1)}, u32[]{:S(2)}, u32[]{:S(2)}) collective-permute-start(bf16[64,1024]{1,0:T(8,128)(2,1)S(1)} %get-tuple-element.50), channel_id=1, source_target_pairs={{0,4},{1,129},{2,6},{3,131},{4,0},{5,133},{6,2},{7,135},{8,12},{9,... | collective-permute-start | bytes 393224 | tf_op jit(solution)/shard_map/ppermute | solution.py:373
  36.8 0.0 collective-permute-done.2.refs_3_
  36.8 1.7 %collective-permute-start.11 = (bf16[64,1024]{1,0:T(8,128)(2,1)S(1)}, bf16[64,1024]{1,0:T(8,128)(2,1)S(1)}, u32[]{:S(2)}, u32[]{:S(2)}) collective-permute-start(bf16[64,1024]{1,0:T(8,128)(2,1)S(1)} %get-tuple-element.51), channel_id=1, source_target_pairs={{0,6},{1,193},{2,0},{3,195},{4,2},{5,197},{6,4},{7,199},{8,14},{9,... | collective-permute-start | bytes 393224 | tf_op jit(solution)/shard_map/ppermute | solution.py:373
  38.5 0.0 collective-permute-done.1.refs_2_
  38.5 0.0 collective-permute-done.refs_1_
  38.5 0.1 arrange.1.r0_ref
  38.7 1.4 %collective-permute-start.8 = (bf16[256,1024]{1,0:T(8,128)(2,1)S(1)}, bf16[256,1024]{1,0:T(8,128)(2,1)S(1)}, u32[]{:S(2)}, u32[]{:S(2)}) collective-permute-start(bf16[256,1024]{1,0:T(8,128)(2,1)S(1)} %arrange.1.r0_ref), channel_id=1, source_target_pairs={{0,192},{1,7},{2,194},{3,1},{4,196},{5,3},{6,198},{7,5},{8,200},{9... | collective-permute-start | bytes 1572872 | tf_op jit(solution)/shard_map/ppermute | solution.py:373
  40.1 1.3 %collective-permute-start.7 = (bf16[256,1024]{1,0:T(8,128)(2,1)S(1)}, bf16[256,1024]{1,0:T(8,128)(2,1)S(1)}, u32[]{:S(2)}, u32[]{:S(2)}) collective-permute-start(bf16[256,1024]{1,0:T(8,128)(2,1)S(1)} %arrange.1.r0_ref), channel_id=1, source_target_pairs={{0,128},{1,5},{2,130},{3,7},{4,132},{5,1},{6,134},{7,3},{8,136},{9... | collective-permute-start | bytes 1572872 | tf_op jit(solution)/shard_map/ppermute | solution.py:373
  41.4 0.0 collective-permute-done.9.refs_1_
  41.4 0.4 collective-permute-start.6
  41.8 0.9 collective-permute-done.10.refs_2_
  42.7 1.7 %collective-permute-done.11.refs_3_ = bf16[64,1024]{1,0:T(8,128)(2,1)S(1)} collective-permute-done((bf16[64,1024]{1,0:T(8,128)(2,1)S(1)}, bf16[64,1024]{1,0:T(8,128)(2,1)S(1)}, u32[]{:S(2)}, u32[]{:S(2)}) %collective-permute-start.11) | collective-permute-done | bytes 131104 | tf_op jit(solution)/shard_map/ppermute | solution.py:373
  44.3 0.8 add.1
  45.1 3.6 %all-to-all-start.1 = ((f32[8,8,1024]{2,1,0:T(8,128)}), f32[8,8,1024]{2,1,0:T(8,128)S(1)}, u32[]{:S(2)}, u32[]{:S(2)}) async-start(f32[8,8,1024]{2,1,0:T(8,128)} %bitcast.10), calls=%async_computation.1 | async-start | bytes 524288 | tf_op jit(solution)/shard_map/all_to_all | solution.py:386
  48.7 0.0 collective-permute-done.8.r3_ref.re_ref
  48.7 0.0 copy-start.6
  48.7 2.5 %early.1.u_ref = f32[1040,1024]{1,0:T(8,128)S(1)} custom-call(bf16[256,1024]{1,0:T(8,128)(2,1)S(1)} %arrange.1.r0_ref, bf16[256,1024]{1,0:T(8,128)(2,1)S(1)} %collective-permute-done.8.r3_ref.re_ref, bf16[8,1024,128]{2,1,0:T(8,128)(2,1)} %get-tuple-element.43.g_hbm), custom_call_target="tpu_custom_call" | custom-call | tf_op jit(solution)/shard_map/early/pallas_call | solution.py:428
  51.3 0.0 collective-permute-done.7.r2_ref.rb_ref
  51.3 5.1 %collective-permute-done.6.r1_ref.ra_ref = bf16[256,1024]{1,0:T(8,128)(2,1)S(1)} collective-permute-done((bf16[256,1024]{1,0:T(8,128)(2,1)S(1)}, bf16[256,1024]{1,0:T(8,128)(2,1)S(1)}, u32[]{:S(2)}, u32[]{:S(2)}) %collective-permute-start.6) | collective-permute-done | bytes 524320 | tf_op jit(solution)/shard_map/ppermute | solution.py:373
  56.4 0.0 copy-done.6
  56.4 0.0 copy-start
  56.4 0.0 copy-start.1
  56.4 0.0 copy-start.2
  56.4 0.0 copy-start.3
  56.4 0.0 copy-start.4
  56.4 4.8 %second.1 = (f32[256,32]{1,0:T(8,128)S(1)}, bf16[32,32,128]{2,1,0:T(8,128)(2,1)}, f32[1,128]{1,0:T(1,128)S(1)}) custom-call(bf16[256,1024]{1,0:T(8,128)(2,1)S(1)} %collective-permute-done.6.r1_ref.ra_ref, bf16[256,1024]{1,0:T(8,128)(2,1)S(1)} %collective-permute-done.7.r2_ref.rb_ref, f32[1040,1024]{1,0:T(8,128)S(1)} %early.1.u_ref, ...), custom_call_target="tpu_custom_call" | custom-call | flops 99999997952 | tf_op jit(solution)/shard_map/second/pallas_call | solution.py:436
  61.2 0.0 copy-start.5
  61.2 0.0 all-to-all-done.1
  61.2 0.0 copy-done
  61.2 0.0 copy-done.1
  61.2 0.0 copy-done.2
  61.2 0.0 copy-done.3
  61.2 0.0 copy-done.4
  61.3 2.3 %third.1 = (f32[256,256]{1,0:T(8,128)}, bf16[16,96,128]{2,1,0:T(8,128)(2,1)S(1)}) custom-call(f32[256,32]{1,0:T(8,128)S(1)} %get-tuple-element.46.left_grad_ref, bf16[32,32,128]{2,1,0:T(8,128)(2,1)} %get-tuple-element.47.w_hbm, f32[1,128]{1,0:T(1,128)S(1)} %get-tuple-element.48.bias_grad_ref, bf16[256,256]{1,0:T(8,128)(2,1)S(1)} %bitcast.26, ...), custom_call_target="tpu_custom_call" | custom-call | tf_op jit(solution)/shard_map/third/pallas_call | solution.py:448
  63.5 12.1 %all_to_all.38.in_ref = bf16[16,96,128]{2,1,0:T(8,128)(2,1)S(1)} all-to-all(bf16[16,96,128]{2,1,0:T(8,128)(2,1)S(1)} %get-tuple-element.53), channel_id=1, replica_groups=mesh['x'=4,'z'=8,'y'=4,'dp'=2] {'x','y'}, dimensions={0} | all-to-all | bytes 786432 | tf_op jit(solution)/shard_map/all_to_all | solution.py:386
  75.7 0.1 sum.1
  75.7 12.8 %all_to_all.39.in_ref = bf16[8,96,128]{2,1,0:T(8,128)(2,1)S(1)} all-to-all(bf16[8,96,128]{2,1,0:T(8,128)(2,1)S(1)} %sum.1), channel_id=1, replica_groups=mesh['x'=4,'z'=8,'y'=4,'dp'=2] {'z'}, dimensions={0} | all-to-all | bytes 393216 | tf_op jit(solution)/shard_map/all_to_all | solution.py:386
  88.5 0.8 spread.1
  89.3 5.3 %all-to-all-start.4 = ((bf16[16,96,128]{2,1,0:T(8,128)(2,1)}), bf16[16,96,128]{2,1,0:T(8,128)(2,1)S(1)}, u32[]{:S(2)}, u32[]{:S(2)}) async-start(bf16[16,96,128]{2,1,0:T(8,128)(2,1)} %spread.1), calls=%async_computation.4 | async-start | bytes 786432 | tf_op jit(solution)/shard_map/all_to_all | solution.py:386
  94.6 0.0 copy-done.5
  94.6 5.4 %update.1 = bf16[8,1024,128]{2,1,0:T(8,128)(2,1)} custom-call(bf16[256,1024]{1,0:T(8,128)(2,1)S(1)} %arrange.1.r0_ref, bf16[256,1024]{1,0:T(8,128)(2,1)S(1)} %collective-permute-done.6.r1_ref.ra_ref, bf16[256,1024]{1,0:T(8,128)(2,1)S(1)} %collective-permute-done.7.r2_ref.rb_ref, bf16[256,1024]{1,0:T(8,128)(2,1)S(1)} %collective-permute-done.8.r3_ref.re_ref, ...), custom_call_target="tpu_custom_call" | custom-call | tf_op jit(solution)/shard_map/update/pallas_call | solution.py:459
  100.0 2.1 %all-to-all-done.4.in_ref = bf16[16,96,128]{2,1,0:T(8,128)(2,1)S(1)} async-done(((bf16[16,96,128]{2,1,0:T(8,128)(2,1)}), bf16[16,96,128]{2,1,0:T(8,128)(2,1)S(1)}, u32[]{:S(2)}, u32[]{:S(2)}) %all-to-all-start.4) | async-done | bytes 393248 | tf_op jit(solution)/shard_map/all_to_all | solution.py:386
  102.2 1.2 %last.1 = (f32[1,256]{1,0:T(1,128)}, f32[1,256]{1,0:T(1,128)}, f32[32,256]{1,0:T(8,128)}, f32[1,32]{1,0:T(1,128)}, f32[32,256]{1,0:T(8,128)}, /*index=5*/f32[1,3...) custom-call(bf16[16,96,128]{2,1,0:T(8,128)(2,1)S(1)} %all-to-all-done.4.in_ref), custom_call_target="tpu_custom_call" | custom-call | tf_op jit(solution)/shard_map/last/pallas_call | solution.py:473
Async XLA Ops:
  6.0 26.3 %collective-permute-start.3 = (bf16[256,1024]{1,0:T(8,128)(2,1)S(1)}, bf16[256,1024]{1,0:T(8,128)(2,1)S(1)}, u32[]{:S(2)}, u32[]{:S(2)}) collective-permute-start(bf16[256,1024]{1,0:T(8,128)(2,1)S(1)} %get-tuple-element.38), channel_id=1, source_target_pairs={{0,64},{1,3},{2,66},{3,5},{4,68},{5,7},{6,70},{7,1},{8,72},{9,11},... | collective-permute-start | bytes 1572872 | tf_op jit(solution)/shard_map/ppermute | solution.py:373
  7.6 26.6 %collective-permute-start.4 = (bf16[256,1024]{1,0:T(8,128)(2,1)S(1)}, bf16[256,1024]{1,0:T(8,128)(2,1)S(1)}, u32[]{:S(2)}, u32[]{:S(2)}) collective-permute-start(bf16[256,1024]{1,0:T(8,128)(2,1)S(1)} %get-tuple-element.39), channel_id=1, source_target_pairs={{0,128},{1,5},{2,130},{3,7},{4,132},{5,1},{6,134},{7,3},{8,136},{9... | collective-permute-start | bytes 1572872 | tf_op jit(solution)/shard_map/ppermute | solution.py:373
  10.3 23.9 %collective-permute-start.5 = (bf16[256,1024]{1,0:T(8,128)(2,1)S(1)}, bf16[256,1024]{1,0:T(8,128)(2,1)S(1)}, u32[]{:S(2)}, u32[]{:S(2)}) collective-permute-start(bf16[256,1024]{1,0:T(8,128)(2,1)S(1)} %get-tuple-element.40), channel_id=1, source_target_pairs={{0,192},{1,7},{2,194},{3,1},{4,196},{5,3},{6,198},{7,5},{8,200},{9... | collective-permute-start | bytes 1572872 | tf_op jit(solution)/shard_map/ppermute | solution.py:373
  29.3 7.5 %collective-permute-start.2 = (bf16[64,1024]{1,0:T(8,128)(2,1)S(1)}, bf16[64,1024]{1,0:T(8,128)(2,1)S(1)}, u32[]{:S(2)}, u32[]{:S(2)}) collective-permute-start(bf16[64,1024]{1,0:T(8,128)(2,1)S(1)} %bitcast.21), channel_id=1, source_target_pairs={{0,6},{1,193},{2,0},{3,195},{4,2},{5,197},{6,4},{7,199},{8,14},{9,... | collective-permute-start | bytes 393224 | tf_op jit(solution)/shard_map/ppermute | solution.py:373
  29.8 8.7 %collective-permute-start.1 = (bf16[64,1024]{1,0:T(8,128)(2,1)S(1)}, bf16[64,1024]{1,0:T(8,128)(2,1)S(1)}, u32[]{:S(2)}, u32[]{:S(2)}) collective-permute-start(bf16[64,1024]{1,0:T(8,128)(2,1)S(1)} %bitcast.22), channel_id=1, source_target_pairs={{0,4},{1,129},{2,6},{3,131},{4,0},{5,133},{6,2},{7,135},{8,12},{9,... | collective-permute-start | bytes 393224 | tf_op jit(solution)/shard_map/ppermute | solution.py:373
  32.4 6.1 %collective-permute-start = (bf16[64,1024]{1,0:T(8,128)(2,1)S(1)}, bf16[64,1024]{1,0:T(8,128)(2,1)S(1)}, u32[]{:S(2)}, u32[]{:S(2)}) collective-permute-start(bf16[64,1024]{1,0:T(8,128)(2,1)S(1)} %bitcast.23), channel_id=1, source_target_pairs={{0,2},{1,65},{2,4},{3,67},{4,6},{5,69},{6,0},{7,71},{8,10},{9,73},... | collective-permute-start | bytes 393224 | tf_op jit(solution)/shard_map/ppermute | solution.py:373
  34.6 6.8 %collective-permute-start.9 = (bf16[64,1024]{1,0:T(8,128)(2,1)S(1)}, bf16[64,1024]{1,0:T(8,128)(2,1)S(1)}, u32[]{:S(2)}, u32[]{:S(2)}) collective-permute-start(bf16[64,1024]{1,0:T(8,128)(2,1)S(1)} %get-tuple-element.49), channel_id=1, source_target_pairs={{0,2},{1,65},{2,4},{3,67},{4,6},{5,69},{6,0},{7,71},{8,10},{9,73},... | collective-permute-start | bytes 393224 | tf_op jit(solution)/shard_map/ppermute | solution.py:373
  34.6 8.0 %collective-permute-start.10 = (bf16[64,1024]{1,0:T(8,128)(2,1)S(1)}, bf16[64,1024]{1,0:T(8,128)(2,1)S(1)}, u32[]{:S(2)}, u32[]{:S(2)}) collective-permute-start(bf16[64,1024]{1,0:T(8,128)(2,1)S(1)} %get-tuple-element.50), channel_id=1, source_target_pairs={{0,4},{1,129},{2,6},{3,131},{4,0},{5,133},{6,2},{7,135},{8,12},{9,... | collective-permute-start | bytes 393224 | tf_op jit(solution)/shard_map/ppermute | solution.py:373
  36.8 7.5 %collective-permute-start.11 = (bf16[64,1024]{1,0:T(8,128)(2,1)S(1)}, bf16[64,1024]{1,0:T(8,128)(2,1)S(1)}, u32[]{:S(2)}, u32[]{:S(2)}) collective-permute-start(bf16[64,1024]{1,0:T(8,128)(2,1)S(1)} %get-tuple-element.51), channel_id=1, source_target_pairs={{0,6},{1,193},{2,0},{3,195},{4,2},{5,197},{6,4},{7,199},{8,14},{9,... | collective-permute-start | bytes 393224 | tf_op jit(solution)/shard_map/ppermute | solution.py:373
  38.7 10.0 %collective-permute-start.8 = (bf16[256,1024]{1,0:T(8,128)(2,1)S(1)}, bf16[256,1024]{1,0:T(8,128)(2,1)S(1)}, u32[]{:S(2)}, u32[]{:S(2)}) collective-permute-start(bf16[256,1024]{1,0:T(8,128)(2,1)S(1)} %arrange.1.r0_ref), channel_id=1, source_target_pairs={{0,192},{1,7},{2,194},{3,1},{4,196},{5,3},{6,198},{7,5},{8,200},{9... | collective-permute-start | bytes 1572872 | tf_op jit(solution)/shard_map/ppermute | solution.py:373
  40.1 11.2 %collective-permute-start.7 = (bf16[256,1024]{1,0:T(8,128)(2,1)S(1)}, bf16[256,1024]{1,0:T(8,128)(2,1)S(1)}, u32[]{:S(2)}, u32[]{:S(2)}) collective-permute-start(bf16[256,1024]{1,0:T(8,128)(2,1)S(1)} %arrange.1.r0_ref), channel_id=1, source_target_pairs={{0,128},{1,5},{2,130},{3,7},{4,132},{5,1},{6,134},{7,3},{8,136},{9... | collective-permute-start | bytes 1572872 | tf_op jit(solution)/shard_map/ppermute | solution.py:373
  41.4 15.0 %collective-permute-start.6 = (bf16[256,1024]{1,0:T(8,128)(2,1)S(1)}, bf16[256,1024]{1,0:T(8,128)(2,1)S(1)}, u32[]{:S(2)}, u32[]{:S(2)}) collective-permute-start(bf16[256,1024]{1,0:T(8,128)(2,1)S(1)} %arrange.1.r0_ref), channel_id=1, source_target_pairs={{0,64},{1,3},{2,66},{3,5},{4,68},{5,7},{6,70},{7,1},{8,72},{9,11},... | collective-permute-start | bytes 1572872 | tf_op jit(solution)/shard_map/ppermute | solution.py:373
  45.1 16.1 %all-to-all-start.1 = ((f32[8,8,1024]{2,1,0:T(8,128)}), f32[8,8,1024]{2,1,0:T(8,128)S(1)}, u32[]{:S(2)}, u32[]{:S(2)}) async-start(f32[8,8,1024]{2,1,0:T(8,128)} %bitcast.10), calls=%async_computation.1 | async-start | bytes 524288 | tf_op jit(solution)/shard_map/all_to_all | solution.py:386
  48.7 7.7 %copy-start.6 = (bf16[256,32]{1,0:T(8,128)(2,1)S(1)}, bf16[256,32]{1,0:T(8,128)(2,1)}, u32[]{:S(2)}) copy-start(bf16[256,32]{1,0:T(8,128)(2,1)} %get-tuple-element.45.left_ref) | copy-start | bytes 49156
  56.4 4.8 %copy-start = (bf16[32,8,256]{2,1,0:T(8,128)(2,1)S(1)}, bf16[32,8,256]{2,1,0:T(8,128)(2,1)}, u32[]{:S(2)}) copy-start(bf16[32,8,256]{2,1,0:T(8,128)(2,1)} %param.10) | copy-start | bytes 393220
  56.4 4.8 %copy-start.1 = (bf16[256,32]{0,1:T(8,128)(2,1)S(1)}, bf16[256,32]{0,1:T(8,128)(2,1)}, u32[]{:S(2)}) copy-start(bf16[256,32]{0,1:T(8,128)(2,1)} %param.13) | copy-start | bytes 49156
  56.4 4.9 %copy-start.2 = (bf16[256,32]{0,1:T(8,128)(2,1)S(1)}, bf16[256,32]{0,1:T(8,128)(2,1)}, u32[]{:S(2)}) copy-start(bf16[256,32]{0,1:T(8,128)(2,1)} %param.15) | copy-start | bytes 49156
  56.4 4.9 %copy-start.3 = (f32[256]{0:T(256)S(1)}, f32[256]{0:T(256)}, u32[]{:S(2)}) copy-start(f32[256]{0:T(256)} %param.11) | copy-start | bytes 3076
  56.4 4.9 %copy-start.4 = (f32[256]{0:T(256)S(1)}, f32[256]{0:T(256)}, u32[]{:S(2)}) copy-start(f32[256]{0:T(256)} %param.12) | copy-start | bytes 3076
  61.2 33.4 %copy-start.5 = (f32[128]{0:T(128)S(1)}, f32[128]{0:T(128)}, u32[]{:S(2)}) copy-start(f32[128]{0:T(128)} %param.18) | copy-start | bytes 1540
  89.3 12.9 %all-to-all-start.4 = ((bf16[16,96,128]{2,1,0:T(8,128)(2,1)}), bf16[16,96,128]{2,1,0:T(8,128)(2,1)S(1)}, u32[]{:S(2)}, u32[]{:S(2)}) async-start(bf16[16,96,128]{2,1,0:T(8,128)(2,1)} %spread.1), calls=%async_computation.4 | async-start | bytes 786432 | tf_op jit(solution)/shard_map/all_to_all | solution.py:386

commit v7 on v5

--- a/solution.py
+++ b/solution.py
@@ -252,7 +252,7 @@
 
 def third_kernel(
     left_grad_ref, w_hbm, bias_grad_ref, x_ref, gain_ref, shift_ref, k1_ref, k2_ref, pieces_ref,
-    align_ref, pack_ref, w_ref, sem,
+    align_hbm, pack_ref, w_ref, align_ref, sem, align_sem,
 ):
     load = pltpu.make_async_copy(w_hbm, w_ref, sem)
     load.start()
@@ -283,6 +283,8 @@
     mean_one = jnp.mean(unit_grad, axis=-1, keepdims=True)
     mean_two = jnp.mean(unit_grad * unit, axis=-1, keepdims=True)
     align_ref[...] = inverse * (unit_grad - mean_one - unit * mean_two)
+    store = pltpu.make_async_copy(align_ref, align_hbm, align_sem)
+    store.start()
     gain_grad = jnp.sum(normed_grad * unit, axis=0, keepdims=True)
     offset_grad = jnp.sum(normed_grad, axis=0, keepdims=True)
     both = jnp.concatenate([lg_high, rg_high, lg_low, rg_low], axis=1)
@@ -297,6 +299,7 @@
     small = jnp.concatenate([weights.reshape(NP, 8, Z), rest], axis=1)
     load.wait()
     pack_ref[...] = packed(w_ref[...].astype(F32).reshape(NP, WR, Z), small)
+    store.wait()
 
 
 def packed(w_rows, small):
@@ -380,10 +383,6 @@
     return lax.all_to_all(array, axes, 0, 0, tiled=True)
 
 
-def blocking_exchange(array, axes):
-    return lax.cond(lax.axis_index("x") < NX, lambda v: exchange(v, axes), jnp.zeros_like, array)
-
-
 def per_device(x, gain, shift, k1, b1, k2, b2, w, bias, g):
     gain, shift, b1, b2, bias = [v.reshape(1, -1) for v in (gain, shift, b1, b2, bias)]
     x, k1, k2 = x.reshape(S * I, H), k1.T, k2.T
@@ -410,7 +409,7 @@
     quarter = ((Q, C * S), BF16)
     column = ((G, C * S), BF16)
     planes = shifted((p0, p1, p2, p3), True)
-    near = blocking_exchange(copies, "z")
+    near = exchange(copies, "z")
     lines = shifted([near] * NY, False)
     parts = call(
         fold_kernel, "fold", 8, (pltpu.VMEM(*column),) * NY, [pltpu.VMEM((Q, C * S), F32)]
@@ -446,8 +445,10 @@
         third_kernel,
         "third",
         12,
-        (shape((S * I, H), F32), shape((NP, WR + 32, Z), BF16)),
-        [pltpu.VMEM((C, C, Z), BF16), pltpu.SemaphoreType.DMA],
+        (pltpu.HBM((S * I, H), F32), shape((NP, WR + 32, Z), BF16)),
+        [pltpu.VMEM((C, C, Z), BF16), pltpu.VMEM((S * I, H), F32)]
+        + [pltpu.SemaphoreType.DMA, pltpu.SemaphoreType.DMA],
+        out_specs=[HBM, VMEM],
         in_specs=[VMEM, HBM] + [VMEM] * 7,
     )(left_grad, in_hbm(w_part), bias_grad, x, gain, shift, k1, k2, pieces)
     parts = exchange(pack, ("x", "y"))

time: 105 us -> 103 us (0.981)
  Pallas kernels: 24.6 us -> 23.1 us
where the time goes in v7:
time: 103 us
  blocking collectives  42.4 us (41%)
  starting transfers between devices  26.6 us (26%)
  Pallas kernels  23.1 us (22%)
  waiting for transfers between devices  9.85 us (10%)
    all_to_all x3, blocking collectives, exchange(): return lax.all_to_all(array, axes, 0, 0, tiled=True)  42.4 us
    ppermute x12, starting transfers between devices, shifted(): lax.ppermute(arrays[k], ('x', 'z', 'y', 'dp'), ring(k, long))  17.7 us
    all_to_all x2, starting transfers between devices, exchange(): return lax.all_to_all(array, axes, 0, 0, tiled=True)  8.93 us
    ppermute x12, waiting for transfers between devices, shifted(): lax.ppermute(arrays[k], ('x', 'z', 'y', 'dp'), ring(k, long))  7.71 us
    pallas_call x1, Pallas kernels, per_device(): call(first_kernel, 'first', 24, tuple((pltpu.HBM(*v) for v in made)) + (p...  5.39 us
    pallas_call x1, Pallas kernels, per_device(): call(update_kernel, 'update', 20, pltpu.HBM((I, J, Z), BF16), [pltpu.VMEM...  5.38 us
    pallas_call x1, Pallas kernels, per_device(): call(second_kernel, 'second', 16, (shape((I * S, C), F32), pltpu.HBM((C,...  4.37 us
    pallas_call x1, Pallas kernels, per_device(): call(early_kernel, 'early', 16, pltpu.VMEM((C * S + 16, I * Z), F32), [pl...  2.53 us
  transfers between devices with their start and end apart: 14, of which 4 were waited for; matrix products, arithmetic and copies ran while one was open for 0% of the time, Pallas kernels for 13%

profile of v7, /device:TPU:8, one launch (start us, length us, event | category | flops | bytes accessed | tf_op | source)
XLA Modules:
  0.0 102.9 jit_solution(11174046988619483068)
XLA Ops:
  0.6 5.4 %first.1 = (bf16[256,32]{1,0:T(8,128)(2,1)}, bf16[64,1024]{1,0:T(8,128)(2,1)}, bf16[32,4096]{1,0:T(8,128)(2,1)}, bf16[1024,1024]{1,0:T(8,128)(2,1)}, bf16[8,1024...) custom-call(bf16[256,256]{1,0:T(8,128)(2,1)} %bitcast.25, ...), custom_call_target="tpu_custom_call" | custom-call | tf_op jit(solution)/shard_map/first/pallas_call | solution.py:397
  6.0 1.6 %collective-permute-start.3 = (bf16[256,1024]{1,0:T(8,128)(2,1)S(1)}, bf16[256,1024]{1,0:T(8,128)(2,1)S(1)}, u32[]{:S(2)}, u32[]{:S(2)}) collective-permute-start(bf16[256,1024]{1,0:T(8,128)(2,1)S(1)} %get-tuple-element.38), channel_id=1, source_target_pairs={{0,64},{1,3},{2,66},{3,5},{4,68},{5,7},{6,70},{7,1},{8,72},{9,11},... | collective-permute-start | bytes 1572872 | tf_op jit(solution)/shard_map/ppermute | solution.py:370
  7.6 2.7 %collective-permute-start.4 = (bf16[256,1024]{1,0:T(8,128)(2,1)S(1)}, bf16[256,1024]{1,0:T(8,128)(2,1)S(1)}, u32[]{:S(2)}, u32[]{:S(2)}) collective-permute-start(bf16[256,1024]{1,0:T(8,128)(2,1)S(1)} %get-tuple-element.39), channel_id=1, source_target_pairs={{0,128},{1,5},{2,130},{3,7},{4,132},{5,1},{6,134},{7,3},{8,136},{9... | collective-permute-start | bytes 1572872 | tf_op jit(solution)/shard_map/ppermute | solution.py:370
  10.3 1.4 %collective-permute-start.5 = (bf16[256,1024]{1,0:T(8,128)(2,1)S(1)}, bf16[256,1024]{1,0:T(8,128)(2,1)S(1)}, u32[]{:S(2)}, u32[]{:S(2)}) collective-permute-start(bf16[256,1024]{1,0:T(8,128)(2,1)S(1)} %get-tuple-element.40), channel_id=1, source_target_pairs={{0,192},{1,7},{2,194},{3,1},{4,196},{5,3},{6,198},{7,5},{8,200},{9... | collective-permute-start | bytes 1572872 | tf_op jit(solution)/shard_map/ppermute | solution.py:370
  11.8 17.5 %all_to_all.37 = bf16[8,8,1024]{2,1,0:T(8,128)(2,1)S(1)} all-to-all(bf16[8,8,1024]{2,1,0:T(8,128)(2,1)} %bitcast.36), channel_id=1, replica_groups=mesh['x'=4,'z'=8,'y'=4,'dp'=2] {'z'}, dimensions={0} | all-to-all | bytes 262144 | tf_op jit(solution)/shard_map/all_to_all | solution.py:383
  29.3 0.4 collective-permute-start.2
  29.8 2.6 %collective-permute-start.1 = (bf16[64,1024]{1,0:T(8,128)(2,1)S(1)}, bf16[64,1024]{1,0:T(8,128)(2,1)S(1)}, u32[]{:S(2)}, u32[]{:S(2)}) collective-permute-start(bf16[64,1024]{1,0:T(8,128)(2,1)S(1)} %bitcast.22), channel_id=1, source_target_pairs={{0,4},{1,129},{2,6},{3,131},{4,0},{5,133},{6,2},{7,135},{8,12},{9,... | collective-permute-start | bytes 393224 | tf_op jit(solution)/shard_map/ppermute | solution.py:370
  32.4 0.0 collective-permute-done.3.refs_1_
  32.4 1.9 %collective-permute-start = (bf16[64,1024]{1,0:T(8,128)(2,1)S(1)}, bf16[64,1024]{1,0:T(8,128)(2,1)S(1)}, u32[]{:S(2)}, u32[]{:S(2)}) collective-permute-start(bf16[64,1024]{1,0:T(8,128)(2,1)S(1)} %bitcast.23), channel_id=1, source_target_pairs={{0,2},{1,65},{2,4},{3,67},{4,6},{5,69},{6,0},{7,71},{8,10},{9,73},... | collective-permute-start | bytes 393224 | tf_op jit(solution)/shard_map/ppermute | solution.py:370
  34.2 0.0 collective-permute-done.4.refs_2_
  34.2 0.0 collective-permute-done.5.refs_3_
  34.3 0.3 fold.1
  34.6 0.1 collective-permute-start.9
  34.6 2.2 %collective-permute-start.10 = (bf16[64,1024]{1,0:T(8,128)(2,1)S(1)}, bf16[64,1024]{1,0:T(8,128)(2,1)S(1)}, u32[]{:S(2)}, u32[]{:S(2)}) collective-permute-start(bf16[64,1024]{1,0:T(8,128)(2,1)S(1)} %get-tuple-element.50), channel_id=1, source_target_pairs={{0,4},{1,129},{2,6},{3,131},{4,0},{5,133},{6,2},{7,135},{8,12},{9,... | collective-permute-start | bytes 393224 | tf_op jit(solution)/shard_map/ppermute | solution.py:370
  36.8 0.0 collective-permute-done.2.refs_3_
  36.8 1.7 %collective-permute-start.11 = (bf16[64,1024]{1,0:T(8,128)(2,1)S(1)}, bf16[64,1024]{1,0:T(8,128)(2,1)S(1)}, u32[]{:S(2)}, u32[]{:S(2)}) collective-permute-start(bf16[64,1024]{1,0:T(8,128)(2,1)S(1)} %get-tuple-element.51), channel_id=1, source_target_pairs={{0,6},{1,193},{2,0},{3,195},{4,2},{5,197},{6,4},{7,199},{8,14},{9,... | collective-permute-start | bytes 393224 | tf_op jit(solution)/shard_map/ppermute | solution.py:370
  38.5 0.0 collective-permute-done.1.refs_2_
  38.5 0.0 collective-permute-done.refs_1_
  38.5 0.1 arrange.1.r0_ref
  38.7 1.4 %collective-permute-start.8 = (bf16[256,1024]{1,0:T(8,128)(2,1)S(1)}, bf16[256,1024]{1,0:T(8,128)(2,1)S(1)}, u32[]{:S(2)}, u32[]{:S(2)}) collective-permute-start(bf16[256,1024]{1,0:T(8,128)(2,1)S(1)} %arrange.1.r0_ref), channel_id=1, source_target_pairs={{0,192},{1,7},{2,194},{3,1},{4,196},{5,3},{6,198},{7,5},{8,200},{9... | collective-permute-start | bytes 1572872 | tf_op jit(solution)/shard_map/ppermute | solution.py:370
  40.1 1.3 %collective-permute-start.7 = (bf16[256,1024]{1,0:T(8,128)(2,1)S(1)}, bf16[256,1024]{1,0:T(8,128)(2,1)S(1)}, u32[]{:S(2)}, u32[]{:S(2)}) collective-permute-start(bf16[256,1024]{1,0:T(8,128)(2,1)S(1)} %arrange.1.r0_ref), channel_id=1, source_target_pairs={{0,128},{1,5},{2,130},{3,7},{4,132},{5,1},{6,134},{7,3},{8,136},{9... | collective-permute-start | bytes 1572872 | tf_op jit(solution)/shard_map/ppermute | solution.py:370
  41.4 0.0 collective-permute-done.9.refs_1_
  41.4 0.4 collective-permute-start.6
  41.8 0.9 collective-permute-done.10.refs_2_
  42.7 1.7 %collective-permute-done.11.refs_3_ = bf16[64,1024]{1,0:T(8,128)(2,1)S(1)} collective-permute-done((bf16[64,1024]{1,0:T(8,128)(2,1)S(1)}, bf16[64,1024]{1,0:T(8,128)(2,1)S(1)}, u32[]{:S(2)}, u32[]{:S(2)}) %collective-permute-start.11) | collective-permute-done | bytes 131104 | tf_op jit(solution)/shard_map/ppermute | solution.py:370
  44.3 0.8 add.1
  45.1 3.6 %all-to-all-start.1 = ((f32[8,8,1024]{2,1,0:T(8,128)}), f32[8,8,1024]{2,1,0:T(8,128)S(1)}, u32[]{:S(2)}, u32[]{:S(2)}) async-start(f32[8,8,1024]{2,1,0:T(8,128)} %bitcast.10), calls=%async_computation.1 | async-start | bytes 524288 | tf_op jit(solution)/shard_map/all_to_all | solution.py:383
  48.7 0.0 collective-permute-done.8.r3_ref.re_ref
  48.7 0.0 copy-start.6
  48.7 2.5 %early.1.u_ref = f32[1040,1024]{1,0:T(8,128)S(1)} custom-call(bf16[256,1024]{1,0:T(8,128)(2,1)S(1)} %arrange.1.r0_ref, bf16[256,1024]{1,0:T(8,128)(2,1)S(1)} %collective-permute-done.8.r3_ref.re_ref, bf16[8,1024,128]{2,1,0:T(8,128)(2,1)} %get-tuple-element.43.g_hbm), custom_call_target="tpu_custom_call" | custom-call | tf_op jit(solution)/shard_map/early/pallas_call | solution.py:425
  51.3 0.0 collective-permute-done.7.r2_ref.rb_ref
  51.3 5.1 %collective-permute-done.6.r1_ref.ra_ref = bf16[256,1024]{1,0:T(8,128)(2,1)S(1)} collective-permute-done((bf16[256,1024]{1,0:T(8,128)(2,1)S(1)}, bf16[256,1024]{1,0:T(8,128)(2,1)S(1)}, u32[]{:S(2)}, u32[]{:S(2)}) %collective-permute-start.6) | collective-permute-done | bytes 524320 | tf_op jit(solution)/shard_map/ppermute | solution.py:370
  56.4 0.0 copy-done.6
  56.4 0.0 copy-start
  56.4 0.0 copy-start.1
  56.4 0.0 copy-start.2
  56.4 0.0 copy-start.3
  56.4 0.0 copy-start.4
  56.4 4.4 %second.1 = (f32[256,32]{1,0:T(8,128)S(1)}, bf16[32,32,128]{2,1,0:T(8,128)(2,1)}, f32[1,128]{1,0:T(1,128)S(1)}) custom-call(bf16[256,1024]{1,0:T(8,128)(2,1)S(1)} %collective-permute-done.6.r1_ref.ra_ref, bf16[256,1024]{1,0:T(8,128)(2,1)S(1)} %collective-permute-done.7.r2_ref.rb_ref, f32[1040,1024]{1,0:T(8,128)S(1)} %early.1.u_ref, ...), custom_call_target="tpu_custom_call" | custom-call | flops 99999997952 | tf_op jit(solution)/shard_map/second/pallas_call | solution.py:433
  60.8 0.0 copy-start.5
  60.8 0.0 all-to-all-done.1
  60.8 0.0 copy-done
  60.8 0.0 copy-done.1
  60.8 0.0 copy-done.2
  60.8 0.0 copy-done.3
  60.8 0.0 copy-done.4
  60.9 2.3 %third.1 = (f32[256,256]{1,0:T(8,128)}, bf16[16,96,128]{2,1,0:T(8,128)(2,1)S(1)}) custom-call(f32[256,32]{1,0:T(8,128)S(1)} %get-tuple-element.46.left_grad_ref, bf16[32,32,128]{2,1,0:T(8,128)(2,1)} %get-tuple-element.47.w_hbm, f32[1,128]{1,0:T(1,128)S(1)} %get-tuple-element.48.bias_grad_ref, bf16[256,256]{1,0:T(8,128)(2,1)S(1)} %bitcast.26, ...), custom_call_target="tpu_custom_call" | custom-call | tf_op jit(solution)/shard_map/third/pallas_call | solution.py:444
  63.1 12.1 %all_to_all.38.in_ref = bf16[16,96,128]{2,1,0:T(8,128)(2,1)S(1)} all-to-all(bf16[16,96,128]{2,1,0:T(8,128)(2,1)S(1)} %get-tuple-element.53), channel_id=1, replica_groups=mesh['x'=4,'z'=8,'y'=4,'dp'=2] {'x','y'}, dimensions={0} | all-to-all | bytes 786432 | tf_op jit(solution)/shard_map/all_to_all | solution.py:383
  75.2 0.1 sum.1
  75.3 12.8 %all_to_all.39.in_ref = bf16[8,96,128]{2,1,0:T(8,128)(2,1)S(1)} all-to-all(bf16[8,96,128]{2,1,0:T(8,128)(2,1)S(1)} %sum.1), channel_id=1, replica_groups=mesh['x'=4,'z'=8,'y'=4,'dp'=2] {'z'}, dimensions={0} | all-to-all | bytes 393216 | tf_op jit(solution)/shard_map/all_to_all | solution.py:383
  88.1 0.8 spread.1
  88.9 5.3 %all-to-all-start.4 = ((bf16[16,96,128]{2,1,0:T(8,128)(2,1)}), bf16[16,96,128]{2,1,0:T(8,128)(2,1)S(1)}, u32[]{:S(2)}, u32[]{:S(2)}) async-start(bf16[16,96,128]{2,1,0:T(8,128)(2,1)} %spread.1), calls=%async_computation.4 | async-start | bytes 786432 | tf_op jit(solution)/shard_map/all_to_all | solution.py:383
  94.2 0.0 copy-done.5
  94.2 5.4 %update.1 = bf16[8,1024,128]{2,1,0:T(8,128)(2,1)} custom-call(bf16[256,1024]{1,0:T(8,128)(2,1)S(1)} %arrange.1.r0_ref, bf16[256,1024]{1,0:T(8,128)(2,1)S(1)} %collective-permute-done.6.r1_ref.ra_ref, bf16[256,1024]{1,0:T(8,128)(2,1)S(1)} %collective-permute-done.7.r2_ref.rb_ref, bf16[256,1024]{1,0:T(8,128)(2,1)S(1)} %collective-permute-done.8.r3_ref.re_ref, ...), custom_call_target="tpu_custom_call" | custom-call | tf_op jit(solution)/shard_map/update/pallas_call | solution.py:455
  99.6 2.1 %all-to-all-done.4.in_ref = bf16[16,96,128]{2,1,0:T(8,128)(2,1)S(1)} async-done(((bf16[16,96,128]{2,1,0:T(8,128)(2,1)}), bf16[16,96,128]{2,1,0:T(8,128)(2,1)S(1)}, u32[]{:S(2)}, u32[]{:S(2)}) %all-to-all-start.4) | async-done | bytes 393248 | tf_op jit(solution)/shard_map/all_to_all | solution.py:383
  101.8 1.2 %last.1 = (f32[1,256]{1,0:T(1,128)}, f32[1,256]{1,0:T(1,128)}, f32[32,256]{1,0:T(8,128)}, f32[1,32]{1,0:T(1,128)}, f32[32,256]{1,0:T(8,128)}, /*index=5*/f32[1,3...) custom-call(bf16[16,96,128]{2,1,0:T(8,128)(2,1)S(1)} %all-to-all-done.4.in_ref), custom_call_target="tpu_custom_call" | custom-call | tf_op jit(solution)/shard_map/last/pallas_call | solution.py:469
Async XLA Ops:
  6.0 26.3 %collective-permute-start.3 = (bf16[256,1024]{1,0:T(8,128)(2,1)S(1)}, bf16[256,1024]{1,0:T(8,128)(2,1)S(1)}, u32[]{:S(2)}, u32[]{:S(2)}) collective-permute-start(bf16[256,1024]{1,0:T(8,128)(2,1)S(1)} %get-tuple-element.38), channel_id=1, source_target_pairs={{0,64},{1,3},{2,66},{3,5},{4,68},{5,7},{6,70},{7,1},{8,72},{9,11},... | collective-permute-start | bytes 1572872 | tf_op jit(solution)/shard_map/ppermute | solution.py:370
  7.6 26.6 %collective-permute-start.4 = (bf16[256,1024]{1,0:T(8,128)(2,1)S(1)}, bf16[256,1024]{1,0:T(8,128)(2,1)S(1)}, u32[]{:S(2)}, u32[]{:S(2)}) collective-permute-start(bf16[256,1024]{1,0:T(8,128)(2,1)S(1)} %get-tuple-element.39), channel_id=1, source_target_pairs={{0,128},{1,5},{2,130},{3,7},{4,132},{5,1},{6,134},{7,3},{8,136},{9... | collective-permute-start | bytes 1572872 | tf_op jit(solution)/shard_map/ppermute | solution.py:370
  10.3 23.9 %collective-permute-start.5 = (bf16[256,1024]{1,0:T(8,128)(2,1)S(1)}, bf16[256,1024]{1,0:T(8,128)(2,1)S(1)}, u32[]{:S(2)}, u32[]{:S(2)}) collective-permute-start(bf16[256,1024]{1,0:T(8,128)(2,1)S(1)} %get-tuple-element.40), channel_id=1, source_target_pairs={{0,192},{1,7},{2,194},{3,1},{4,196},{5,3},{6,198},{7,5},{8,200},{9... | collective-permute-start | bytes 1572872 | tf_op jit(solution)/shard_map/ppermute | solution.py:370
  29.3 7.5 %collective-permute-start.2 = (bf16[64,1024]{1,0:T(8,128)(2,1)S(1)}, bf16[64,1024]{1,0:T(8,128)(2,1)S(1)}, u32[]{:S(2)}, u32[]{:S(2)}) collective-permute-start(bf16[64,1024]{1,0:T(8,128)(2,1)S(1)} %bitcast.21), channel_id=1, source_target_pairs={{0,6},{1,193},{2,0},{3,195},{4,2},{5,197},{6,4},{7,199},{8,14},{9,... | collective-permute-start | bytes 393224 | tf_op jit(solution)/shard_map/ppermute | solution.py:370
  29.8 8.7 %collective-permute-start.1 = (bf16[64,1024]{1,0:T(8,128)(2,1)S(1)}, bf16[64,1024]{1,0:T(8,128)(2,1)S(1)}, u32[]{:S(2)}, u32[]{:S(2)}) collective-permute-start(bf16[64,1024]{1,0:T(8,128)(2,1)S(1)} %bitcast.22), channel_id=1, source_target_pairs={{0,4},{1,129},{2,6},{3,131},{4,0},{5,133},{6,2},{7,135},{8,12},{9,... | collective-permute-start | bytes 393224 | tf_op jit(solution)/shard_map/ppermute | solution.py:370
  32.4 6.1 %collective-permute-start = (bf16[64,1024]{1,0:T(8,128)(2,1)S(1)}, bf16[64,1024]{1,0:T(8,128)(2,1)S(1)}, u32[]{:S(2)}, u32[]{:S(2)}) collective-permute-start(bf16[64,1024]{1,0:T(8,128)(2,1)S(1)} %bitcast.23), channel_id=1, source_target_pairs={{0,2},{1,65},{2,4},{3,67},{4,6},{5,69},{6,0},{7,71},{8,10},{9,73},... | collective-permute-start | bytes 393224 | tf_op jit(solution)/shard_map/ppermute | solution.py:370
  34.6 6.8 %collective-permute-start.9 = (bf16[64,1024]{1,0:T(8,128)(2,1)S(1)}, bf16[64,1024]{1,0:T(8,128)(2,1)S(1)}, u32[]{:S(2)}, u32[]{:S(2)}) collective-permute-start(bf16[64,1024]{1,0:T(8,128)(2,1)S(1)} %get-tuple-element.49), channel_id=1, source_target_pairs={{0,2},{1,65},{2,4},{3,67},{4,6},{5,69},{6,0},{7,71},{8,10},{9,73},... | collective-permute-start | bytes 393224 | tf_op jit(solution)/shard_map/ppermute | solution.py:370
  34.6 8.0 %collective-permute-start.10 = (bf16[64,1024]{1,0:T(8,128)(2,1)S(1)}, bf16[64,1024]{1,0:T(8,128)(2,1)S(1)}, u32[]{:S(2)}, u32[]{:S(2)}) collective-permute-start(bf16[64,1024]{1,0:T(8,128)(2,1)S(1)} %get-tuple-element.50), channel_id=1, source_target_pairs={{0,4},{1,129},{2,6},{3,131},{4,0},{5,133},{6,2},{7,135},{8,12},{9,... | collective-permute-start | bytes 393224 | tf_op jit(solution)/shard_map/ppermute | solution.py:370
  36.8 7.5 %collective-permute-start.11 = (bf16[64,1024]{1,0:T(8,128)(2,1)S(1)}, bf16[64,1024]{1,0:T(8,128)(2,1)S(1)}, u32[]{:S(2)}, u32[]{:S(2)}) collective-permute-start(bf16[64,1024]{1,0:T(8,128)(2,1)S(1)} %get-tuple-element.51), channel_id=1, source_target_pairs={{0,6},{1,193},{2,0},{3,195},{4,2},{5,197},{6,4},{7,199},{8,14},{9,... | collective-permute-start | bytes 393224 | tf_op jit(solution)/shard_map/ppermute | solution.py:370
  38.7 10.0 %collective-permute-start.8 = (bf16[256,1024]{1,0:T(8,128)(2,1)S(1)}, bf16[256,1024]{1,0:T(8,128)(2,1)S(1)}, u32[]{:S(2)}, u32[]{:S(2)}) collective-permute-start(bf16[256,1024]{1,0:T(8,128)(2,1)S(1)} %arrange.1.r0_ref), channel_id=1, source_target_pairs={{0,192},{1,7},{2,194},{3,1},{4,196},{5,3},{6,198},{7,5},{8,200},{9... | collective-permute-start | bytes 1572872 | tf_op jit(solution)/shard_map/ppermute | solution.py:370
  40.1 11.2 %collective-permute-start.7 = (bf16[256,1024]{1,0:T(8,128)(2,1)S(1)}, bf16[256,1024]{1,0:T(8,128)(2,1)S(1)}, u32[]{:S(2)}, u32[]{:S(2)}) collective-permute-start(bf16[256,1024]{1,0:T(8,128)(2,1)S(1)} %arrange.1.r0_ref), channel_id=1, source_target_pairs={{0,128},{1,5},{2,130},{3,7},{4,132},{5,1},{6,134},{7,3},{8,136},{9... | collective-permute-start | bytes 1572872 | tf_op jit(solution)/shard_map/ppermute | solution.py:370
  41.4 15.0 %collective-permute-start.6 = (bf16[256,1024]{1,0:T(8,128)(2,1)S(1)}, bf16[256,1024]{1,0:T(8,128)(2,1)S(1)}, u32[]{:S(2)}, u32[]{:S(2)}) collective-permute-start(bf16[256,1024]{1,0:T(8,128)(2,1)S(1)} %arrange.1.r0_ref), channel_id=1, source_target_pairs={{0,64},{1,3},{2,66},{3,5},{4,68},{5,7},{6,70},{7,1},{8,72},{9,11},... | collective-permute-start | bytes 1572872 | tf_op jit(solution)/shard_map/ppermute | solution.py:370
  45.1 15.7 %all-to-all-start.1 = ((f32[8,8,1024]{2,1,0:T(8,128)}), f32[8,8,1024]{2,1,0:T(8,128)S(1)}, u32[]{:S(2)}, u32[]{:S(2)}) async-start(f32[8,8,1024]{2,1,0:T(8,128)} %bitcast.10), calls=%async_computation.1 | async-start | bytes 524288 | tf_op jit(solution)/shard_map/all_to_all | solution.py:383
  48.7 7.7 %copy-start.6 = (bf16[256,32]{1,0:T(8,128)(2,1)S(1)}, bf16[256,32]{1,0:T(8,128)(2,1)}, u32[]{:S(2)}) copy-start(bf16[256,32]{1,0:T(8,128)(2,1)} %get-tuple-element.45.left_ref) | copy-start | bytes 49156
  56.4 4.4 %copy-start = (bf16[32,8,256]{2,1,0:T(8,128)(2,1)S(1)}, bf16[32,8,256]{2,1,0:T(8,128)(2,1)}, u32[]{:S(2)}) copy-start(bf16[32,8,256]{2,1,0:T(8,128)(2,1)} %param.10) | copy-start | bytes 393220
  56.4 4.4 %copy-start.1 = (bf16[256,32]{0,1:T(8,128)(2,1)S(1)}, bf16[256,32]{0,1:T(8,128)(2,1)}, u32[]{:S(2)}) copy-start(bf16[256,32]{0,1:T(8,128)(2,1)} %param.13) | copy-start | bytes 49156
  56.4 4.5 %copy-start.2 = (bf16[256,32]{0,1:T(8,128)(2,1)S(1)}, bf16[256,32]{0,1:T(8,128)(2,1)}, u32[]{:S(2)}) copy-start(bf16[256,32]{0,1:T(8,128)(2,1)} %param.15) | copy-start | bytes 49156
  56.4 4.5 %copy-start.3 = (f32[256]{0:T(256)S(1)}, f32[256]{0:T(256)}, u32[]{:S(2)}) copy-start(f32[256]{0:T(256)} %param.11) | copy-start | bytes 3076
  56.4 4.5 %copy-start.4 = (f32[256]{0:T(256)S(1)}, f32[256]{0:T(256)}, u32[]{:S(2)}) copy-start(f32[256]{0:T(256)} %param.12) | copy-start | bytes 3076
  60.8 33.4 %copy-start.5 = (f32[128]{0:T(128)S(1)}, f32[128]{0:T(128)}, u32[]{:S(2)}) copy-start(f32[128]{0:T(128)} %param.18) | copy-start | bytes 1540
  88.9 12.9 %all-to-all-start.4 = ((bf16[16,96,128]{2,1,0:T(8,128)(2,1)}), bf16[16,96,128]{2,1,0:T(8,128)(2,1)S(1)}, u32[]{:S(2)}, u32[]{:S(2)}) async-start(bf16[16,96,128]{2,1,0:T(8,128)(2,1)} %spread.1), calls=%async_computation.4 | async-start | bytes 786432 | tf_op jit(solution)/shard_map/all_to_all | solution.py:383
